TPU v7x, 32 devices: a whole 2x2x4 slice. The times are simulated.
32 devices in a mesh: dp: 8 (over z, x), seq: 2 (over y), mlp: 2 (over core).
Axes of the slice: x: 2, y: 2, z: 4, core: 2. Of those that a mesh axis runs over, the one named last changes fastest.
Arguments:
- patches: bfloat16 [1024, 48, 768], P('seq', 'dp'), may hold values from -6 to 6
- segments: int32 [1024, 48], P(None, 'dp'), may hold values from -1 to 992, as said below
- w_qkv: float32 [3, 768, 768], P(None, 'dp', 'mlp'), may hold values from -0.21875 to 0.21875
- w_out: float32 [768, 768], P('mlp', 'dp'), may hold values from -0.875 to 0.875
- w_up: float32 [768, 3072], P('dp', 'mlp'), may hold values from -0.21875 to 0.21875
- w_down: float32 [3072, 768], P('mlp', 'dp'), may hold values from -0.109375 to 0.109375
- ln_gain: float32 [2, 768], P(None, 'dp'), may hold values from 0.5 to 1.5
- ln_bias: float32 [2, 768], P(None, 'dp'), may hold values from -1.5 to 1.5
- head_gain: float32 [2, 12, 64], P(None, 'mlp', 'dp'), may hold values from 0.8 to 1.6
- cotangent: bfloat16 [1024, 48, 768], P('seq', 'dp', 'mlp'), may hold values from -6 to 6
Outputs:
- out: bfloat16 [1024, 48, 768], P('seq', 'dp', 'mlp')
- grad_patches: bfloat16 [1024, 48, 768], P('seq', 'dp')
- grad_w_qkv: float32 [3, 768, 768], P(None, 'dp', 'mlp')
- grad_w_out: float32 [768, 768], P('mlp', 'dp')
- grad_w_up: float32 [768, 3072], P('dp', 'mlp')
- grad_w_down: float32 [3072, 768], P('mlp', 'dp')
- grad_ln_gain: float32 [2, 768], P(None, 'dp')
- grad_ln_bias: float32 [2, 768], P(None, 'dp')
- grad_head_gain: float32 [2, 12, 64], P(None, 'mlp', 'dp')
Inputs may be any that keep to these rules, and one draw needn't show every extreme that they name: `segments`: in each sequence (a column) every position carries the first position of its image; images are 16 to 1024 positions long, lengths multiples of 16, packed from position 0 and followed by -1 at the padding positions at the end. In each group of 6 consecutive sequences one sequence is a single image without padding.
All inputs are finite; a program needn't handle non-finite values.
Results may differ from a plain program's by a relative error of at most 0.02.
Values may be sent and summed in bfloat16 or wider, within the bound.
No kernel may reach another device: no remote copies, remote signals or barrier semaphores. Data moves between devices by JAX's collectives and lax.ppermute only.
A program may use at most 320 MiB of HBM per device.

v0:
```python
from functools import partial
import math

import jax
import jax.numpy as jnp
from jax import lax
from jax.sharding import PartitionSpec as P

norm_eps = 1e-06
masked_value = -1e30


def layer_norm(values, gain_row, bias_row):
    average = jnp.mean(values, axis=-1, keepdims=True)
    centered = values - average
    variance = jnp.mean(centered * centered, axis=-1, keepdims=True)
    return centered * lax.rsqrt(variance + norm_eps) * gain_row + bias_row


def head_norm(values, gain_rows):
    average = jnp.mean(values, axis=-1, keepdims=True)
    centered = values - average
    variance = jnp.mean(centered * centered, axis=-1, keepdims=True)
    return centered * lax.rsqrt(variance + norm_eps) * gain_rows


def on_device(
    patches, segments, w_qkv, w_out, w_up, w_down, ln_gain, ln_bias, head_gain, cotangent
):
    (
        query_weight,
        out_weight,
        up_projection_weight,
        down_projection_weight,
        norm_gains,
        norm_biases,
        head_gains,
    ) = (
        lax.all_gather(w_qkv.astype(jnp.bfloat16), "dp", axis=1, tiled=True),
        lax.all_gather(w_out.astype(jnp.bfloat16), "dp", axis=1, tiled=True),
        lax.all_gather(w_up.astype(jnp.bfloat16), "dp", axis=0, tiled=True),
        lax.all_gather(w_down.astype(jnp.bfloat16), "dp", axis=1, tiled=True),
        lax.all_gather(ln_gain.astype(jnp.bfloat16), "dp", axis=1, tiled=True),
        lax.all_gather(ln_bias.astype(jnp.bfloat16), "dp", axis=1, tiled=True),
        lax.all_gather(head_gain.astype(jnp.bfloat16), "dp", axis=2, tiled=True),
    )
    local_rows = patches.shape[0]
    seq_here = patches.shape[1]
    width = patches.shape[2]
    head_cols = query_weight.shape[2]
    heads_here = head_gains.shape[1]
    head_size = head_gains.shape[2]
    seq_len = local_rows * lax.axis_size("seq")
    feature_cols = width // lax.axis_size("mlp")
    score_scale = head_size ** (-0.5)
    gain_float = norm_gains.astype(jnp.float32)
    bias_float = norm_biases.astype(jnp.float32)
    head_float = head_gains.astype(jnp.float32)
    seg_here = lax.dynamic_slice_in_dim(segments, lax.axis_index("seq") * local_rows, local_rows, 0)
    valid_mask = (seg_here >= 0).astype(jnp.float32)[:, :, None]
    query_segs = jnp.transpose(seg_here)
    key_segs = jnp.transpose(segments)
    patch_float = patches.astype(jnp.float32)
    normed = layer_norm(patch_float, gain_float[0], bias_float[0]).astype(jnp.bfloat16)
    projected = jnp.einsum(
        "lsd,cde->csle", normed, query_weight, preferred_element_type=jnp.float32
    )
    shape_heads = (seq_here, local_rows, heads_here, head_size)
    query_raw = projected[0].reshape(shape_heads)
    key_raw = projected[1].reshape(shape_heads)
    query_low = head_norm(query_raw, head_float[0]).astype(jnp.bfloat16)
    key_low = head_norm(key_raw, head_float[1]).astype(jnp.bfloat16)
    value_low = projected[2].astype(jnp.bfloat16)
    key_pairs = jnp.concatenate(
        [key_low.reshape(seq_here, local_rows, head_cols), value_low], axis=2
    )

    def split_pairs(gathered):
        key_heads = gathered[:, :head_cols].reshape(gathered.shape[0], heads_here, head_size)
        value_heads = gathered[:, head_cols:].reshape(gathered.shape[0], heads_here, head_size)
        return (key_heads, value_heads)

    def attend_forward(unused, inputs_seq):
        query_seq, pairs_seq, query_rows, key_rows = inputs_seq
        gathered = lax.all_gather(pairs_seq, "seq", axis=0, tiled=True)
        key_heads, value_heads = split_pairs(gathered)
        logits = (
            jnp.einsum("qhe,khe->hqk", query_seq, key_heads, preferred_element_type=jnp.float32)
            * score_scale
        )
        visible = (query_rows[:, None] == key_rows[None, :])[None]
        masked = jnp.where(visible, logits, masked_value)
        largest = jnp.max(masked, axis=2, keepdims=True)
        powered = jnp.exp(masked - largest)
        totals = jnp.sum(powered, axis=2, keepdims=True)
        attention = (powered / totals).astype(jnp.bfloat16)
        mixed = jnp.einsum(
            "hqk,khe->qhe", attention, value_heads, preferred_element_type=jnp.float32
        )
        log_total = (largest + jnp.log(totals))[:, :, 0]
        return (unused, (mixed.astype(jnp.bfloat16).reshape(local_rows, head_cols), log_total))

    _, (attn_heads, log_totals) = lax.scan(
        attend_forward, 0, (query_low, key_pairs, query_segs, key_segs)
    )
    attn_part = jnp.einsum(
        "slf,fd->lsd", attn_heads, out_weight, preferred_element_type=jnp.float32
    )
    attn_mine = lax.psum_scatter(
        attn_part.astype(jnp.bfloat16), "mlp", scatter_dimension=2, tiled=True
    ).astype(jnp.float32)
    patch_mine = lax.dynamic_slice_in_dim(
        patch_float, lax.axis_index("mlp") * feature_cols, feature_cols, 2
    )
    resid_mine = patch_mine + attn_mine
    residual = lax.all_gather(resid_mine.astype(jnp.bfloat16), "mlp", axis=2, tiled=True).astype(
        resid_mine.dtype
    )
    second_normalized = layer_norm(residual, gain_float[1], bias_float[1]).astype(jnp.bfloat16)
    hidden_pre = jnp.einsum(
        "own,nr->owr", second_normalized, up_projection_weight, preferred_element_type=jnp.float32
    )
    mlp_activation = jax.nn.gelu(hidden_pre, approximate=True).astype(jnp.bfloat16)
    branch_part = jnp.einsum(
        "ruo,oe->rue", mlp_activation, down_projection_weight, preferred_element_type=jnp.float32
    )
    branch_mine = lax.psum_scatter(
        branch_part.astype(jnp.bfloat16), "mlp", scatter_dimension=2, tiled=True
    ).astype(jnp.float32)
    out = (valid_mask * (resid_mine + branch_mine)).astype(jnp.bfloat16)
    cot_full = lax.all_gather(cotangent, "mlp", axis=2, tiled=True)
    grad_out = valid_mask * cot_full.astype(jnp.float32)
    output_gradient_reduced = grad_out.astype(jnp.bfloat16)
    grad_down = jnp.einsum(
        "xgr,xge->re", mlp_activation, output_gradient_reduced, preferred_element_type=jnp.float32
    )
    grad_act = jnp.einsum(
        "mit,nt->min",
        output_gradient_reduced,
        down_projection_weight,
        preferred_element_type=jnp.float32,
    )
    _, gelu_pull = jax.vjp(partial(jax.nn.gelu, approximate=True), hidden_pre)
    hidden_gradient = gelu_pull(grad_act)[0].astype(jnp.bfloat16)
    up_projection_gradient = jnp.einsum(
        "gih,giv->hv", second_normalized, hidden_gradient, preferred_element_type=jnp.float32
    )
    grad_normed_two = lax.psum(
        jnp.einsum(
            "vwb,kb->vwk", hidden_gradient, up_projection_weight, preferred_element_type=jnp.float32
        ).astype(jnp.bfloat16),
        "mlp",
    ).astype(jnp.float32)
    _, second_pull = jax.vjp(layer_norm, residual, gain_float[1], bias_float[1])
    grad_resid_norm, grad_gain_two, grad_bias_two = second_pull(grad_normed_two)
    grad_resid = grad_out + grad_resid_norm
    grad_resid_low = grad_resid.astype(jnp.bfloat16)
    grad_out_weight = jnp.einsum(
        "slf,lsd->fd", attn_heads, grad_resid_low, preferred_element_type=jnp.float32
    )
    grad_mixed = jnp.einsum(
        "lsd,fd->slf", grad_resid_low, out_weight, preferred_element_type=jnp.float32
    ).astype(jnp.bfloat16)

    def attend_backward(unused, inputs_seq):
        query_seq, pairs_seq, query_rows, key_rows, log_total, grad_seq = inputs_seq
        gathered = lax.all_gather(pairs_seq, "seq", axis=0, tiled=True)
        key_heads, value_heads = split_pairs(gathered)
        logits = (
            jnp.einsum("qhe,khe->hqk", query_seq, key_heads, preferred_element_type=jnp.float32)
            * score_scale
        )
        visible = (query_rows[:, None] == key_rows[None, :])[None]
        attention = jnp.exp(jnp.where(visible, logits - log_total[:, :, None], masked_value))
        attention_low = attention.astype(jnp.bfloat16)
        grad_heads = grad_seq.reshape(local_rows, heads_here, head_size)
        grad_attention = jnp.einsum(
            "qhe,khe->hqk", grad_heads, value_heads, preferred_element_type=jnp.float32
        )
        inner = jnp.sum(grad_attention * attention, axis=2, keepdims=True)
        grad_logits = (attention * (grad_attention - inner)).astype(jnp.bfloat16)
        grad_query = (
            jnp.einsum("hqk,khe->qhe", grad_logits, key_heads, preferred_element_type=jnp.float32)
            * score_scale
        )
        grad_key = (
            jnp.einsum("hqk,qhe->khe", grad_logits, query_seq, preferred_element_type=jnp.float32)
            * score_scale
        )
        grad_value = jnp.einsum(
            "hqk,qhe->khe", attention_low, grad_heads, preferred_element_type=jnp.float32
        )
        grad_pairs = lax.psum_scatter(
            jnp.concatenate(
                [
                    grad_key.reshape(lax.axis_size("seq") * local_rows, head_cols),
                    grad_value.reshape(lax.axis_size("seq") * local_rows, head_cols),
                ],
                axis=1,
            ).astype(jnp.bfloat16),
            "seq",
            scatter_dimension=0,
            tiled=True,
        ).astype(jnp.float32)
        return (unused, (grad_query.reshape(local_rows, head_cols), grad_pairs))

    _, (grad_queries, grad_pairs_all) = lax.scan(
        attend_backward, 0, (query_low, key_pairs, query_segs, key_segs, log_totals, grad_mixed)
    )
    _, query_pull = jax.vjp(head_norm, query_raw, head_float[0])
    grad_query_raw, grad_query_gain = query_pull(grad_queries.reshape(shape_heads))
    _, key_pull = jax.vjp(head_norm, key_raw, head_float[1])
    grad_key_raw, grad_key_gain = key_pull(grad_pairs_all[:, :, :head_cols].reshape(shape_heads))
    grad_projected = jnp.stack(
        [
            grad_query_raw.reshape(seq_here, local_rows, head_cols),
            grad_key_raw.reshape(seq_here, local_rows, head_cols),
            grad_pairs_all[:, :, head_cols:],
        ],
        axis=0,
    ).astype(jnp.bfloat16)
    grad_query_weight = jnp.einsum(
        "lsd,csle->cde", normed, grad_projected, preferred_element_type=jnp.float32
    )
    grad_normed = lax.psum(
        jnp.einsum(
            "csle,cde->lsd", grad_projected, query_weight, preferred_element_type=jnp.float32
        ).astype(jnp.bfloat16),
        "mlp",
    ).astype(jnp.float32)
    _, first_pull = jax.vjp(layer_norm, patch_float, gain_float[0], bias_float[0])
    grad_patch_norm, grad_gain_one, grad_bias_one = first_pull(grad_normed)
    grad_patches = (grad_resid + grad_patch_norm).astype(jnp.bfloat16)
    grad_scale = 1.0 / math.sqrt(lax.axis_size("dp") * seq_here * seq_len)
    term_qkv = grad_query_weight * grad_scale
    term_out = grad_out_weight * grad_scale
    term_up = up_projection_gradient * grad_scale
    term_down = grad_down * grad_scale
    term_gain = jnp.stack([grad_gain_one, grad_gain_two]) * grad_scale
    term_bias = jnp.stack([grad_bias_one, grad_bias_two]) * grad_scale
    term_head = jnp.stack([grad_query_gain, grad_key_gain]) * grad_scale
    summed = (
        lax.psum(term_qkv.astype(jnp.bfloat16), "seq").astype(jnp.float32),
        lax.psum(term_out.astype(jnp.bfloat16), "seq").astype(jnp.float32),
        lax.psum(term_up.astype(jnp.bfloat16), "seq").astype(jnp.float32),
        lax.psum(term_down.astype(jnp.bfloat16), "seq").astype(jnp.float32),
        lax.psum(term_gain.astype(jnp.bfloat16), "seq").astype(jnp.float32),
        lax.psum(term_bias.astype(jnp.bfloat16), "seq").astype(jnp.float32),
        lax.psum(term_head.astype(jnp.bfloat16), "seq").astype(jnp.float32),
    )
    shards = (
        lax.psum_scatter(
            summed[0].astype(jnp.bfloat16), "dp", scatter_dimension=1, tiled=True
        ).astype(jnp.float32),
        lax.psum_scatter(
            summed[1].astype(jnp.bfloat16), "dp", scatter_dimension=1, tiled=True
        ).astype(jnp.float32),
        lax.psum_scatter(
            summed[2].astype(jnp.bfloat16), "dp", scatter_dimension=0, tiled=True
        ).astype(jnp.float32),
        lax.psum_scatter(
            summed[3].astype(jnp.bfloat16), "dp", scatter_dimension=1, tiled=True
        ).astype(jnp.float32),
        lax.psum_scatter(
            summed[4].astype(jnp.bfloat16), "dp", scatter_dimension=1, tiled=True
        ).astype(jnp.float32),
        lax.psum_scatter(
            summed[5].astype(jnp.bfloat16), "dp", scatter_dimension=1, tiled=True
        ).astype(jnp.float32),
        lax.psum_scatter(
            summed[6].astype(jnp.bfloat16), "dp", scatter_dimension=2, tiled=True
        ).astype(jnp.float32),
    )
    return (
        out,
        grad_patches,
        shards[0],
        shards[1],
        shards[2],
        shards[3],
        shards[4],
        shards[5],
        shards[6],
    )


def solution(mesh):
    return jax.shard_map(
        on_device,
        mesh=mesh,
        in_specs=(
            P("seq", "dp", None),
            P(None, "dp"),
            P(None, "dp", "mlp"),
            P("mlp", "dp"),
            P("dp", "mlp"),
            P("mlp", "dp"),
            P(None, "dp"),
            P(None, "dp"),
            P(None, "mlp", "dp"),
            P("seq", "dp", "mlp"),
        ),
        out_specs=(
            P("seq", "dp", "mlp"),
            P("seq", "dp", None),
            P(None, "dp", "mlp"),
            P("mlp", "dp"),
            P("dp", "mlp"),
            P("mlp", "dp"),
            P(None, "dp"),
            P(None, "dp"),
            P(None, "mlp", "dp"),
        ),
        check_vma=False,
    )
```

profile of v0, /device:TPU:0, one launch (start us, length us, event | category | flops | bytes accessed | tf_op | source)
XLA Modules:
  0.0 1770.8 jit_solution(11671423733943078725)
XLA Ops:
  49.7 30.4 %all_gather.36 = bf16[2,6,64]{1,0,2:T(2,128)(2,1)S(1)} all-gather(bf16[2,6,8]{1,0,2:T(2,128)(2,1)S(1)} %copy.64), channel_id=1, replica_groups=mesh['dp'=8,'seq'=2,'mlp'=2] {'dp'}, dimensions={2}, use_global_device_ids=true | all-gather | bytes 1728 | tf_op jit(solution)/shard_map/all_gather | solution.py:45
  89.9 33.5 %all_gather.37 = bf16[384,768]{0,1:T(8,128)(2,1)} all-gather(bf16[384,96]{0,1:T(8,128)(2,1)S(1)} %convert_element_type.206), channel_id=1, replica_groups=mesh['dp'=8,'seq'=2,'mlp'=2] {'dp'}, dimensions={1}, use_global_device_ids=true | all-gather | bytes 663552 | tf_op jit(solution)/shard_map/all_gather | solution.py:40
  163.4 262.5 %while.24 = (s32[]{:T(128)}, bf16[6,512,384]{1,2,0:T(8,128)(2,1)}, f32[6,6,512]{2,1,0:T(8,128)}, bf16[6,512,768]{1,2,0:T(8,128)(2,1)}, s32[6,512]{1,0:T(8,128)S(...) while((s32[]{:T(128)}, bf16[6,512,384]{1,2,0:T(8,128)(2,1)}, ...), condition=%wide.region_9.10_spmd, body=%wide.region_6.9_spmd.sunk | while | flops 843772928 | bytes 54909084 | solution.py:103
  167.1 25.1 %all-gather.26.cloned.1.call-done = bf16[1,1024,768]{1,2,0:T(8,128)(2,1)} async-done(((bf16[1,512,768]{1,2,0:T(8,128)(2,1)}), bf16[1,1024,768]{1,2,0:T(8,128)(2,1)}) %all-gather.26.cloned.1.call-update) | async-done | bytes 1572880 | tf_op jit(solution)/shard_map/while/body/eval_jaxpr/all_gather | solution.py:85
  209.8 26.4 %all-gather.26.cloned.1.call-done = bf16[1,1024,768]{1,2,0:T(8,128)(2,1)} async-done(((bf16[1,512,768]{1,2,0:T(8,128)(2,1)}), bf16[1,1024,768]{1,2,0:T(8,128)(2,1)}) %all-gather.26.cloned.1.call-update) | async-done | bytes 1572880 | tf_op jit(solution)/shard_map/while/body/eval_jaxpr/all_gather | solution.py:85
  253.8 26.2 %all-gather.26.cloned.1.call-done = bf16[1,1024,768]{1,2,0:T(8,128)(2,1)} async-done(((bf16[1,512,768]{1,2,0:T(8,128)(2,1)}), bf16[1,1024,768]{1,2,0:T(8,128)(2,1)}) %all-gather.26.cloned.1.call-update) | async-done | bytes 1572880 | tf_op jit(solution)/shard_map/while/body/eval_jaxpr/all_gather | solution.py:85
  297.6 26.2 %all-gather.26.cloned.1.call-done = bf16[1,1024,768]{1,2,0:T(8,128)(2,1)} async-done(((bf16[1,512,768]{1,2,0:T(8,128)(2,1)}), bf16[1,1024,768]{1,2,0:T(8,128)(2,1)}) %all-gather.26.cloned.1.call-update) | async-done | bytes 1572880 | tf_op jit(solution)/shard_map/while/body/eval_jaxpr/all_gather | solution.py:85
  341.4 26.2 %all-gather.26.cloned.1.call-done = bf16[1,1024,768]{1,2,0:T(8,128)(2,1)} async-done(((bf16[1,512,768]{1,2,0:T(8,128)(2,1)}), bf16[1,1024,768]{1,2,0:T(8,128)(2,1)}) %all-gather.26.cloned.1.call-update) | async-done | bytes 1572880 | tf_op jit(solution)/shard_map/while/body/eval_jaxpr/all_gather | solution.py:85
  385.2 26.4 %all-gather.26.cloned.1.call-done = bf16[1,1024,768]{1,2,0:T(8,128)(2,1)} async-done(((bf16[1,512,768]{1,2,0:T(8,128)(2,1)}), bf16[1,1024,768]{1,2,0:T(8,128)(2,1)}) %all-gather.26.cloned.1.call-update) | async-done | bytes 1572880 | tf_op jit(solution)/shard_map/while/body/eval_jaxpr/all_gather | solution.py:85
  498.1 50.5 %all-gather.20.cloned.1.call-done = bf16[768,1536]{1,0:T(8,128)(2,1)} async-done(((bf16[96,1536]{1,0:T(8,128)(2,1)}), bf16[768,1536]{1,0:T(8,128)(2,1)}) %all-gather.20.cloned.1.call-update) | async-done | bytes 2359312 | tf_op jit(solution)/shard_map/all_gather | solution.py:41
  562.8 39.4 %all-gather.22.cloned.1.call-done = bf16[1536,768]{0,1:T(8,128)(2,1)} async-done(((bf16[1536,96]{0,1:T(8,128)(2,1)}), bf16[1536,768]{0,1:T(8,128)(2,1)}) %all-gather.22.cloned.1.call-update) | async-done | bytes 2359312 | tf_op jit(solution)/shard_map/all_gather | solution.py:42
  651.7 29.8 %all-reduce.7.cloned.1.call-done = bf16[512,6,768]{2,0,1:T(8,128)(2,1)} async-done(((bf16[512,6,768]{2,0,1:T(8,128)(2,1)}), bf16[512,6,768]{2,0,1:T(8,128)(2,1)}) %all-reduce.7.cloned.1.call-update) | async-done | bytes 4718608 | tf_op jit(solution)/shard_map/psum | solution.py:148
  704.0 518.0 %while.25 = (s32[]{:T(128)}, f32[6,512,384]{1,2,0:T(8,128)}, f32[6,512,768]{1,2,0:T(8,128)}, bf16[6,512,768]{1,2,0:T(8,128)(2,1)}, s32[6,512]{1,0:T(8,128)S(1)},...) while((s32[]{:T(128)}, f32[6,512,384]{1,2,0:T(8,128)}, ...), condition=%wide.region_20.21_spmd, body=%wide.region_17.20_spmd.sunk | while | flops 2065888256 | bytes 155556080 | solution.py:207
  709.4 25.4 %all-gather.28.cloned.1.call-done = bf16[1,1024,768]{1,2,0:T(8,128)(2,1)} async-done(((bf16[1,512,768]{1,2,0:T(8,128)(2,1)}), bf16[1,1024,768]{1,2,0:T(8,128)(2,1)}) %all-gather.28.cloned.1.call-update) | async-done | bytes 1572880 | tf_op jit(solution)/shard_map/while/body/eval_jaxpr/all_gather | solution.py:167
  796.6 24.2 %all-gather.28.cloned.1.call-done = bf16[1,1024,768]{1,2,0:T(8,128)(2,1)} async-done(((bf16[1,512,768]{1,2,0:T(8,128)(2,1)}), bf16[1,1024,768]{1,2,0:T(8,128)(2,1)}) %all-gather.28.cloned.1.call-update) | async-done | bytes 1572880 | tf_op jit(solution)/shard_map/while/body/eval_jaxpr/all_gather | solution.py:167
  882.7 24.2 %all-gather.28.cloned.1.call-done = bf16[1,1024,768]{1,2,0:T(8,128)(2,1)} async-done(((bf16[1,512,768]{1,2,0:T(8,128)(2,1)}), bf16[1,1024,768]{1,2,0:T(8,128)(2,1)}) %all-gather.28.cloned.1.call-update) | async-done | bytes 1572880 | tf_op jit(solution)/shard_map/while/body/eval_jaxpr/all_gather | solution.py:167
  968.8 24.2 %all-gather.28.cloned.1.call-done = bf16[1,1024,768]{1,2,0:T(8,128)(2,1)} async-done(((bf16[1,512,768]{1,2,0:T(8,128)(2,1)}), bf16[1,1024,768]{1,2,0:T(8,128)(2,1)}) %all-gather.28.cloned.1.call-update) | async-done | bytes 1572880 | tf_op jit(solution)/shard_map/while/body/eval_jaxpr/all_gather | solution.py:167
  1054.9 24.4 %all-gather.28.cloned.1.call-done = bf16[1,1024,768]{1,2,0:T(8,128)(2,1)} async-done(((bf16[1,512,768]{1,2,0:T(8,128)(2,1)}), bf16[1,1024,768]{1,2,0:T(8,128)(2,1)}) %all-gather.28.cloned.1.call-update) | async-done | bytes 1572880 | tf_op jit(solution)/shard_map/while/body/eval_jaxpr/all_gather | solution.py:167
  1141.1 24.2 %all-gather.28.cloned.1.call-done = bf16[1,1024,768]{1,2,0:T(8,128)(2,1)} async-done(((bf16[1,512,768]{1,2,0:T(8,128)(2,1)}), bf16[1,1024,768]{1,2,0:T(8,128)(2,1)}) %all-gather.28.cloned.1.call-update) | async-done | bytes 1572880 | tf_op jit(solution)/shard_map/while/body/eval_jaxpr/all_gather | solution.py:167
  1330.2 69.8 %reduce-scatter.25.cloned.1.call-done = bf16[1536,96]{0,1:T(8,128)(2,1)} async-done(((bf16[1536,768]{0,1:T(8,128)(2,1)}), bf16[1536,96]{0,1:T(8,128)(2,1)}) %reduce-scatter.25.cloned.1.call-update) | async-done | bytes 294928 | tf_op jit(solution)/shard_map/reduce_scatter | solution.py:261
  1400.0 72.0 %reduce-scatter.23.cloned.1.call-done = bf16[96,1536]{1,0:T(8,128)(2,1)} async-done(((bf16[768,1536]{1,0:T(8,128)(2,1)}), bf16[96,1536]{1,0:T(8,128)(2,1)}) %reduce-scatter.23.cloned.1.call-update) | async-done | bytes 294928 | tf_op jit(solution)/shard_map/reduce_scatter | solution.py:258
  1471.9 65.4 %reduce-scatter.21.cloned.1.call-done = bf16[384,96]{0,1:T(8,128)(2,1)} async-done(((bf16[384,768]{0,1:T(8,128)(2,1)}), bf16[384,96]{0,1:T(8,128)(2,1)}) %reduce-scatter.21.cloned.1.call-update) | async-done | bytes 73744 | tf_op jit(solution)/shard_map/reduce_scatter | solution.py:255
  1658.8 33.6 %reduce-scatter.33.cloned.1.call-done = bf16[96,2]{1,0:T(8,128)(2,1)} async-done(((bf16[768,2]{1,0:T(8,128)(2,1)}), bf16[96,2]{1,0:T(8,128)(2,1)}) %reduce-scatter.33.cloned.1.call-update) | async-done | bytes 400
  1693.2 62.9 %reduce-scatter.35.cloned.1.call-done = bf16[96,2]{1,0:T(8,128)(2,1)} async-done(((bf16[768,2]{1,0:T(8,128)(2,1)}), bf16[96,2]{1,0:T(8,128)(2,1)}) %reduce-scatter.35.cloned.1.call-update) | async-done | bytes 400
  (542 shorter events, 962.5 us)
Async XLA Ops:
  7.2 116.2 %all-gather.16.cloned.1.call-start = ((), (), s32[]{:S(2)}) async-start(), calls=%async_computation.9 | async-start | bytes 1990656 | tf_op jit(solution)/shard_map/all_gather | solution.py:39
  425.9 36.2 %reduce-scatter.27.cloned.1.call-start = ((), (), s32[]{:S(2)}) async-start(), calls=%async_computation.19 | async-start | bytes 7077888
  449.3 43.2 %all-gather.18.cloned.1.call-start = ((), (), s32[]{:S(2)}) async-start(), calls=%async_computation.10 | async-start | bytes 7077888 | tf_op jit(solution)/shard_map/all_gather | solution.py:116
  476.8 71.7 %all-gather.20.cloned.1.call-start = ((), (), s32[]{:S(2)}) async-start(), calls=%async_computation.11 | async-start | bytes 2654208 | tf_op jit(solution)/shard_map/all_gather | solution.py:41
  477.7 124.5 %all-gather.22.cloned.1.call-start = ((), (), s32[]{:S(2)}) async-start(), calls=%async_computation.12 | async-start | bytes 2654208 | tf_op jit(solution)/shard_map/all_gather | solution.py:42
  478.5 138.0 %all-gather.24.cloned.1.call-start = ((), (), s32[]{:S(2)}) async-start(), calls=%async_computation.13 | async-start | bytes 7077888 | tf_op jit(solution)/shard_map/all_gather | solution.py:131
  479.1 202.4 %all-reduce.7.cloned.1.call-start = ((), (), s32[]{:S(2)}) async-start(), calls=%async_computation.14 | async-start | bytes 9437184 | tf_op jit(solution)/shard_map/psum | solution.py:148
  704.0 30.7 %all-gather.28.cloned.1.call-start = ((), (), s32[]{:S(2)}) async-start(), calls=%async_computation.26 | async-start | bytes 2359296 | tf_op jit(solution)/shard_map/while/body/eval_jaxpr/all_gather | solution.py:167
  706.2 82.6 %reduce-scatter.37.cloned.1.call-start = ((), (), s32[]{:S(2)}) async-start(), calls=%async_computation.27 | async-start | bytes 2359296 | tf_op jit(solution)/shard_map/while/body/eval_jaxpr/reduce_scatter | solution.py:193
  793.4 81.5 %reduce-scatter.37.cloned.1.call-start = ((), (), s32[]{:S(2)}) async-start(), calls=%async_computation.27 | async-start | bytes 2359296 | tf_op jit(solution)/shard_map/while/body/eval_jaxpr/reduce_scatter | solution.py:193
  879.5 81.4 %reduce-scatter.37.cloned.1.call-start = ((), (), s32[]{:S(2)}) async-start(), calls=%async_computation.27 | async-start | bytes 2359296 | tf_op jit(solution)/shard_map/while/body/eval_jaxpr/reduce_scatter | solution.py:193
  965.6 81.5 %reduce-scatter.37.cloned.1.call-start = ((), (), s32[]{:S(2)}) async-start(), calls=%async_computation.27 | async-start | bytes 2359296 | tf_op jit(solution)/shard_map/while/body/eval_jaxpr/reduce_scatter | solution.py:193
  1049.6 29.7 %all-gather.28.cloned.1.call-start = ((), (), s32[]{:S(2)}) async-start(), calls=%async_computation.26 | async-start | bytes 2359296 | tf_op jit(solution)/shard_map/while/body/eval_jaxpr/all_gather | solution.py:167
  1051.7 81.7 %reduce-scatter.37.cloned.1.call-start = ((), (), s32[]{:S(2)}) async-start(), calls=%async_computation.27 | async-start | bytes 2359296 | tf_op jit(solution)/shard_map/while/body/eval_jaxpr/reduce_scatter | solution.py:193
  1138.0 81.5 %reduce-scatter.37.cloned.1.call-start = ((), (), s32[]{:S(2)}) async-start(), calls=%async_computation.27 | async-start | bytes 2359296 | tf_op jit(solution)/shard_map/while/body/eval_jaxpr/reduce_scatter | solution.py:193
  1222.0 106.3 %reduce-scatter.31.cloned.1.call-start = ((), (), s32[]{:S(2)}) async-start(), calls=%async_computation.21 | async-start | bytes 1990656
  1262.0 138.0 %reduce-scatter.25.cloned.1.call-start = ((), (), s32[]{:S(2)}) async-start(), calls=%async_computation.18 | async-start | bytes 2654208 | tf_op jit(solution)/shard_map/reduce_scatter | solution.py:261
  1278.4 193.5 %reduce-scatter.23.cloned.1.call-start = ((), (), s32[]{:S(2)}) async-start(), calls=%async_computation.17 | async-start | bytes 2654208 | tf_op jit(solution)/shard_map/reduce_scatter | solution.py:258
  1294.2 243.2 %reduce-scatter.21.cloned.1.call-start = ((), (), s32[]{:S(2)}) async-start(), calls=%async_computation.16 | async-start | bytes 663552 | tf_op jit(solution)/shard_map/reduce_scatter | solution.py:255
  1304.9 303.7 %all-reduce.11.cloned.1.call-start = ((), (), s32[]{:S(2)}) async-start(), calls=%async_computation.24 | async-start | bytes 1916928 | tf_op jit(solution)/shard_map/psum | solution.py:243
  1537.4 78.3 %all-reduce.9.cloned.1.call-start = ((), (), s32[]{:S(2)}) async-start(), calls=%async_computation.15 | async-start | bytes 9437184 | tf_op jit(solution)/shard_map/psum | solution.py:225
  1547.7 83.2 %reduce-scatter.29.cloned.1.call-start = ((), (), s32[]{:S(2)}) async-start(), calls=%async_computation.20 | async-start | bytes 7077888
  1582.0 110.4 %reduce-scatter.33.cloned.1.call-start = ((), (), s32[]{:S(2)}) async-start(), calls=%async_computation.22 | async-start | bytes 221184
  1630.3 125.9 %reduce-scatter.35.cloned.1.call-start = ((), (), s32[]{:S(2)}) async-start(), calls=%async_computation.23 | async-start | bytes 221184
  (95 other events, 3660.7 us)
Sparse Core Ops, SparseCore 0:
  10.8 48.4 all-gather.15
  209.0 27.1 all-gather.25
  252.8 27.2 all-gather.25
  296.6 27.2 all-gather.25
  340.4 27.2 all-gather.25
  384.3 27.1 all-gather.25
  495.3 53.2 all-gather.19
  551.5 50.5 all-gather.21
  651.1 30.3 all-reduce.6
  706.3 28.3 all-gather.27
  793.6 27.2 all-gather.27
  848.8 26.0 reduce-scatter.36
  879.6 27.2 all-gather.27
  965.7 27.2 all-gather.27
  1052.0 27.2 all-gather.27
  1138.1 27.2 all-gather.27
  1262.0 66.1 reduce-scatter.30
  1332.0 67.9 reduce-scatter.24
  1403.9 68.0 reduce-scatter.22
  1476.1 61.1 reduce-scatter.20
  1540.3 37.6 all-reduce.10
  1580.6 29.3 all-reduce.8
  1630.4 61.9 reduce-scatter.32
  1696.0 60.0 reduce-scatter.34
  (10 shorter events, 210.3 us)
where the time goes:
time: 1780 us; the launch traced here: 1770 us
  waiting for transfers between devices  906 us (51%)
  matrix products  313 us (18%)
  other arithmetic  223 us (13%)
  local copies, waits for them, and re-layouts  182 us (10%)
  blocking collectives  127 us (7%)
    all_gather x6, waiting for transfers between devices, attend_forward(): gathered = lax.all_gather(pairs_seq, 'seq', axis=0, tiled=True)  157 us
    all_gather x6, waiting for transfers between devices, attend_backward(): gathered = lax.all_gather(pairs_seq, 'seq', axis=0, tiled=True)  147 us
    unnamed x21, waiting for transfers between devices  126 us
    reduce_scatter x6, waiting for transfers between devices, attend_backward(): lax.psum_scatter(jnp.concatenate([grad_key.reshape(lax.axis_size('seq') *...  123 us
    unnamed x178, local copies, waits for them, and re-layouts  79.2 us
    reduce_scatter x1, waiting for transfers between devices, on_device(): lax.psum_scatter(summed[2].astype(jnp.bfloat16), 'dp', scatter_dimension=...  72 us
    reduce_scatter x1, waiting for transfers between devices, on_device(): lax.psum_scatter(summed[3].astype(jnp.bfloat16), 'dp', scatter_dimension=...  69.8 us
    reduce_scatter x1, waiting for transfers between devices, on_device(): lax.psum_scatter(summed[1].astype(jnp.bfloat16), 'dp', scatter_dimension=...  65.4 us
  transfers between devices with their start and end apart: 34, of which 30 were waited for; matrix products, arithmetic and copies ran while one was open for 14% of the time, Pallas kernels for 0%

commit v1 on v0

--- a/solution.py
+++ b/solution.py
@@ -4,6 +4,8 @@
 import jax
 import jax.numpy as jnp
 from jax import lax
+from jax.experimental import pallas as pl
+from jax.experimental.pallas import tpu as pltpu
 from jax.sharding import PartitionSpec as P
 
 norm_eps = 1e-06
@@ -284,9 +286,687 @@
     )
 
 
+low = jnp.bfloat16
+wide = jnp.float32
+log2e = math.log2(math.e)
+mask_weight = 128.0
+query_block = 256
+windows = (384, 512, 1024)
+vmem_bytes = 56 * 1024 * 1024
+
+
+def dot(left, right, left_dim=1, right_dim=0):
+    return lax.dot_general(
+        left, right, (((left_dim,), (right_dim,)), ((), ())), preferred_element_type=wide
+    )
+
+
+def params(count):
+    return pltpu.CompilerParams(
+        dimension_semantics=("arbitrary",) * count, vmem_limit_bytes=vmem_bytes
+    )
+
+
+def split_dot(values, ones_matrix):
+    top = values.astype(low)
+    rest = (values - top.astype(wide)).astype(low)
+    return dot(top, ones_matrix) + dot(rest, ones_matrix)
+
+
+def qkv_kernel(
+    x_ref, gain_ref, bias_ref, w_ref, hg_ref, mean_ref, q_ref, k_ref, v_ref, rq_ref, rk_ref, h_ref
+):
+    x = x_ref[0].astype(wide)
+    centered = x - jnp.mean(x, axis=1, keepdims=True)
+    variance = jnp.mean(centered * centered, axis=1, keepdims=True)
+    h = (centered * lax.rsqrt(variance + norm_eps) * gain_ref[...] + bias_ref[...]).astype(low)
+    h_ref[0] = h
+    cols = q_ref.shape[2]
+    means = mean_ref[...]
+    for index, out_ref, rate_ref in ((0, q_ref, rq_ref), (1, k_ref, rk_ref)):
+        raw = dot(h, w_ref[:, cols * index : cols * (index + 1)])
+        inner = raw - split_dot(raw, means)
+        rate = lax.rsqrt(dot((inner * inner).astype(low), means) + norm_eps)
+        rate_ref[0] = rate
+        out_ref[0] = (inner * rate * hg_ref[index : index + 1, :]).astype(low)
+    v_ref[0] = dot(h, w_ref[:, 2 * cols :]).astype(low)
+
+
+def attn_fwd_kernel(start_ref, kind_ref, q_ref, k_ref, v_ref, aug_ref, side_ref, o_ref, inv_ref):
+    seq = pl.program_id(0)
+    blocks = q_ref.shape[1] // query_block
+    lane = lax.broadcasted_iota(jnp.int32, (query_block, 128), 1)
+
+    def step(block, carry):
+        row = pl.multiple_of(block * query_block, query_block)
+        which = seq * blocks + block
+
+        def body(size):
+            begin = pl.multiple_of(start_ref[which], 16)
+            q_pair = q_ref[0, pl.ds(row, query_block), :]
+            q_side = aug_ref[0, pl.ds(row, query_block), :] * side_ref[...]
+            keys = jnp.concatenate(
+                [k_ref[0, pl.ds(begin, size), :], aug_ref[0, pl.ds(begin, size), :]], axis=1
+            )
+            values = jnp.concatenate(
+                [v_ref[0, pl.ds(begin, size), :], jnp.ones((size, 128), low)], axis=1
+            )
+            mixed = []
+            for head in range(2):
+                mine = jnp.where(lane // 64 == head, q_pair, jnp.zeros_like(q_pair))
+                scores = dot(jnp.concatenate([mine, q_side], axis=1), keys, 1, 1)
+                mixed.append(dot(jnp.exp2(scores).astype(low), values))
+            inverse = 1.0 / jnp.where(lane < 64, mixed[0][:, 128:], mixed[1][:, 128:])
+            outcome = jnp.where(lane < 64, mixed[0][:, :128], mixed[1][:, :128]) * inverse
+            o_ref[0, pl.ds(row, query_block), :] = outcome.astype(low)
+            inv_ref[0, pl.ds(row, query_block), :] = inverse
+
+        for index, size in enumerate(windows):
+            pl.when(kind_ref[which] == index)(partial(body, size))
+        return carry
+
+    lax.fori_loop(0, blocks, step, 0)
+
+
+def attn_bwd_kernel(
+    start_ref,
+    kind_ref,
+    q_ref,
+    k_ref,
+    v_ref,
+    go_ref,
+    o_ref,
+    inv_ref,
+    rq_ref,
+    rk_ref,
+    aug_ref,
+    side_ref,
+    hg_ref,
+    mean_ref,
+    gq_ref,
+    gk_ref,
+    gv_ref,
+    gain_ref,
+    gq_acc,
+    gk_acc,
+    gv_acc,
+):
+    seq = pl.program_id(1)
+    blocks = q_ref.shape[1] // query_block
+    lane = lax.broadcasted_iota(jnp.int32, (query_block, 128), 1)
+    gk_acc[...] = jnp.zeros_like(gk_acc)
+    gv_acc[...] = jnp.zeros_like(gv_acc)
+
+    def step(block, carry):
+        row = pl.multiple_of(block * query_block, query_block)
+        which = seq * blocks + block
+
+        def body(size):
+            begin = pl.multiple_of(start_ref[which], 16)
+            rows = pl.ds(row, query_block)
+            span = pl.ds(begin, size)
+            q_pair = q_ref[0, rows, :]
+            q_side = aug_ref[0, rows, :] * side_ref[...]
+            k_pair = k_ref[0, span, :]
+            k_side = aug_ref[0, span, :]
+            keys = jnp.concatenate([k_pair, k_side], axis=1)
+            values = jnp.concatenate([v_ref[0, span, :], k_side], axis=1)
+            scaled = go_ref[0, rows, :].astype(wide) * inv_ref[0, rows, :]
+            scaled_low = scaled.astype(low)
+            product = scaled_low.astype(wide) * o_ref[0, rows, :].astype(wide)
+            powers, grads, queries, pulls = [], [], [], []
+            for head in range(2):
+                mine = lane // 64 == head
+                inner = jnp.sum(jnp.where(mine, product, 0.0), axis=1, keepdims=True)
+                one = inner.astype(low)
+                two = (inner - one.astype(wide)).astype(low)
+                three = (inner - one.astype(wide) - two.astype(wide)).astype(low)
+                go_side = jnp.where(
+                    lane == 6,
+                    -one,
+                    jnp.where(lane == 7, -two, jnp.where(lane == 8, -three, jnp.zeros_like(q_pair))),
+                )
+                q_mine = jnp.where(mine, q_pair, jnp.zeros_like(q_pair))
+                go_mine = jnp.where(mine, scaled_low, jnp.zeros_like(q_pair))
+                power = jnp.exp2(dot(keys, jnp.concatenate([q_mine, q_side], axis=1), 1, 1))
+                slope = dot(values, jnp.concatenate([go_mine, go_side], axis=1), 1, 1)
+                grad = (power * slope).astype(low)
+                powers.append(power.astype(low))
+                grads.append(grad)
+                queries.append(q_mine)
+                pulls.append(go_mine)
+            gv_acc[span, :] += dot(
+                jnp.concatenate(powers, axis=1), jnp.concatenate(pulls, axis=0)
+            )
+            gk_acc[span, :] += dot(
+                jnp.concatenate(grads, axis=1), jnp.concatenate(queries, axis=0)
+            )
+            gq_acc[rows, :] = jnp.where(
+                lane < 64, dot(grads[0], k_pair, 0, 0), dot(grads[1], k_pair, 0, 0)
+            )
+
+        for index, size in enumerate(windows):
+            pl.when(kind_ref[which] == index)(partial(body, size))
+        return carry
+
+    lax.fori_loop(0, blocks, step, 0)
+    gv_ref[0] = gv_acc[...].astype(low)
+    means = mean_ref[...]
+
+    @pl.when(seq == 0)
+    def _():
+        gain_ref[...] = jnp.zeros_like(gain_ref)
+
+    for index, acc, raw_ref, rate_ref, out_ref, scale, unscale in (
+        (0, gq_acc, q_ref, rq_ref, gq_ref, 0.125, 8.0 / log2e),
+        (1, gk_acc, k_ref, rk_ref, gk_ref, 1.0 / log2e, 1.0),
+    ):
+        gain = hg_ref[index : index + 1, :]
+        grad = acc[...] * scale
+        normed = raw_ref[0].astype(wide) * unscale
+        weighted = grad * gain
+        cross = grad * normed
+        first = split_dot(weighted, means)
+        second = split_dot(cross, means)
+        out_ref[0] = (rate_ref[0] * (weighted - first - normed / gain * second)).astype(low)
+        gain_ref[0, index : index + 1, :] += jnp.sum(cross, axis=0, keepdims=True) / gain
+
+
+def attn_out_kernel(
+    o_mine_ref, o_other_ref, w_mine_ref, w_other_ref, x_ref, gy_ref, gain_ref, bias_ref,
+    x2_ref, h_ref, ht_ref, gyt_ref,
+):
+    x2 = (
+        x_ref[...].astype(wide)
+        + dot(o_mine_ref[...], w_mine_ref[...], 1, 1)
+        + dot(o_other_ref[...], w_other_ref[...], 1, 1)
+    )
+    x2_ref[...] = x2
+    centered = x2 - jnp.mean(x2, axis=1, keepdims=True)
+    variance = jnp.mean(centered * centered, axis=1, keepdims=True)
+    h = centered * lax.rsqrt(variance + norm_eps) * gain_ref[...] + bias_ref[...]
+    h_ref[...] = h.astype(low)
+    ht_ref[...] = jnp.transpose(h).astype(low)
+    gyt_ref[...] = jnp.transpose(gy_ref[...].astype(wide)).astype(low)
+
+
+def mlp_kernel(
+    first, scale, h_ref, ht_ref, gy_ref, gyt_ref, up_mine_ref, up_other_ref, down_mine_ref,
+    down_other_ref, *refs,
+):
+    if first:
+        out_in_ref, *refs = refs
+    else:
+        out_in_ref, gh_in_ref, *refs = refs
+    out_ref, gh_ref, *refs = refs
+    grad_refs, accs = refs[:4], refs[4:]
+    step = pl.program_id(0)
+    h = h_ref[...]
+    gy = gy_ref[...]
+    out_sum = out_in_ref[...]
+    gh_sum = None if first else gh_in_ref[...]
+    root = math.sqrt(2.0 / math.pi)
+    for up_ref, down_ref, up_acc, down_acc in (
+        (up_mine_ref, down_mine_ref, accs[0], accs[1]),
+        (up_other_ref, down_other_ref, accs[2], accs[3]),
+    ):
+        up = up_ref[...]
+        down = down_ref[...]
+        t = dot(h, up)
+        square = t * t
+        gate = 0.5 + 0.5 * jnp.tanh(t * (root + (root * 0.044715) * square))
+        act = t * gate
+        slope = gate + 2.0 * act * (1.0 - gate) * (root + (3.0 * root * 0.044715) * square)
+        act_low = act.astype(low)
+        grad = (dot(gy, down) * slope).astype(low)
+        out_sum = out_sum + dot(act_low, down, 1, 1)
+        back = dot(grad, up, 1, 1)
+        gh_sum = back if gh_sum is None else gh_sum + back
+        up_grad = dot(ht_ref[...], grad)
+        down_grad = dot(gyt_ref[...], act_low)
+
+        @pl.when(step == 0)
+        def _():
+            up_acc[...] = up_grad
+            down_acc[...] = down_grad
+
+        @pl.when(step > 0)
+        def _():
+            up_acc[...] += up_grad
+            down_acc[...] += down_grad
+
+    out_ref[...] = out_sum
+    gh_ref[...] = gh_sum
+
+    @pl.when(step == pl.num_programs(0) - 1)
+    def _():
+        for ref, acc in zip(grad_refs, accs):
+            ref[...] = (acc[...] * scale).astype(low)
+
+
+def second_norm_kernel(
+    scale, x2_ref, gh_ref, gy_ref, y_ref, valid_ref, o_mine_ref, o_other_ref, w_mine_ref,
+    w_other_ref, gain_ref, out_ref, gx_ref, go_mine_ref, go_other_ref, gw_mine_ref, gw_other_ref,
+    sums_ref, acc_mine, acc_other,
+):
+    step = pl.program_id(0)
+    x2 = x2_ref[...]
+    gh = gh_ref[...]
+    out_ref[...] = (y_ref[...] * valid_ref[...][:, :1]).astype(low)
+    centered = x2 - jnp.mean(x2, axis=1, keepdims=True)
+    rate = lax.rsqrt(jnp.mean(centered * centered, axis=1, keepdims=True) + norm_eps)
+    normed = centered * rate
+    weighted = gh * gain_ref[...]
+    gx = gy_ref[...].astype(wide) + rate * (
+        weighted
+        - jnp.mean(weighted, axis=1, keepdims=True)
+        - normed * jnp.mean(weighted * normed, axis=1, keepdims=True)
+    )
+    gx_ref[...] = gx
+    gx_low = gx.astype(low)
+    go_mine_ref[...] = dot(gx_low, w_mine_ref[...]).astype(low)
+    go_other_ref[...] = dot(gx_low, w_other_ref[...]).astype(low)
+    gx_turned = jnp.transpose(gx).astype(low)
+
+    @pl.when(step == 0)
+    def _():
+        sums_ref[...] = jnp.zeros_like(sums_ref)
+        acc_mine[...] = jnp.zeros_like(acc_mine)
+        acc_other[...] = jnp.zeros_like(acc_other)
+
+    sums_ref[0:1, :] += jnp.sum(gh * normed, axis=0, keepdims=True)
+    sums_ref[1:2, :] += jnp.sum(gh, axis=0, keepdims=True)
+    acc_mine[...] += dot(gx_turned, o_mine_ref[...])
+    acc_other[...] += dot(gx_turned, o_other_ref[...])
+
+    @pl.when(step == pl.num_programs(0) - 1)
+    def _():
+        gw_mine_ref[...] = (acc_mine[...] * scale).astype(low)
+        gw_other_ref[...] = (acc_other[...] * scale).astype(low)
+
+
+def first_norm_kernel(x_ref, a_ref, b_ref, gx2_ref, gain_ref, out_ref, sums_ref):
+    x = x_ref[...].astype(wide)
+    gh = a_ref[...].astype(wide) + b_ref[...].astype(wide)
+    centered = x - jnp.mean(x, axis=1, keepdims=True)
+    rate = lax.rsqrt(jnp.mean(centered * centered, axis=1, keepdims=True) + norm_eps)
+    normed = centered * rate
+    weighted = gh * gain_ref[...]
+    out_ref[...] = (
+        gx2_ref[...]
+        + rate
+        * (
+            weighted
+            - jnp.mean(weighted, axis=1, keepdims=True)
+            - normed * jnp.mean(weighted * normed, axis=1, keepdims=True)
+        )
+    ).astype(low)
+
+    @pl.when(pl.program_id(0) == 0)
+    def _():
+        sums_ref[...] = jnp.zeros_like(sums_ref)
+
+    sums_ref[0:1, :] += jnp.sum(gh * normed, axis=0, keepdims=True)
+    sums_ref[1:2, :] += jnp.sum(gh, axis=0, keepdims=True)
+
+
+def shape_of(dims, kind=low):
+    return jax.ShapeDtypeStruct(dims, kind)
+
+
+def window_table(segs, blocks):
+    length = segs.shape[1]
+    pad_begin = jnp.sum((segs >= 0).astype(jnp.int32), axis=1, keepdims=True)
+    begins = jnp.where(segs >= 0, segs, pad_begin)
+    size = length // blocks
+    firsts = begins[:, ::size]
+    lasts = begins[:, size - 1 :: size]
+    ends = jnp.sum((begins[:, None, :] <= lasts[:, :, None]).astype(jnp.int32), axis=2)
+    reach = ends - firsts
+    kinds = jnp.zeros_like(reach)
+    spans = jnp.full_like(reach, windows[0])
+    for index in range(1, len(windows)):
+        larger = reach > windows[index - 1]
+        kinds = jnp.where(larger, index, kinds)
+        spans = jnp.where(larger, windows[index], spans)
+    starts = jnp.minimum(firsts, length - spans)
+    return starts.reshape(-1), kinds.reshape(-1)
+
+
+def mask_columns(segs):
+    codes = (segs + 16) // 16
+    lane = jnp.arange(128, dtype=jnp.int32)
+    bits = (codes[:, :, None] >> jnp.minimum(lane, 5)) & 1
+    signs = (2 * bits - 1).astype(wide)
+    return jnp.where(lane < 6, signs, jnp.where(lane < 9, 1.0, 0.0)).astype(low)
+
+
+def swap(values, axis):
+    return lax.ppermute(values, axis, [(0, 1), (1, 0)])
+
+
+def in_order(index, mine, other, axis):
+    return jnp.where(
+        index == 0,
+        jnp.concatenate([mine, other], axis=axis),
+        jnp.concatenate([other, mine], axis=axis),
+    )
+
+
+def pick(values, index, axis):
+    return lax.dynamic_index_in_dim(values, index, axis, keepdims=False)
+
+
+def on_device_small(
+    patches, segments, w_qkv, w_out, w_up, w_down, ln_gain, ln_bias, head_gain, cotangent
+):
+    half, seqs_all, width = patches.shape
+    length = 2 * half
+    seqs = seqs_all // 2
+    cols = w_qkv.shape[2]
+    part = half // 2
+    y = lax.axis_index("seq")
+    c = lax.axis_index("mlp")
+    dp_size = lax.axis_size("dp")
+    scale = 1.0 / math.sqrt(dp_size * seqs_all * length)
+    own_rows = seqs * 2 * part
+    hidden = w_up.shape[1]
+
+    gather = partial(lax.all_gather, axis_name="dp", axis=0, tiled=True)
+    w_in = gather(jnp.transpose(w_qkv.astype(low), (1, 0, 2)).reshape(-1, 3 * cols))
+    w_o = gather(jnp.transpose(w_out.astype(low)))
+    w_u = gather(w_up.astype(low))
+    w_d = gather(jnp.transpose(w_down.astype(low)))
+    small = gather(
+        jnp.concatenate(
+            [jnp.transpose(ln_gain), jnp.transpose(ln_bias)], axis=1
+        ).astype(low)
+    )
+    gains = jnp.transpose(small[:, :2]).astype(wide)
+    biases = jnp.transpose(small[:, 2:]).astype(wide)
+    head_gains = lax.all_gather(head_gain.astype(low), "dp", axis=2, tiled=True)
+    head_gains = head_gains.reshape(2, cols).astype(wide)
+    w_o_other = swap(w_o, "mlp")
+    w_u_other = swap(w_u, "mlp")
+    w_d_other = swap(w_d, "mlp")
+
+    turned = jnp.transpose(patches, (1, 0, 2)).reshape(2, seqs, 2, part, width)
+    mine = pick(turned, y, 0)
+    sent = pick(pick(turned, 1 - y, 0), c, 1)
+    got = swap(sent, "seq")
+    got_other = swap(got, "mlp")
+    other = in_order(c, got[:, None], got_other[:, None], 1)
+    x = in_order(y, mine[:, None], other[:, None], 1)
+    segs = lax.dynamic_slice_in_dim(jnp.transpose(segments), y * seqs, seqs, 0)
+
+    cot = cotangent.reshape(2, part, seqs_all, cols)
+    cot_other = swap(pick(cot, 1 - c, 0), "mlp")
+    cot = jnp.transpose(in_order(c, pick(cot, c, 0), cot_other, 2), (1, 0, 2))
+    cot = cot.reshape(2, seqs, part, width)
+    cot_got = swap(pick(cot, 1 - y, 0), "seq")
+    cot = in_order(y, pick(cot, y, 0)[:, None], cot_got[:, None], 1)
+    valid = pick((segs >= 0).reshape(seqs, 2, 2, part), c, 2)
+    gy = jnp.where(valid[..., None], cot, jnp.zeros_like(cot)).reshape(own_rows, width)
+    valid = jnp.broadcast_to(valid.reshape(own_rows, 1).astype(wide), (own_rows, 128))
+    x_own = pick(x, c, 2).reshape(own_rows, width)
+    x = x.reshape(seqs, length, width)
+
+    starts, kinds = window_table(segs, length // query_block)
+    aug = mask_columns(segs)
+    lanes = jnp.arange(128)
+    side = jnp.where(lanes < 6, mask_weight, jnp.where(lanes == 6, -6.0 * mask_weight, 0.0))
+    side = side.astype(low)[None]
+    index = jnp.arange(cols)
+    means = jnp.where(index[:, None] // 64 == index[None] // 64, 1.0 / 64, 0.0).astype(low)
+    block = 512
+    row_spec = pl.BlockSpec((1, block, width), lambda i, j: (i, j, 0))
+    col_spec = pl.BlockSpec((1, block, cols), lambda i, j: (i, j, 0))
+
+    def whole(dims):
+        return pl.BlockSpec(dims, lambda *ids: (0,) * len(dims))
+
+    q, k, v, rate_q, rate_k, h1 = pl.pallas_call(
+        qkv_kernel,
+        grid=(seqs, length // block),
+        in_specs=[
+            row_spec,
+            whole((1, width)),
+            whole((1, width)),
+            whole((width, 3 * cols)),
+            whole((2, cols)),
+            whole((cols, cols)),
+        ],
+        out_specs=[col_spec] * 5 + [row_spec],
+        out_shape=[shape_of((seqs, length, cols))] * 3
+        + [shape_of((seqs, length, cols), wide)] * 2
+        + [shape_of((seqs, length, width))],
+        compiler_params=params(2),
+        name="qkv",
+    )(
+        x,
+        gains[:1],
+        biases[:1],
+        w_in,
+        head_gains * jnp.array([[log2e / 8.0], [1.0]], wide),
+        means,
+    )
+    pairs = cols // 128
+
+    def pair_spec(order):
+        return pl.BlockSpec((1, length, 128), lambda *ids: order(*ids))
+
+    by_seq = pair_spec(lambda s, p, *_: (s, 0, p))
+    aug_seq = pair_spec(lambda s, p, *_: (s, 0, 0))
+    o, inverse = pl.pallas_call(
+        attn_fwd_kernel,
+        grid_spec=pltpu.PrefetchScalarGridSpec(
+            num_scalar_prefetch=2,
+            grid=(seqs, pairs),
+            in_specs=[by_seq, by_seq, by_seq, aug_seq, whole((1, 128))],
+            out_specs=[by_seq, by_seq],
+        ),
+        out_shape=[shape_of((seqs, length, cols)), shape_of((seqs, length, cols), wide)],
+        compiler_params=params(2),
+        name="attn_fwd",
+    )(starts, kinds, q, k, v, aug, side)
+
+    o_parts = o.reshape(seqs, 2, 2, part, cols)
+    o_mine = pick(o_parts, c, 2).reshape(own_rows, cols)
+    o_other = swap(pick(o_parts, 1 - c, 2), "mlp").reshape(own_rows, cols)
+    steps = own_rows // block
+    rows_spec = pl.BlockSpec((block, width), lambda i: (i, 0))
+    turned_spec = pl.BlockSpec((width, block), lambda i: (0, i))
+    part_spec = pl.BlockSpec((block, cols), lambda i: (i, 0))
+    x2, h2, h2t, gyt = pl.pallas_call(
+        attn_out_kernel,
+        grid=(steps,),
+        in_specs=[
+            part_spec,
+            part_spec,
+            whole((width, cols)),
+            whole((width, cols)),
+            rows_spec,
+            rows_spec,
+            whole((1, width)),
+            whole((1, width)),
+        ],
+        out_specs=[rows_spec, rows_spec, turned_spec, turned_spec],
+        out_shape=[
+            shape_of((own_rows, width), wide),
+            shape_of((own_rows, width)),
+            shape_of((width, own_rows)),
+            shape_of((width, own_rows)),
+        ],
+        compiler_params=params(1),
+        name="attn_out",
+    )(o_mine, o_other, w_o, w_o_other, x_own, gy, gains[1:], biases[1:])
+
+    chunk = 512
+    chunks = hidden // chunk
+    total, gh = x2, None
+    up_grads, down_grads = [], []
+    for f in range(chunks):
+        weight_spec = pl.BlockSpec((width, chunk), lambda i, f=f: (0, f))
+        grad_spec = whole((width, chunk))
+        first = f == 0
+        carried = [total] if first else [total, gh]
+        total, gh, *grads = pl.pallas_call(
+            partial(mlp_kernel, first, scale),
+            grid=(steps,),
+            in_specs=[rows_spec, turned_spec, rows_spec, turned_spec]
+            + [weight_spec] * 4
+            + [rows_spec] * len(carried),
+            out_specs=[rows_spec] * 2 + [grad_spec] * 4,
+            out_shape=[shape_of((own_rows, width), wide)] * 2 + [shape_of((width, chunk))] * 4,
+            scratch_shapes=[pltpu.VMEM((width, chunk), wide)] * 4,
+            compiler_params=params(1),
+            name="mlp",
+        )(h2, h2t, gy, gyt, w_u, w_u_other, w_d, w_d_other, *carried)
+        up_grads.append((grads[0], grads[2]))
+        down_grads.append((grads[1], grads[3]))
+
+    out_rows, gx2, go_mine, go_other, gwo_mine, gwo_other, second_sums = pl.pallas_call(
+        partial(second_norm_kernel, scale),
+        grid=(steps,),
+        in_specs=[
+            rows_spec,
+            rows_spec,
+            rows_spec,
+            rows_spec,
+            pl.BlockSpec((block, 128), lambda i: (i, 0)),
+            part_spec,
+            part_spec,
+            whole((width, cols)),
+            whole((width, cols)),
+            whole((1, width)),
+        ],
+        out_specs=[
+            rows_spec,
+            rows_spec,
+            part_spec,
+            part_spec,
+            whole((width, cols)),
+            whole((width, cols)),
+            whole((8, width)),
+        ],
+        out_shape=[
+            shape_of((own_rows, width)),
+            shape_of((own_rows, width), wide),
+            shape_of((own_rows, cols)),
+            shape_of((own_rows, cols)),
+            shape_of((width, cols)),
+            shape_of((width, cols)),
+            shape_of((8, width), wide),
+        ],
+        scratch_shapes=[pltpu.VMEM((width, cols), wide)] * 2,
+        compiler_params=params(1),
+        name="second_norm",
+    )(x2, gh, gy, total, valid, o_mine, o_other, w_o, w_o_other, gains[1:])
+
+    go_shape = (seqs, 2, 1, part, cols)
+    go = in_order(c, go_mine.reshape(go_shape), swap(go_other, "mlp").reshape(go_shape), 2)
+    go = go.reshape(seqs, length, cols)
+    by_pair = pair_spec(lambda p, s, *_: (s, 0, p))
+    gain_spec = pl.BlockSpec((2, 128), lambda p, s, *_: (0, p))
+    gq, gk, gv, gain_sums = pl.pallas_call(
+        attn_bwd_kernel,
+        grid_spec=pltpu.PrefetchScalarGridSpec(
+            num_scalar_prefetch=2,
+            grid=(pairs, seqs),
+            in_specs=[by_pair] * 8
+            + [
+                pair_spec(lambda p, s, *_: (s, 0, 0)),
+                whole((1, 128)),
+                gain_spec,
+                whole((128, 128)),
+            ],
+            out_specs=[by_pair] * 3 + [pl.BlockSpec((1, 8, 128), lambda p, s, *_: (p, 0, 0))],
+            scratch_shapes=[pltpu.VMEM((length, 128), wide)] * 3,
+        ),
+        out_shape=[shape_of((seqs, length, cols))] * 3 + [shape_of((pairs, 8, 128), wide)],
+        compiler_params=params(2),
+        name="attn_bwd",
+    )(starts, kinds, q, k, v, go, o, inverse, rate_q, rate_k, aug, side, head_gains, means[:128, :128])
+
+    gw_in = jnp.concatenate(
+        [
+            jnp.einsum("sld,slf->df", h1, grad, preferred_element_type=wide)
+            for grad in (gq, gk, gv)
+        ],
+        axis=1,
+    )
+    gw_in = (gw_in * scale).astype(low)
+    gh1 = sum(
+        jnp.einsum(
+            "slf,df->sld",
+            grad,
+            w_in[:, cols * i : cols * (i + 1)],
+            preferred_element_type=wide,
+        )
+        for i, grad in enumerate((gq, gk, gv))
+    ).astype(low)
+    gh1 = gh1.reshape(seqs, 2, 2, part, width)
+    gh1_got = swap(pick(gh1, 1 - c, 2), "mlp").reshape(own_rows, width)
+    gh1_own = pick(gh1, c, 2).reshape(own_rows, width)
+    grad_rows, first_sums = pl.pallas_call(
+        first_norm_kernel,
+        grid=(steps,),
+        in_specs=[rows_spec] * 4 + [whole((1, width))],
+        out_specs=[rows_spec, whole((8, width))],
+        out_shape=[shape_of((own_rows, width)), shape_of((8, width), wide)],
+        compiler_params=params(1),
+        name="first_norm",
+    )(x_own, gh1_own, gh1_got, gx2, gains[:1])
+
+    def all_seqs(rows):
+        rows = rows.reshape(seqs, 2, part, width)
+        return in_order(y, pick(rows, y, 1), swap(pick(rows, 1 - y, 1), "seq"), 0)
+
+    out_six = all_seqs(out_rows).reshape(seqs_all, part, 2, cols)
+    out_got = swap(pick(out_six, 1 - c, 2), "mlp")
+    out = in_order(c, pick(out_six, c, 2), out_got, 1)
+    out = jnp.transpose(out, (1, 0, 2))
+    grad_six = all_seqs(grad_rows)
+    grad_patches = jnp.transpose(in_order(c, grad_six, swap(grad_six, "mlp"), 1), (1, 0, 2))
+
+    def over_cores(mine, other):
+        return (mine.astype(wide) + swap(other, "mlp").astype(wide)).astype(low)
+
+    gw_up = jnp.concatenate([over_cores(*pair) for pair in up_grads], axis=1)
+    gw_down = jnp.concatenate([over_cores(*pair) for pair in down_grads], axis=1)
+    gw_out = over_cores(gwo_mine, gwo_other)
+
+    def shard(grad):
+        mine = lax.psum_scatter(grad, "dp", scatter_dimension=0, tiled=True)
+        return mine.astype(wide) + swap(mine, "seq").astype(wide)
+
+    gw_in, gw_out, gw_up, gw_down = (shard(g) for g in (gw_in, gw_out, gw_up, gw_down))
+    d = lax.axis_index("dp")
+    norm_sums = lax.psum(
+        jnp.concatenate([first_sums[:2], second_sums[:2]]) * scale, ("dp", "seq", "mlp")
+    )
+    norm_sums = lax.dynamic_slice_in_dim(norm_sums, d * (width // dp_size), width // dp_size, 1)
+    head_sums = lax.psum(jnp.transpose(gain_sums[:, :2], (1, 0, 2)) * scale, ("dp", "seq"))
+    head_sums = head_sums.reshape(2, cols // 64, 64)
+    head_sums = lax.dynamic_slice_in_dim(head_sums, d * (64 // dp_size), 64 // dp_size, 2)
+    return (
+        out,
+        grad_patches,
+        jnp.transpose(gw_in.reshape(-1, 3, cols), (1, 0, 2)),
+        jnp.transpose(gw_out),
+        gw_up,
+        jnp.transpose(gw_down),
+        norm_sums[0::2],
+        norm_sums[1::2],
+        head_sums,
+    )
+
+
 def solution(mesh):
+    shape = dict(mesh.shape)
+    small = shape["seq"] == 2 and shape["mlp"] == 2 and shape["dp"] == 8
     return jax.shard_map(
-        on_device,
+        on_device_small if small else on_device,
         mesh=mesh,
         in_specs=(
             P("seq", "dp", None),

time: 1780 us -> 687 us (0.39)
  waiting for transfers between devices: 906 us -> 130 us
  matrix products: 313 us -> 22.6 us
  Pallas kernels: 0 us -> 228 us
  other arithmetic: 223 us -> 53.1 us
  local copies, waits for them, and re-layouts: 182 us -> 55.1 us
  blocking collectives: 127 us -> 159 us
    all_gather x17 -> x3, waiting for transfers between devices: 420 us -> 66 us  [the longest x1 34.2 us: on_device_small(): gather(jnp.transpose(w_qkv.astype(low), (1, 0, 2)).reshape(-1, 3 * cols))]
    reduce_scatter x9 -> x3, waiting for transfers between devices: 330 us -> 15.5 us  [shard(): mine = lax.psum_scatter(grad, 'dp', scatter_dimension=0, tiled=True)]
    dot_general x54 -> x6, matrix products: 313 us -> 22.6 us  [the longest x3 14.6 us: on_device_small(): jnp.einsum('slf,df->sld', grad, w_in[:, cols * i:cols * (i + 1)], preferr...]
    pallas_call x0 -> x9, Pallas kernels: none -> 228 us  [the longest x3 81 us: on_device_small(): pl.pallas_call(partial(mlp_kernel, first, scale), grid=(steps,), in_specs...]
    unnamed x21 -> x8, waiting for transfers between devices: 126 us -> 0.12 us
    reduce_sum x24 -> x2, other arithmetic: 91 us -> 1.11 us  [the longest x1 0.88 us: window_table(): pad_begin = jnp.sum((segs >= 0).astype(jnp.int32), axis=1, keepdims=True)]
    convert_element_type x29 -> x15, other arithmetic: 89.1 us -> 12.1 us  [the longest x7 6.53 us: over_cores(): return (mine.astype(wide) + swap(other, 'mlp').astype(wide)).astype(low)]
    psum x1 -> x2, blocking collectives: 4.99 us -> 75.9 us  [the longest x1 38.4 us: on_device_small(): lax.psum(jnp.concatenate([first_sums[:2], second_sums[:2]]) * scale, ('dp...]
  transfers between devices with their start and end apart: 34 -> 32, of which waited for: 30 -> 11; matrix products, arithmetic and copies ran while one was open for 14% -> 17% of each run, Pallas kernels for 0% -> 19%
where the time goes in v1:
time: 687 us; the launch traced here: 681 us
  Pallas kernels  228 us (33%)
  blocking collectives  159 us (23%)
  waiting for transfers between devices  130 us (19%)
  local copies, waits for them, and re-layouts  55.1 us (8%)
  other arithmetic  53.1 us (8%)
  matrix products  22.6 us (3%)
  starting transfers between devices  17.8 us (3%)
  between operations  15.1 us (2%)
    pallas_call x3, Pallas kernels, on_device_small(): pl.pallas_call(partial(mlp_kernel, first, scale), grid=(steps,), in_specs...  81 us
    pallas_call x1, Pallas kernels, on_device_small(): pl.pallas_call(attn_bwd_kernel, grid_spec=pltpu.PrefetchScalarGridSpec(nu...  59 us
    ppermute x25, waiting for transfers between devices, swap(): return lax.ppermute(values, axis, [(0, 1), (1, 0)])  48.4 us
    psum x1, blocking collectives, on_device_small(): lax.psum(jnp.concatenate([first_sums[:2], second_sums[:2]]) * scale, ('dp...  38.4 us
    psum x1, blocking collectives, on_device_small(): lax.psum(jnp.transpose(gain_sums[:, :2], (1, 0, 2)) * scale, ('dp', 'seq'))  37.6 us
    all_gather x1, waiting for transfers between devices, on_device_small(): gather(jnp.transpose(w_qkv.astype(low), (1, 0, 2)).reshape(-1, 3 * cols))  34.2 us
    all_gather x1, waiting for transfers between devices, on_device_small(): w_u = gather(w_up.astype(low))  31.8 us
    all_gather x1, blocking collectives, on_device_small(): w_o = gather(jnp.transpose(w_out.astype(low)))  31.7 us
  transfers between devices with their start and end apart: 32, of which 11 were waited for; matrix products, arithmetic and copies ran while one was open for 17% of the time, Pallas kernels for 19%

profile of v1, /device:TPU:0, one launch (start us, length us, event | category | flops | bytes accessed | tf_op | source)
XLA Modules:
  0.0 681.3 jit_solution(18115231480255049359)
XLA Ops:
  25.5 20.9 %all-gather = bf16[8,96,4]{1,2,0:T(4,128)(2,1)S(1)} all-gather(bf16[1,96,4]{1,2,0:T(4,128)(2,1)S(1)} %maximum_bitcast_fusion), channel_id=1, replica_groups=mesh['dp'=8,'seq'=2,'mlp'=2] {'dp'}, dimensions={0}, use_global_device_ids=true | all-gather | bytes 6912 | tf_op jit(solution)/shard_map/all_gather | solution.py:680
  46.5 30.6 %all_gather.20 = bf16[2,6,64]{1,0,2:T(2,128)(2,1)S(1)} all-gather(bf16[2,6,8]{1,0,2:T(2,128)(2,1)S(1)} %copy.127), channel_id=1, replica_groups=mesh['dp'=8,'seq'=2,'mlp'=2] {'dp'}, dimensions={2}, use_global_device_ids=true | all-gather | bytes 1728 | tf_op jit(solution)/shard_map/all_gather | solution.py:687
  87.5 31.8 %all-gather.7.cloned.1.call-done.up_mine_ref = bf16[768,1536]{1,0:T(8,128)(2,1)} async-done(((bf16[96,1536]{1,0:T(8,128)(2,1)}), bf16[768,1536]{1,0:T(8,128)(2,1)}) %all-gather.7.cloned.1.call-update) | async-done | bytes 2359312 | tf_op jit(solution)/shard_map/all_gather | solution.py:678
  131.9 34.2 %all-gather.5.cloned.1.call-done.w_ref = bf16[768,1152]{1,0:T(8,128)(2,1)} async-done(((bf16[96,1152]{1,0:T(8,128)(2,1)}), bf16[768,1152]{1,0:T(8,128)(2,1)}) %all-gather.5.cloned.1.call-update) | async-done | bytes 1769488 | tf_op jit(solution)/shard_map/all_gather | solution.py:676
  166.1 23.6 %qkv.1 = (bf16[3,1024,384]{2,1,0:T(8,128)(2,1)}, bf16[3,1024,384]{2,1,0:T(8,128)(2,1)}, bf16[3,1024,384]{2,1,0:T(8,128)(2,1)}, f32[3,1024,384]{2,1,0:T(8,128)}, ...) custom-call(bf16[3,1024,768]{2,1,0:T(8,128)(2,1)} %bitcast.130, f32[1,768]{1,0:T(1,128)} %get-tuple-element.164.gain_ref, ...), custom_call_target="tpu_custom_call" | custom-call | tf_op jit(solution)/shard_map/qkv/pallas_call | solution.py:728
  189.6 29.8 %attn_fwd.1 = (bf16[3,1024,384]{2,1,0:T(8,128)(2,1)}, f32[3,1024,384]{2,1,0:T(8,128)}) custom-call(s32[12]{0:T(128)} %reshape.287.start_ref, s32[12]{0:T(128)} %reshape.288.kind_ref, bf16[3,1024,384]{2,1,0:T(8,128)(2,1)} %get-tuple-element.52.q_ref, bf16[3,1024,384]{2,1,0:T(8,128)(2,1)} %get-tuple-element.53.k_ref, ...), custom_call_target="tpu_custom_call" | custom-call | tf_op jit(solution)/shard_map/attn_fwd/pallas_call | solution.py:760
  222.7 31.7 %all_gather.21.w_mine_ref = bf16[768,384]{1,0:T(8,128)(2,1)S(1)} all-gather(bf16[96,384]{1,0:T(8,128)(2,1)S(1)} %copy-done.20), channel_id=1, replica_groups=mesh['dp'=8,'seq'=2,'mlp'=2] {'dp'}, dimensions={0}, use_global_device_ids=true | all-gather | bytes 663552 | tf_op jit(solution)/shard_map/all_gather | solution.py:677
  262.5 10.4 %attn_out.1 = (f32[1536,768]{1,0:T(8,128)}, bf16[1536,768]{1,0:T(8,128)(2,1)}, bf16[768,1536]{1,0:T(8,128)(2,1)}, bf16[768,1536]{1,0:T(8,128)(2,1)}) custom-call(bf16[1536,384]{1,0:T(8,128)(2,1)} %bitcast.131, bf16[1536,384]{1,0:T(8,128)(2,1)} %bitcast.18.o_other_ref, bf16[768,384]{1,0:T(8,128)(2,1)} %copy-done.4, bf16[768,384]{1,0:T(8,128)(2,1)} %copy-done.7, ...), custom_call_target="tpu_custom_call" | custom-call | tf_op jit(solution)/shard_map/attn_out/pallas_call | solution.py:780
  274.3 26.8 %mlp.3 = (f32[1536,768]{1,0:T(8,128)}, f32[1536,768]{1,0:T(8,128)}, bf16[768,512]{1,0:T(8,128)(2,1)}, bf16[768,512]{1,0:T(8,128)(2,1)}, bf16[768,512]{1,0:T(8,128)(2,1)}, /*index=5*/bf16[768,512]{1,0:T(8,128)(2,1)}) custom-call(bf16[1536,768]{1,0:T(8,128)(2,1)} %get-tuple-element.57.h_ref, bf16[768,1536]{1,0:T(8,128)(2,1)} %get-tuple-element.58.ht_ref, ...), custom_call_target="tpu_custom_call" | custom-call | tf_op jit(solution)/shard_map/mlp/pallas_call | solution.py:813
  301.2 27.0 %mlp.4 = (f32[1536,768]{1,0:T(8,128)}, f32[1536,768]{1,0:T(8,128)}, bf16[768,512]{1,0:T(8,128)(2,1)}, bf16[768,512]{1,0:T(8,128)(2,1)}, bf16[768,512]{1,0:T(8,128)(2,1)}, /*index=5*/bf16[768,512]{1,0:T(8,128)(2,1)}) custom-call(bf16[1536,768]{1,0:T(8,128)(2,1)} %get-tuple-element.57.h_ref, bf16[768,1536]{1,0:T(8,128)(2,1)} %get-tuple-element.58.ht_ref, ...), custom_call_target="tpu_custom_call" | custom-call | tf_op jit(solution)/shard_map/mlp/pallas_call | solution.py:813
  328.1 27.2 %mlp.5 = (f32[1536,768]{1,0:T(8,128)}, f32[1536,768]{1,0:T(8,128)}, bf16[768,512]{1,0:T(8,128)(2,1)}, bf16[768,512]{1,0:T(8,128)(2,1)}, bf16[768,512]{1,0:T(8,128)(2,1)}, /*index=5*/bf16[768,512]{1,0:T(8,128)(2,1)}) custom-call(bf16[1536,768]{1,0:T(8,128)(2,1)} %get-tuple-element.57.h_ref, bf16[768,1536]{1,0:T(8,128)(2,1)} %get-tuple-element.58.ht_ref, ...), custom_call_target="tpu_custom_call" | custom-call | tf_op jit(solution)/shard_map/mlp/pallas_call | solution.py:813
  356.5 16.7 %second_norm.1 = (bf16[1536,768]{1,0:T(8,128)(2,1)}, f32[1536,768]{1,0:T(8,128)}, bf16[1536,384]{1,0:T(8,128)(2,1)}, bf16[1536,384]{1,0:T(8,128)(2,1)}, bf16[768...) custom-call(f32[1536,768]{1,0:T(8,128)} %get-tuple-element.56.refs_0_.x2_ref, ...), custom_call_target="tpu_custom_call" | custom-call | tf_op jit(solution)/shard_map/second_norm/pallas_call | solution.py:828
  381.1 59.0 %attn_bwd.1 = (bf16[3,1024,384]{2,1,0:T(8,128)(2,1)}, bf16[3,1024,384]{2,1,0:T(8,128)(2,1)}, bf16[3,1024,384]{2,1,0:T(8,128)(2,1)}, f32[3,8,128]{2,1,0:T(8,128)}) custom-call(s32[12]{0:T(128)} %reshape.287.start_ref, s32[12]{0:T(128)} %reshape.288.kind_ref, bf16[3,1024,384]{2,1,0:T(8,128)(2,1)} %get-tuple-element.52.q_ref, ...), custom_call_target="tpu_custom_call" | custom-call | tf_op jit(solution)/shard_map/attn_bwd/pallas_call | solution.py:871
  461.7 3.9 fusion.3
  469.3 7.0 %add_convert_fusion = bf16[3,1024,768]{2,1,0:T(8,128)(2,1)} fusion(f32[3,1024,768]{2,1,0:T(8,128)S(1)} %fusion.4, f32[3,1024,768]{2,1,0:T(8,128)S(1)} %fusion.3, bf16[3,1024,384]{2,1,0:T(8,128)(2,1)} %get-tuple-element.74, bf16[768,1152]{1,0:T(8,128)(2,1)} %all-gather.5.cloned.1.call-done.w_ref), kind=kOutput, calls=%fused_computation | convolution fusion | flops 1819017216 | bytes 26542080 | tf_op jit(solution)/shard_map/slf,df->sld/dot_general | solution.py:900
  476.3 5.0 dynamic-slice_bitcast_fusion
  489.6 8.0 %first_norm.1 = (bf16[1536,768]{1,0:T(8,128)(2,1)}, f32[8,768]{1,0:T(8,128)}) custom-call(bf16[1536,768]{1,0:T(8,128)(2,1)} %bitcast.129, bf16[1536,768]{1,0:T(8,128)(2,1)} %bitcast.135, bf16[1536,768]{1,0:T(8,128)(2,1)} %bitcast.53.b_ref, f32[1536,768]{1,0:T(8,128)} %get-tuple-element.75.gx2_ref, f32[1,768]{1,0:T(1,128)} %get-tuple-element.164.gain_ref), custom_call_target="tpu_custom_call" | custom-call | tf_op jit(solution)/shard_map/first_norm/pallas_call | solution.py:911
  503.1 15.6 %collective-permute-done.8 = bf16[3,256,768]{1,2,0:T(8,128)(2,1)} collective-permute-done((bf16[3,256,768]{1,2,0:T(8,128)(2,1)}, bf16[3,256,768]{1,2,0:T(8,128)(2,1)}, u32[]{:S(2)}, u32[]{:S(2)}) %collective-permute-start.8) | collective-permute-done | bytes 1179680 | tf_op jit(solution)/shard_map/ppermute | solution.py:645
  524.5 18.7 %collective-permute-done.12 = bf16[3,256,768]{2,1,0:T(8,128)(2,1)} collective-permute-done((bf16[3,256,768]{2,1,0:T(8,128)(2,1)}, bf16[3,256,768]{2,1,0:T(8,128)(2,1)}, u32[]{:S(2)}, u32[]{:S(2)}) %collective-permute-start.12) | collective-permute-done | bytes 1179680 | tf_op jit(solution)/shard_map/ppermute | solution.py:645
  547.7 37.6 %psum.15 = f32[2,6,64]{2,1,0:T(8,128)S(1)} all-reduce(f32[2,6,64]{2,1,0:T(8,128)S(1)} %reshape.306), channel_id=1, replica_groups=mesh['dp'=8,'seq'=2,'mlp'=2] {'dp','seq'}, use_global_device_ids=true, to_apply=%region_7.8 | all-reduce | flops 768 | bytes 6144 | tf_op jit(solution)/shard_map/psum | solution.py:949
  598.5 38.4 %psum.14 = f32[4,768]{1,0:T(4,128)S(1)} all-reduce(f32[4,768]{1,0:T(4,128)S(1)} %maximum_multiply_fusion.1), channel_id=1, replica_groups=mesh['dp'=8,'seq'=2,'mlp'=2] {'dp','seq','mlp'}, use_global_device_ids=true, to_apply=%region_6.7 | all-reduce | flops 3072 | bytes 24576 | tf_op jit(solution)/shard_map/psum | solution.py:945
  642.4 15.5 %reduce-scatter.11.cloned.1.call-done = bf16[96,1536]{1,0:T(8,128)(2,1)} async-done(((bf16[768,1536]{1,0:T(8,128)(2,1)}), bf16[96,1536]{1,0:T(8,128)(2,1)}) %reduce-scatter.11.cloned.1.call-update) | async-done | bytes 294928 | tf_op jit(solution)/shard_map/reduce_scatter | solution.py:940
  661.3 4.6 collective-permute-done.24
  667.7 6.3 fusion
  (227 shorter events, 136.1 us)
Async XLA Ops:
  7.2 79.8 %all-gather.9.cloned.1.call-start = ((), (), s32[]{:S(2)}) async-start(), calls=%async_computation.6 | async-start | bytes 2654208 | tf_op jit(solution)/shard_map/all_gather | solution.py:679
  9.2 110.2 %all-gather.7.cloned.1.call-start = ((), (), s32[]{:S(2)}) async-start(), calls=%async_computation.5 | async-start | bytes 2654208 | tf_op jit(solution)/shard_map/all_gather | solution.py:678
  11.1 155.0 %all-gather.5.cloned.1.call-start = ((), (), s32[]{:S(2)}) async-start(), calls=%async_computation.4 | async-start | bytes 1990656 | tf_op jit(solution)/shard_map/all_gather | solution.py:676
  13.5 67.4 %collective-permute-start = (bf16[3,256,768]{2,1,0:T(8,128)(2,1)}, bf16[3,256,768]{2,1,0:T(8,128)(2,1)}, u32[]{:S(2)}, u32[]{:S(2)}) collective-permute-start(bf16[3,256,768]{2,1,0:T(8,128)(2,1)} %dynamic-slice_bitcast_fusion.8), channel_id=1, source_target_pairs={{0,2},{2,0},{1,3},{3,1},{4,6},{6,4},{5,7},{7,5},{8,10},{10,8},{9,1... | collective-permute-start | bytes 3538952 | tf_op jit(solution)/shard_map/ppermute | solution.py:645
  17.8 67.5 %collective-permute-start.4 = (bf16[256,6,384]{2,0,1:T(8,128)(2,1)}, bf16[256,6,384]{2,0,1:T(8,128)(2,1)S(1)}, u32[]{:S(2)}, u32[]{:S(2)}) collective-permute-start(bf16[256,6,384]{2,0,1:T(8,128)(2,1)} %get-tuple-element.156), channel_id=1, source_target_pairs={{0,1},{1,0},{2,3},{3,2},{4,5},{5,4},{6,7},{7,6},{8,9},{9,8},{10,11... | collective-permute-start | bytes 3538952 | tf_op jit(solution)/shard_map/ppermute | solution.py:645
  18.6 566.7 %reduce-scatter.7.cloned.1.call-start = ((), (), s32[]{:S(2)}) async-start(), calls=%async_computation.7 | async-start | bytes 663552 | tf_op jit(solution)/shard_map/reduce_scatter | solution.py:940
  81.0 43.1 %collective-permute-start.1 = (bf16[3,256,768]{2,1,0:T(8,128)(2,1)}, bf16[3,256,768]{2,1,0:T(8,128)(2,1)S(1)}, u32[]{:S(2)}, u32[]{:S(2)}) collective-permute-start(bf16[3,256,768]{2,1,0:T(8,128)(2,1)} %collective-permute-done), channel_id=1, source_target_pairs={{0,1},{1,0},{2,3},{3,2},{4,5},{5,4},{6,7},{7,6},{8,9},{9,8},{10,11... | collective-permute-start | bytes 3538952 | tf_op jit(solution)/shard_map/ppermute | solution.py:645
  87.0 185.9 %collective-permute-start.7 = (bf16[768,1536]{1,0:T(8,128)(2,1)}, bf16[768,1536]{1,0:T(8,128)(2,1)S(1)}, u32[]{:S(2)}, u32[]{:S(2)}) collective-permute-start(bf16[768,1536]{1,0:T(8,128)(2,1)} %all-gather.9.cloned.1.call-done.down_mine_ref), channel_id=1, source_target_pairs={{0,1},{1,0},{2,3},{3,2},{4,5},{5,4},{6,7},{7,6},{8,9},{9,8},{10,11... | collective-permute-start | bytes 7077896 | tf_op jit(solution)/shard_map/ppermute | solution.py:645
  119.4 153.6 %collective-permute-start.6 = (bf16[768,1536]{1,0:T(8,128)(2,1)}, bf16[768,1536]{1,0:T(8,128)(2,1)}, u32[]{:S(2)}, u32[]{:S(2)}) collective-permute-start(bf16[768,1536]{1,0:T(8,128)(2,1)} %all-gather.7.cloned.1.call-done.up_mine_ref), channel_id=1, source_target_pairs={{0,1},{1,0},{2,3},{3,2},{4,5},{5,4},{6,7},{7,6},{8,9},{9,8},{10,11... | collective-permute-start | bytes 7077896 | tf_op jit(solution)/shard_map/ppermute | solution.py:645
  122.6 135.3 %collective-permute-start.5 = (bf16[3,256,768]{2,1,0:T(8,128)(2,1)}, bf16[3,256,768]{2,1,0:T(8,128)(2,1)}, u32[]{:S(2)}, u32[]{:S(2)}) collective-permute-start(bf16[3,256,768]{2,1,0:T(8,128)(2,1)} %get-tuple-element.154), channel_id=1, source_target_pairs={{0,2},{2,0},{1,3},{3,1},{4,6},{6,4},{5,7},{7,5},{8,10},{10,8},{9,1... | collective-permute-start | bytes 3538952 | tf_op jit(solution)/shard_map/ppermute | solution.py:645
  222.7 39.0 %collective-permute-start.2 = (bf16[3,2,256,384]{3,2,1,0:T(8,128)(2,1)}, bf16[3,2,256,384]{3,2,1,0:T(8,128)(2,1)}, u32[]{:S(2)}, u32[]{:S(2)}) collective-permute-start(bf16[3,2,256,384]{3,2,1,0:T(8,128)(2,1)} %get-tuple-element.157), channel_id=1, source_target_pairs={{0,1},{1,0},{2,3},{3,2},{4,5},{5,4},{6,7},{7,6},{8,9},{9,8},{10,11... | collective-permute-start | bytes 3538952 | tf_op jit(solution)/shard_map/ppermute | solution.py:645
  379.2 216.3 %reduce-scatter.13.cloned.1.call-start = ((), (), s32[]{:S(2)}) async-start(), calls=%async_computation.10 | async-start | bytes 1990656
  450.8 187.2 %reduce-scatter.9.cloned.1.call-start = ((), (), s32[]{:S(2)}) async-start(), calls=%async_computation.8 | async-start | bytes 2654208 | tf_op jit(solution)/shard_map/reduce_scatter | solution.py:940
  458.0 199.9 %reduce-scatter.11.cloned.1.call-start = ((), (), s32[]{:S(2)}) async-start(), calls=%async_computation.9 | async-start | bytes 2654208 | tf_op jit(solution)/shard_map/reduce_scatter | solution.py:940
  458.5 23.2 %collective-permute-start.23 = (bf16[768,512]{1,0:T(8,128)(2,1)}, bf16[768,512]{1,0:T(8,128)(2,1)}, u32[]{:S(2)}, u32[]{:S(2)}) collective-permute-start(bf16[768,512]{1,0:T(8,128)(2,1)} %get-tuple-element.91), channel_id=1, source_target_pairs={{0,1},{1,0},{2,3},{3,2},{4,5},{5,4},{6,7},{7,6},{8,9},{9,8},{10,11... | collective-permute-start | bytes 2359304 | tf_op jit(solution)/shard_map/ppermute | solution.py:645
  458.6 24.5 %collective-permute-start.22 = (bf16[768,512]{1,0:T(8,128)(2,1)}, bf16[768,512]{1,0:T(8,128)(2,1)}, u32[]{:S(2)}, u32[]{:S(2)}) collective-permute-start(bf16[768,512]{1,0:T(8,128)(2,1)} %get-tuple-element.89), channel_id=1, source_target_pairs={{0,1},{1,0},{2,3},{3,2},{4,5},{5,4},{6,7},{7,6},{8,9},{9,8},{10,11... | collective-permute-start | bytes 2359304 | tf_op jit(solution)/shard_map/ppermute | solution.py:645
  481.3 8.3 %collective-permute-start.11 = (bf16[3,2,256,768]{3,2,1,0:T(8,128)(2,1)}, bf16[3,2,256,768]{3,2,1,0:T(8,128)(2,1)}, u32[]{:S(2)}, u32[]{:S(2)}) collective-permute-start(bf16[3,2,256,768]{3,2,1,0:T(8,128)(2,1)} %get-tuple-element.145), channel_id=1, source_target_pairs={{0,1},{1,0},{2,3},{3,2},{4,5},{5,4},{6,7},{7,6},{8,9},{9,8},{10,11... | collective-permute-start | bytes 7077896 | tf_op jit(solution)/shard_map/ppermute | solution.py:645
  489.6 29.1 %collective-permute-start.8 = (bf16[3,256,768]{1,2,0:T(8,128)(2,1)}, bf16[3,256,768]{1,2,0:T(8,128)(2,1)}, u32[]{:S(2)}, u32[]{:S(2)}) collective-permute-start(bf16[3,256,768]{1,2,0:T(8,128)(2,1)} %bitcast.35), channel_id=1, source_target_pairs={{0,2},{2,0},{1,3},{3,1},{4,6},{6,4},{5,7},{7,5},{8,10},{10,8},{9,1... | collective-permute-start | bytes 3538952 | tf_op jit(solution)/shard_map/ppermute | solution.py:645
  500.4 42.8 %collective-permute-start.12 = (bf16[3,256,768]{2,1,0:T(8,128)(2,1)}, bf16[3,256,768]{2,1,0:T(8,128)(2,1)}, u32[]{:S(2)}, u32[]{:S(2)}) collective-permute-start(bf16[3,256,768]{2,1,0:T(8,128)(2,1)} %get-tuple-element.148), channel_id=1, source_target_pairs={{0,2},{2,0},{1,3},{3,1},{4,6},{6,4},{5,7},{7,5},{8,10},{10,8},{9,1... | collective-permute-start | bytes 3538952 | tf_op jit(solution)/shard_map/ppermute | solution.py:645
  523.2 68.4 %collective-permute-start.9 = (bf16[6,256,384]{2,1,0:T(8,128)(2,1)}, bf16[6,256,384]{2,1,0:T(8,128)(2,1)}, u32[]{:S(2)}, u32[]{:S(2)}) collective-permute-start(bf16[6,256,384]{2,1,0:T(8,128)(2,1)} %bitcast.38), channel_id=1, source_target_pairs={{0,1},{1,0},{2,3},{3,2},{4,5},{5,4},{6,7},{7,6},{8,9},{9,8},{10,11... | collective-permute-start | bytes 3538952 | tf_op jit(solution)/shard_map/ppermute | solution.py:645
  545.1 122.6 %collective-permute-start.13 = (bf16[6,256,768]{2,1,0:T(8,128)(2,1)S(1)}, bf16[6,256,768]{2,1,0:T(8,128)(2,1)}, u32[]{:S(2)}, u32[]{:S(2)}) collective-permute-start(bf16[6,256,768]{2,1,0:T(8,128)(2,1)S(1)} %maximum_select_fusion.8), channel_id=1, source_target_pairs={{0,1},{1,0},{2,3},{3,2},{4,5},{5,4},{6,7},{7,6},{8,9},{9,8},{10,11... | collective-permute-start | bytes 7077896 | tf_op jit(solution)/shard_map/ppermute | solution.py:645
  596.7 43.7 %collective-permute-start.14 = (bf16[96,1152]{0,1:T(8,128)(2,1)S(1)}, bf16[96,1152]{0,1:T(8,128)(2,1)}, u32[]{:S(2)}, u32[]{:S(2)}) collective-permute-start(bf16[96,1152]{0,1:T(8,128)(2,1)S(1)} %copy.151), channel_id=1, source_target_pairs={{0,2},{2,0},{1,3},{3,1},{4,6},{6,4},{5,7},{7,5},{8,10},{10,8},{9,1... | collective-permute-start | bytes 663560 | tf_op jit(solution)/shard_map/ppermute | solution.py:645
  638.1 21.3 %collective-permute-start.20 = (bf16[96,1536]{1,0:T(8,128)(2,1)}, bf16[96,1536]{1,0:T(8,128)(2,1)}, u32[]{:S(2)}, u32[]{:S(2)}) collective-permute-start(bf16[96,1536]{1,0:T(8,128)(2,1)} %reduce-scatter.9.cloned.1.call-done), channel_id=1, source_target_pairs={{0,2},{2,0},{1,3},{3,1},{4,6},{6,4},{5,7},{7,5},{8,10},{10,8},{9,1... | collective-permute-start | bytes 884744 | tf_op jit(solution)/shard_map/ppermute | solution.py:645
  657.9 8.0 %collective-permute-start.24 = (bf16[96,1536]{1,0:T(8,128)(2,1)}, bf16[96,1536]{1,0:T(8,128)(2,1)S(1)}, u32[]{:S(2)}, u32[]{:S(2)}) collective-permute-start(bf16[96,1536]{1,0:T(8,128)(2,1)} %reduce-scatter.11.cloned.1.call-done), channel_id=1, source_target_pairs={{0,2},{2,0},{1,3},{3,1},{4,6},{6,4},{5,7},{7,5},{8,10},{10,8},{9,1... | collective-permute-start | bytes 884744 | tf_op jit(solution)/shard_map/ppermute | solution.py:645
  (41 other events, 369.1 us)
Sparse Core Ops, SparseCore 0:
  10.8 55.1 all-gather.8
  68.7 50.5 all-gather.6
  121.6 44.4 all-gather.4
  379.4 58.4 reduce-scatter.6
  451.0 62.6 reduce-scatter.12
  517.0 67.9 reduce-scatter.8
  589.0 68.8 reduce-scatter.10

commit v2 on v0

--- a/solution.py
+++ b/solution.py
@@ -4,6 +4,8 @@
 import jax
 import jax.numpy as jnp
 from jax import lax
+from jax.experimental import pallas as pl
+from jax.experimental.pallas import tpu as pltpu
 from jax.sharding import PartitionSpec as P
 
 norm_eps = 1e-06
@@ -284,9 +286,1019 @@
     )
 
 
+low = jnp.bfloat16
+wide = jnp.float32
+log2e = math.log2(math.e)
+mask_weight = 128.0
+query_block = 256
+windows = (384, 512, 1024)
+vmem_bytes = 56 * 1024 * 1024
+micros = {
+    "qkv": 23,
+    "attn_fwd": 29,
+    "attn_out": 13,
+    "mlp": 26,
+    "second_norm": 18,
+    "attn_bwd": 53,
+    "gw_in": 11,
+    "gh1": 12,
+    "first_norm": 10,
+}
+
+
+def dot(left, right, left_dim=1, right_dim=0):
+    return lax.dot_general(
+        left, right, (((left_dim,), (right_dim,)), ((), ())), preferred_element_type=wide
+    )
+
+
+def params(count):
+    return pltpu.CompilerParams(
+        dimension_semantics=("arbitrary",) * count, vmem_limit_bytes=vmem_bytes
+    )
+
+
+def split_dot(values, ones_matrix):
+    top = values.astype(low)
+    rest = (values - top.astype(wide)).astype(low)
+    return dot(top, ones_matrix) + dot(rest, ones_matrix)
+
+
+def load_pieces(info_ref, sets, scratch, sems):
+    copies = []
+    rows = scratch.shape[0] // 8
+    for number, (pieces, first, count, target) in enumerate(sets):
+        for index in range(8):
+            if len(pieces) == 8:
+                piece = pieces[index]
+            else:
+                piece = pieces[index % 2].at[index // 2]
+            place = pl.multiple_of(info_ref[2 + index] * rows, rows)
+            copies.append(
+                pltpu.make_async_copy(
+                    piece.at[pl.ds(0, rows), pl.ds(first, count)],
+                    scratch.at[pl.ds(place, rows), pl.ds(target, count)],
+                    sems.at[number, index],
+                )
+            )
+    return copies
+
+
+def load_shards(pairs_of, scratch, sems):
+    copies = []
+    rows = scratch.shape[0] // 8
+    for number, (source, owner, first, count, target) in enumerate(pairs_of):
+        for index in range(8):
+            copies.append(
+                pltpu.make_async_copy(
+                    source.at[2 * index + owner, :, pl.ds(first, count)],
+                    scratch.at[pl.ds(index * rows, rows), pl.ds(target, count)],
+                    sems.at[number, index],
+                )
+            )
+    return copies
+
+
+def run_all(copies):
+    for copy in copies:
+        copy.start()
+    for copy in copies:
+        copy.wait()
+
+
+def qkv_kernel(info_ref, mine_ref, got_ref, far_ref, gain_ref, bias_ref, hg_ref, mean_ref, *refs):
+    pieces, refs = refs[:8], refs[8:]
+    p_ref, rate_ref, ht_ref, w_ref, sems = refs
+    sub = pl.program_id(1)
+
+    @pl.when((pl.program_id(0) == 0) & (sub == 0))
+    def _():
+        run_all(load_pieces(info_ref, [(pieces, 0, w_ref.shape[1], 0)], w_ref, sems))
+
+    x = jnp.where(
+        sub // 2 == info_ref[0],
+        mine_ref[0],
+        jnp.where(sub % 2 == info_ref[1], got_ref[0], far_ref[0]),
+    ).astype(wide)
+    centered = x - jnp.mean(x, axis=1, keepdims=True)
+    variance = jnp.mean(centered * centered, axis=1, keepdims=True)
+    h_wide = centered * lax.rsqrt(variance + norm_eps) * gain_ref[...] + bias_ref[...]
+    h = h_wide.astype(low)
+    ht_ref[...] = jnp.transpose(h_wide).astype(low)
+    means = mean_ref[...]
+    projected = dot(h, w_ref[...])
+    for at in range(0, projected.shape[1], 128):
+        raw = projected[:, at : at + 128]
+        if at % 384 == 256:
+            p_ref[0, :, at : at + 128] = raw.astype(low)
+            continue
+        inner = raw - split_dot(raw, means)
+        rate = lax.rsqrt(dot((inner * inner).astype(low), means) + norm_eps)
+        to = at // 384 * 256 + at % 384
+        rate_ref[0, :, to : to + 128] = rate
+        p_ref[0, :, at : at + 128] = (inner * rate * hg_ref[:, to : to + 128]).astype(low)
+
+
+def attn_fwd_kernel(
+    info_ref, start_ref, kind_ref, p_ref, aug_ref, side_ref, mine_ref, send_ref, inv_ref
+):
+    seq = pl.program_id(0)
+    blocks = p_ref.shape[1] // query_block
+    lane = lax.broadcasted_iota(jnp.int32, (query_block, 128), 1)
+
+    def step(block, carry):
+        row = pl.multiple_of(block * query_block, query_block)
+        which = seq * blocks + block
+
+        def body(size):
+            begin = pl.multiple_of(start_ref[which], 16)
+            q_pair = p_ref[0, pl.ds(row, query_block), 0:128]
+            q_side = aug_ref[0, pl.ds(row, query_block), :] * side_ref[...]
+            keys = jnp.concatenate(
+                [p_ref[0, pl.ds(begin, size), 128:256], aug_ref[0, pl.ds(begin, size), :]], axis=1
+            )
+            values = jnp.concatenate(
+                [p_ref[0, pl.ds(begin, size), 256:384], jnp.ones((size, 128), low)], axis=1
+            )
+            mixed = []
+            for head in range(2):
+                mine = jnp.where(lane // 64 == head, q_pair, jnp.zeros_like(q_pair))
+                scores = dot(jnp.concatenate([mine, q_side], axis=1), keys, 1, 1)
+                mixed.append(dot(jnp.exp2(scores).astype(low), values))
+            inverse = 1.0 / jnp.where(lane < 64, mixed[0][:, 128:], mixed[1][:, 128:])
+            outcome = jnp.where(lane < 64, mixed[0][:, :128], mixed[1][:, :128]) * inverse
+
+            @pl.when(block % 2 == info_ref[1])
+            def _():
+                mine_ref[0, block // 2] = outcome.astype(low)
+
+            @pl.when(block % 2 != info_ref[1])
+            def _():
+                send_ref[0, block // 2] = outcome.astype(low)
+
+            inv_ref[0, pl.ds(row, query_block), :] = inverse
+
+        for index, size in enumerate(windows):
+            pl.when(kind_ref[which] == index)(partial(body, size))
+        return carry
+
+    lax.fori_loop(0, blocks, step, 0)
+
+
+def attn_bwd_kernel(
+    base,
+    info_ref,
+    start_ref,
+    kind_ref,
+    p_ref,
+    go_mine_ref,
+    go_got_ref,
+    o_mine_ref,
+    o_send_ref,
+    inv_ref,
+    rate_ref,
+    aug_ref,
+    side_ref,
+    hg_ref,
+    mean_ref,
+    g_ref,
+    gain_ref,
+    gq_acc,
+    gk_acc,
+    gv_acc,
+):
+    seq = pl.program_id(0) + base
+    blocks = p_ref.shape[1] // query_block
+    lane = lax.broadcasted_iota(jnp.int32, (query_block, 128), 1)
+    gk_acc[...] = jnp.zeros_like(gk_acc)
+    gv_acc[...] = jnp.zeros_like(gv_acc)
+
+    def step(block, carry):
+        row = pl.multiple_of(block * query_block, query_block)
+        which = seq * blocks + block
+
+        def body(size):
+            begin = pl.multiple_of(start_ref[which], 16)
+            rows = pl.ds(row, query_block)
+            span = pl.ds(begin, size)
+            q_pair = p_ref[0, rows, 0:128]
+            q_side = aug_ref[0, rows, :] * side_ref[...]
+            k_pair = p_ref[0, span, 128:256]
+            k_side = aug_ref[0, span, :]
+            keys = jnp.concatenate([k_pair, k_side], axis=1)
+            values = jnp.concatenate([p_ref[0, span, 256:384], k_side], axis=1)
+            near = block % 2 == info_ref[1]
+            go = jnp.where(near, go_mine_ref[0, block // 2], go_got_ref[0, block // 2])
+            o = jnp.where(near, o_mine_ref[0, block // 2], o_send_ref[0, block // 2])
+            scaled = go.astype(wide) * inv_ref[0, rows, :]
+            scaled_low = scaled.astype(low)
+            product = scaled_low.astype(wide) * o.astype(wide)
+            powers, grads, queries, pulls = [], [], [], []
+            for head in range(2):
+                mine = lane // 64 == head
+                inner = jnp.sum(jnp.where(mine, product, 0.0), axis=1, keepdims=True)
+                one = inner.astype(low)
+                two = (inner - one.astype(wide)).astype(low)
+                three = (inner - one.astype(wide) - two.astype(wide)).astype(low)
+                go_side = jnp.where(
+                    lane == 6,
+                    -one,
+                    jnp.where(lane == 7, -two, jnp.where(lane == 8, -three, jnp.zeros_like(q_pair))),
+                )
+                q_mine = jnp.where(mine, q_pair, jnp.zeros_like(q_pair))
+                go_mine = jnp.where(mine, scaled_low, jnp.zeros_like(q_pair))
+                power = jnp.exp2(dot(keys, jnp.concatenate([q_mine, q_side], axis=1), 1, 1))
+                slope = dot(values, jnp.concatenate([go_mine, go_side], axis=1), 1, 1)
+                grad = (power * slope).astype(low)
+                powers.append(power.astype(low))
+                grads.append(grad)
+                queries.append(q_mine)
+                pulls.append(go_mine)
+            gv_acc[span, :] += dot(
+                jnp.concatenate(powers, axis=1), jnp.concatenate(pulls, axis=0)
+            )
+            gk_acc[span, :] += dot(
+                jnp.concatenate(grads, axis=1), jnp.concatenate(queries, axis=0)
+            )
+            gq_acc[rows, :] = jnp.where(
+                lane < 64, dot(grads[0], k_pair, 0, 0), dot(grads[1], k_pair, 0, 0)
+            )
+
+        for index, size in enumerate(windows):
+            pl.when(kind_ref[which] == index)(partial(body, size))
+        return carry
+
+    lax.fori_loop(0, blocks, step, 0)
+    g_ref[0, :, 256:384] = gv_acc[...].astype(low)
+    means = mean_ref[...]
+
+    @pl.when(pl.program_id(0) == 0)
+    def _():
+        gain_ref[...] = jnp.zeros_like(gain_ref)
+
+    for index, acc, scale, unscale in (
+        (0, gq_acc, 0.125, 8.0 / log2e),
+        (1, gk_acc, 1.0 / log2e, 1.0),
+    ):
+        at = slice(128 * index, 128 * index + 128)
+        gain = hg_ref[:, at]
+        grad = acc[...] * scale
+        normed = p_ref[0, :, at].astype(wide) * unscale
+        weighted = grad * gain
+        cross = grad * normed
+        first = split_dot(weighted, means)
+        second = split_dot(cross, means)
+        g_ref[0, :, at] = (
+            rate_ref[0, :, at] * (weighted - first - normed / gain * second)
+        ).astype(low)
+        gain_ref[index : index + 1, :] += jnp.sum(cross, axis=0, keepdims=True) / gain
+
+
+def attn_out_kernel(info_ref, o_mine_ref, o_got_ref, mine_ref, got_ref, gy_ref, gain_ref, bias_ref, shards, *refs):
+    x2_ref, h_ref, ht_ref, gyt_ref, w_ref, sems = refs
+    cols = o_mine_ref.shape[3]
+    c = info_ref[1]
+
+    @pl.when((pl.program_id(0) == 0) & (pl.program_id(1) == 0))
+    def _():
+        run_all(
+            load_shards([(shards, c, 0, cols, 0), (shards, 1 - c, 0, cols, cols)], w_ref, sems)
+        )
+
+    x = jnp.where(pl.program_id(1) == info_ref[0], mine_ref[0], got_ref[0]).astype(wide)
+    x2 = x + dot(jnp.concatenate([o_mine_ref[0, 0], o_got_ref[0, 0]], axis=1), w_ref[...], 1, 1)
+    x2_ref[...] = x2
+    centered = x2 - jnp.mean(x2, axis=1, keepdims=True)
+    variance = jnp.mean(centered * centered, axis=1, keepdims=True)
+    h = centered * lax.rsqrt(variance + norm_eps) * gain_ref[...] + bias_ref[...]
+    h_ref[...] = h.astype(low)
+    ht_ref[...] = jnp.transpose(h).astype(low)
+    gyt_ref[...] = jnp.transpose(gy_ref[...].astype(wide)).astype(low)
+
+
+def spread(info_ref, acc, scale, mine_ref, other_ref, from_col, to_col, count):
+    rows = mine_ref.shape[2]
+    for side, ref in enumerate((mine_ref, other_ref)):
+        if ref is None:
+            continue
+        for index in range(8):
+            place = pl.multiple_of(info_ref[2 + index] * rows, rows)
+            ref[index % 2, index // 2, :, to_col : to_col + count] = (
+                acc[pl.ds(place, rows), from_col + side * count : from_col + (side + 1) * count]
+                * scale
+            ).astype(low)
+
+
+def blocks(grad_ref, acc, scale, owners, to_col, count):
+    rows = grad_ref.shape[1]
+    for number, owner in enumerate(owners):
+        for index in range(8):
+            grad_ref[2 * index + owner, :, to_col : to_col + count] = (
+                acc[index * rows : (index + 1) * rows, number * count : (number + 1) * count]
+                * scale
+            ).astype(low)
+
+
+def mlp_kernel(first, begin, scale, info_ref, h_ref, ht_ref, gy_ref, gyt_ref, out_in_ref, *refs):
+    if not first:
+        gh_in_ref, *refs = refs
+    shards, *refs = refs if first else [refs[0], *refs[2:]]
+    out_ref, gh_ref, grad_ref, up_ref, down_ref, up_acc, down_acc, sems = refs
+    step = pl.program_id(0)
+    chunk = up_ref.shape[1] // 2
+
+    @pl.when(step == 0)
+    def _():
+        run_all(
+            load_shards([(shards, m, begin, chunk, m * chunk) for m in range(2)], up_ref, sems)
+            + load_shards(
+                [(shards, m, begin + chunk, chunk, m * chunk) for m in range(2)],
+                down_ref,
+                sems.at[pl.ds(2, 2)],
+            )
+        )
+
+    root = math.sqrt(2.0 / math.pi)
+    t = dot(h_ref[...], up_ref[...])
+    square = t * t
+    gate = 0.5 + 0.5 * jnp.tanh(t * (root + (root * 0.044715) * square))
+    act = t * gate
+    slope = gate + 2.0 * act * (1.0 - gate) * (root + (3.0 * root * 0.044715) * square)
+    act = act.astype(low)
+    grad = (dot(gy_ref[...], down_ref[...]) * slope).astype(low)
+    out_ref[...] = out_in_ref[...] + dot(act, down_ref[...], 1, 1)
+    back = dot(grad, up_ref[...], 1, 1)
+    gh_ref[...] = back if first else gh_in_ref[...] + back
+
+    @pl.when(step == 0)
+    def _():
+        up_acc[...] = dot(ht_ref[...], grad)
+        down_acc[...] = dot(gyt_ref[...], act)
+
+    @pl.when(step > 0)
+    def _():
+        up_acc[...] += dot(ht_ref[...], grad)
+        down_acc[...] += dot(gyt_ref[...], act)
+
+    @pl.when(step == pl.num_programs(0) - 1)
+    def _():
+        blocks(grad_ref, up_acc, scale, (0, 1), 0, chunk)
+        blocks(grad_ref, down_acc, scale, (0, 1), chunk, chunk)
+
+
+def norm_back(values, grad, gain):
+    centered = values - jnp.mean(values, axis=1, keepdims=True)
+    rate = lax.rsqrt(jnp.mean(centered * centered, axis=1, keepdims=True) + norm_eps)
+    normed = centered * rate
+    weighted = grad * gain
+    result = rate * (
+        weighted
+        - jnp.mean(weighted, axis=1, keepdims=True)
+        - normed * jnp.mean(weighted * normed, axis=1, keepdims=True)
+    )
+    return result, normed
+
+
+def second_norm_kernel(
+    scale, info_ref, x2_ref, gh_ref, gy_ref, y_ref, valid_ref, o_mine_ref, o_got_ref, gain_ref, *refs
+):
+    shards, refs = refs[0], refs[2:]
+    keep_ref, send_ref, gx_ref, go_mine_ref, go_send_ref, grad_ref, sums_ref = refs[:7]
+    w_ref, acc, sems = refs[7:]
+    c = info_ref[1]
+    cols = o_mine_ref.shape[3]
+    half = pl.program_id(1)
+    start = (pl.program_id(0) == 0) & (half == 0)
+    end = (pl.program_id(0) == pl.num_programs(0) - 1) & (half == 1)
+
+    @pl.when(start)
+    def _():
+        run_all(
+            load_shards([(shards, c, 0, cols, 0), (shards, 1 - c, 0, cols, cols)], w_ref, sems)
+        )
+        sums_ref[...] = jnp.zeros_like(sums_ref)
+        acc[...] = jnp.zeros_like(acc)
+
+    out = (y_ref[...] * valid_ref[...][:, :1]).astype(low)
+
+    @pl.when(half == info_ref[0])
+    def _():
+        keep_ref[0] = out
+
+    @pl.when(half != info_ref[0])
+    def _():
+        send_ref[0] = out
+
+    gh = gh_ref[...]
+    back, normed = norm_back(x2_ref[...], gh, gain_ref[...])
+    gx = gy_ref[...].astype(wide) + back
+    gx_ref[...] = gx
+    go = dot(gx.astype(low), w_ref[...]).astype(low)
+    go_mine_ref[0, 0] = go[:, :cols]
+    go_send_ref[0, 0] = go[:, cols:]
+    turned = jnp.transpose(gx).astype(low)
+    sums_ref[0:1, :] += jnp.sum(gh * normed, axis=0, keepdims=True)
+    sums_ref[1:2, :] += jnp.sum(gh, axis=0, keepdims=True)
+    acc[...] += dot(turned, jnp.concatenate([o_mine_ref[0, 0], o_got_ref[0, 0]], axis=1))
+
+    @pl.when(end)
+    def _():
+        blocks(grad_ref, acc, scale, (c, 1 - c), 0, cols)
+
+
+def gw_in_kernel(scale, info_ref, ht_ref, *refs):
+    grads, (out_ref, acc) = refs[:-2], refs[-2:]
+    step = pl.program_id(0)
+
+    def add(grad_ref):
+        @pl.when(step == 0)
+        def _():
+            acc[...] = dot(ht_ref[...], grad_ref[0])
+
+        @pl.when(step > 0)
+        def _():
+            acc[...] += dot(ht_ref[...], grad_ref[0])
+
+    if len(grads) == 1:
+        add(grads[0])
+    else:
+        for index, grad_ref in enumerate(grads):
+            pl.when(step == index)(partial(add, grad_ref))
+
+    @pl.when(step == pl.num_programs(0) - 1)
+    def _():
+        spread(info_ref, acc, scale, out_ref, None, 0, 0, out_ref.shape[3])
+
+
+def gh1_kernel(info_ref, *refs):
+    grads, pieces = refs[:3], refs[3:11]
+    mine_ref, send_ref, w_ref, sems = refs[11:]
+
+    @pl.when(pl.program_id(0) == 0)
+    def _():
+        run_all(load_pieces(info_ref, [(pieces, 0, w_ref.shape[1], 0)], w_ref, sems))
+
+    both = dot(jnp.concatenate([ref[0] for ref in grads], axis=1), w_ref[...], 1, 1).astype(low)
+    part = mine_ref.shape[1]
+    near = info_ref[1] == 0
+    mine_ref[0] = jnp.where(near, both[:part], both[part:])
+    send_ref[0] = jnp.where(near, both[part:], both[:part])
+
+
+def first_norm_kernel(
+    info_ref, mine_ref, got_ref, a_ref, b_ref, gx2_ref, gain_ref, keep_ref, send_ref, sums_ref
+):
+    half = pl.program_id(0)
+    x = jnp.where(half == info_ref[0], mine_ref[0], got_ref[0]).astype(wide)
+    gh = a_ref[0].astype(wide) + b_ref[0].astype(wide)
+    back, normed = norm_back(x, gh, gain_ref[...])
+    out = (gx2_ref[...] + back).astype(low)
+
+    @pl.when(half == info_ref[0])
+    def _():
+        keep_ref[...] = out
+
+    @pl.when(half != info_ref[0])
+    def _():
+        send_ref[...] = out
+
+    @pl.when(half == 0)
+    def _():
+        sums_ref[...] = jnp.zeros_like(sums_ref)
+
+    sums_ref[0:1, :] += jnp.sum(gh * normed, axis=0, keepdims=True)
+    sums_ref[1:2, :] += jnp.sum(gh, axis=0, keepdims=True)
+
+
+def shape_of(dims, kind=low):
+    return jax.ShapeDtypeStruct(dims, kind)
+
+
+def window_table(segs, blocks):
+    length = segs.shape[1]
+    pad_begin = jnp.sum((segs >= 0).astype(jnp.int32), axis=1, keepdims=True)
+    begins = jnp.where(segs >= 0, segs, pad_begin)
+    size = length // blocks
+    firsts = begins[:, ::size]
+    lasts = begins[:, size - 1 :: size]
+    ends = jnp.sum((begins[:, None, :] <= lasts[:, :, None]).astype(jnp.int32), axis=2)
+    reach = ends - firsts
+    kinds = jnp.zeros_like(reach)
+    spans = jnp.full_like(reach, windows[0])
+    for index in range(1, len(windows)):
+        larger = reach > windows[index - 1]
+        kinds = jnp.where(larger, index, kinds)
+        spans = jnp.where(larger, windows[index], spans)
+    starts = jnp.minimum(firsts, length - spans)
+    return starts.reshape(-1), kinds.reshape(-1)
+
+
+def mask_columns(segs):
+    codes = (segs + 16) // 16
+    lane = jnp.arange(128, dtype=jnp.int32)
+    bits = (codes[:, :, None] >> jnp.minimum(lane, 5)) & 1
+    signs = (2 * bits - 1).astype(wide)
+    return jnp.where(lane < 6, signs, jnp.where(lane < 9, 1.0, 0.0)).astype(low)
+
+
+def swap(values, axis):
+    return lax.ppermute(values, axis, [(0, 1), (1, 0)])
+
+
+def in_order(index, mine, other, axis):
+    return jnp.where(
+        index == 0,
+        jnp.concatenate([mine, other], axis=axis),
+        jnp.concatenate([other, mine], axis=axis),
+    )
+
+
+def pick(values, index, axis):
+    return lax.dynamic_index_in_dim(values, index, axis, keepdims=False)
+
+
+def shift_far(values, step):
+    return lax.ppermute(
+        values,
+        "dp",
+        [(2 * ((z + step) % 4) + x, 2 * z + x) for z in range(4) for x in range(2)],
+    )
+
+
+def swap_x(values):
+    return lax.ppermute(values, "dp", [(d, d ^ 1) for d in range(8)])
+
+
+def gather_pieces(shard):
+    pieces = []
+    for step in range(4):
+        piece = shard if step == 0 else shift_far(shard, step)
+        pieces += [piece, swap_x(piece)]
+    return pieces
+
+
+class Reduce:
+    def __init__(self, mine, other=None):
+        self.mine = mine
+        self.other = other
+        self.got = None
+        self.state = None
+        self.phase = "core" if other is not None else "x"
+
+    def advance(self):
+        if self.phase == "core":
+            self.state = self.got = swap(self.other, "mlp")
+            self.phase = "x"
+        elif self.phase == "x":
+            far = self.mine[1]
+            if self.got is not None:
+                far = (far.astype(wide) + self.got[1].astype(wide)).astype(low)
+            self.state = swap_x(far)
+            self.phase = "z"
+        elif self.phase == "z":
+            total = self.mine[0].astype(wide) + self.state.astype(wide)
+            if self.got is not None:
+                total = total + self.got[0].astype(wide)
+            low_total = total.astype(low)
+            self.mine = total[0]
+            self.state = [shift_far(low_total[step], 4 - step) for step in range(1, 4)]
+            self.phase = "y"
+        elif self.phase == "y":
+            self.mine = self.mine + sum(part.astype(wide) for part in self.state)
+            self.state = swap(self.mine.astype(low), "seq")
+            self.phase = "end"
+        elif self.phase == "end":
+            self.mine = self.mine + self.state.astype(wide)
+            self.state = None
+            self.phase = "done"
+
+    def result(self):
+        while self.phase != "done":
+            self.advance()
+        return self.mine
+
+
+def on_device_small(
+    patches, segments, w_qkv, w_out, w_up, w_down, ln_gain, ln_bias, head_gain, cotangent
+):
+    half, seqs_all, width = patches.shape
+    length = 2 * half
+    seqs = seqs_all // 2
+    cols = w_qkv.shape[2]
+    part = half // 2
+    y = lax.axis_index("seq")
+    c = lax.axis_index("mlp")
+    d = lax.axis_index("dp")
+    dp_size = lax.axis_size("dp")
+    scale = 1.0 / math.sqrt(dp_size * seqs_all * length)
+    own_rows = seqs * half
+    hidden = w_up.shape[1]
+    shard_rows = width // dp_size
+    places = jnp.stack(
+        [2 * ((d // 2 + index // 2) % 4) + ((d % 2) ^ (index % 2)) for index in range(8)]
+    )
+    info = jnp.concatenate([jnp.stack([y, c]), places]).astype(jnp.int32)
+
+    turned = jnp.transpose(patches, (1, 0, 2)).reshape(2, seqs, 2, part, width)
+    got = swap(pick(pick(turned, 1 - y, 0), c, 1), "seq")
+    far = swap(got, "mlp")
+    turned = turned.reshape(seqs_all, half, width)
+    small = jnp.concatenate(
+        [
+            ln_gain.astype(low),
+            ln_bias.astype(low),
+            head_gain.astype(low).reshape(1, -1),
+            jnp.zeros((3, shard_rows), low),
+        ]
+    )
+    small = jnp.pad(small, ((0, 8), (0, 3 * cols - shard_rows)))
+    pairs = cols // 128
+    w_in = jnp.transpose(w_qkv.astype(low).reshape(3, shard_rows, pairs, 128), (1, 2, 0, 3))
+    w_in = w_in.reshape(shard_rows, 3 * cols)
+    in_pieces = gather_pieces(
+        jnp.concatenate(
+            [w_in, small]
+        )
+    )
+    small = [piece[shard_rows : shard_rows + 8, :shard_rows] for piece in in_pieces]
+    chunk = 512
+    chunks = hidden // chunk
+    up_low = w_up.astype(low)
+    down_low = jnp.transpose(w_down.astype(low))
+    parts = [jnp.transpose(w_out.astype(low))]
+    for f in range(chunks):
+        at = slice(f * chunk, (f + 1) * chunk)
+        parts += [up_low[:, at], down_low[:, at]]
+
+    def gather_shards(parts):
+        return lax.all_gather(jnp.concatenate(parts, axis=1), ("dp", "mlp"), axis=0)
+
+    split = 5
+    shards_a = gather_shards(parts[:split])
+    shards_b = gather_shards(parts[split:])
+
+    order = (places[None, :] == jnp.arange(8)[:, None]).astype(low)
+    small = jnp.einsum("nr,rkw->knw", order, jnp.stack(small), preferred_element_type=wide)
+    gains = small[0:2].reshape(2, width)
+    biases = small[2:4].reshape(2, width)
+    head_gains = jnp.transpose(small[4].reshape(dp_size, 2, cols // 64, 64 // dp_size), (1, 2, 0, 3))
+    head_gains = jnp.transpose(head_gains.reshape(2, pairs, 128), (1, 0, 2))
+    key_scale = jnp.array([[[log2e / 8.0], [1.0]]], wide)
+    head_scaled = (head_gains * key_scale).reshape(1, 2 * cols)
+    head_gains = head_gains.reshape(1, 2 * cols)
+
+    segs = lax.dynamic_slice_in_dim(jnp.transpose(segments), y * seqs, seqs, 0)
+    cot = cotangent.reshape(2, part, seqs_all, cols)
+    cot_other = swap(pick(cot, 1 - c, 0), "mlp")
+    cot = jnp.transpose(in_order(c, pick(cot, c, 0), cot_other, 2), (1, 0, 2))
+    cot = cot.reshape(2, seqs, part, width)
+    cot_got = swap(pick(cot, 1 - y, 0), "seq")
+    cot = in_order(y, pick(cot, y, 0)[:, None], cot_got[:, None], 1)
+    valid = pick((segs >= 0).reshape(seqs, 2, 2, part), c, 2)
+    gy = jnp.where(valid[..., None], cot, jnp.zeros_like(cot)).reshape(own_rows, width)
+    valid = jnp.broadcast_to(valid.reshape(own_rows, 1).astype(wide), (own_rows, 128))
+
+    starts, kinds = window_table(segs, length // query_block)
+    aug = mask_columns(segs)
+    lanes = jnp.arange(128)
+    side = jnp.where(lanes < 6, mask_weight, jnp.where(lanes == 6, -6.0 * mask_weight, 0.0))
+    side = side.astype(low)[None]
+    means = jnp.where(lanes[:, None] // 64 == lanes[None] // 64, 1.0 / 64, 0.0).astype(low)
+    anywhere = pl.BlockSpec(memory_space=pl.ANY)
+
+    def whole(dims):
+        return pl.BlockSpec(dims, lambda *ids: (0,) * len(dims))
+
+    def call(kernel, grid, in_specs, out_specs, out_shape, scratch, name, scalars, pins=(), share=1, alias=None):
+        work = micros[name] * 1150000000 // share
+        ends = scalars + len(in_specs)
+
+        def unpinned(*refs):
+            kernel(*refs[:ends], *refs[ends + len(pins) :])
+
+        run = pl.pallas_call(
+            unpinned,
+            grid_spec=pltpu.PrefetchScalarGridSpec(
+                num_scalar_prefetch=scalars,
+                grid=grid,
+                in_specs=in_specs + [anywhere] * len(pins),
+                out_specs=out_specs,
+                scratch_shapes=scratch,
+            ),
+            out_shape=out_shape,
+            compiler_params=params(len(grid)),
+            input_output_aliases=alias or {},
+            cost_estimate=pl.CostEstimate(flops=work, bytes_accessed=1000000, transcendentals=0),
+            name=name,
+        )
+        return lambda *operands: run(*operands, *pins)
+
+    piece_sems = pltpu.SemaphoreType.DMA((4, 8))
+    one_seq = pl.BlockSpec((1, part, width), lambda s, j, *_: (s, 0, 0))
+    projected, rates, h1t = call(
+        qkv_kernel,
+        (seqs, 4),
+        [
+            pl.BlockSpec((1, part, width), lambda s, j, info: (seqs * info[0] + s, j % 2, 0)),
+            one_seq,
+            one_seq,
+            whole((1, width)),
+            whole((1, width)),
+            whole((1, 2 * cols)),
+            whole((128, 128)),
+        ]
+        + [anywhere] * 8,
+        [
+            pl.BlockSpec((1, part, 3 * cols), lambda s, j, *_: (s, j, 0)),
+            pl.BlockSpec((1, part, 2 * cols), lambda s, j, *_: (s, j, 0)),
+            pl.BlockSpec((width, part), lambda s, j, *_: (0, 4 * s + j)),
+        ],
+        [
+            shape_of((seqs, length, 3 * cols)),
+            shape_of((seqs, length, 2 * cols), wide),
+            shape_of((width, seqs * length)),
+        ],
+        [pltpu.VMEM((width, 3 * cols), low), piece_sems],
+        "qkv",
+        1,
+    )(info, turned, got, far, gains[:1], biases[:1], head_scaled, means, *in_pieces)
+    split_seq = pl.BlockSpec((1, 2, part, 128), lambda s, p, *_: (s, 0, 0, p))
+    o_mine, o_send, inverse = call(
+        attn_fwd_kernel,
+        (seqs, pairs),
+        [
+            pl.BlockSpec((1, length, 384), lambda s, p, *_: (s, 0, p)),
+            pl.BlockSpec((1, length, 128), lambda s, p, *_: (s, 0, 0)),
+            whole((1, 128)),
+        ],
+        [split_seq, split_seq, pl.BlockSpec((1, length, 128), lambda s, p, *_: (s, 0, p))],
+        [shape_of((seqs, 2, part, cols))] * 2 + [shape_of((seqs, length, cols), wide)],
+        [],
+        "attn_fwd",
+        3,
+    )(info, starts, kinds, projected, aug, side)
+
+    o_got = swap(o_send, "mlp")
+    mine_spec = pl.BlockSpec((1, part, width), lambda s, h, info: (seqs * info[0] + s, info[1], 0))
+    got_spec = pl.BlockSpec((1, part, width), lambda s, h, *_: (s, 0, 0))
+    rows_spec = pl.BlockSpec((part, width), lambda s, h, *_: (2 * s + h, 0))
+    turned_spec = pl.BlockSpec((width, part), lambda s, h, *_: (0, 2 * s + h))
+    part_spec = pl.BlockSpec((1, 1, part, cols), lambda s, h, *_: (s, h, 0, 0))
+    x2, h2, h2t, gyt = call(
+        attn_out_kernel,
+        (seqs, 2),
+        [part_spec, part_spec, mine_spec, got_spec, rows_spec, whole((1, width)), whole((1, width))]
+        + [anywhere],
+        [rows_spec, rows_spec, turned_spec, turned_spec],
+        [
+            shape_of((own_rows, width), wide),
+            shape_of((own_rows, width)),
+            shape_of((width, own_rows)),
+            shape_of((width, own_rows)),
+        ],
+        [pltpu.VMEM((width, width), low), piece_sems],
+        "attn_out",
+        1,
+    )(info, o_mine, o_got, turned, got, gy, gains[1:], biases[1:], shards_a)
+
+    block = half
+    block_spec = pl.BlockSpec((block, width), lambda i, *_: (i, 0))
+    block_turned = pl.BlockSpec((width, block), lambda i, *_: (0, i))
+    total, gh = x2, None
+    sums = []
+
+    def advance():
+        pins = []
+        for one in sums:
+            pins += jax.tree.leaves(one.state)
+            one.advance()
+        return pins
+
+    grads = None
+    grad_shape = shape_of((16, shard_rows, cols + 2 * hidden))
+    for f in range(chunks):
+        first = f == 0
+        carried = [total] if first else [total, gh]
+        begin = cols + f * 2 * chunk
+        source = shards_a
+        if begin >= shards_a.shape[2]:
+            source, begin = shards_b, begin - shards_a.shape[2]
+        extra = [] if first else [grads]
+        total, gh, grads = call(
+            partial(mlp_kernel, first, begin, scale),
+            (seqs,),
+            [block_spec, block_turned, block_spec, block_turned]
+            + [block_spec] * len(carried)
+            + [anywhere] * (1 + len(extra)),
+            [block_spec] * 2
+            + [pl.BlockSpec((16, shard_rows, 2 * chunk), lambda *_, f=f: (0, 0, f))],
+            [shape_of((own_rows, width), wide)] * 2 + [grad_shape],
+            [pltpu.VMEM((width, 2 * chunk), low)] * 2
+            + [pltpu.VMEM((width, 2 * chunk), wide)] * 2
+            + [piece_sems],
+            "mlp",
+            1,
+            alias={} if first else {8: 2},
+        )(info, h2, h2t, gy, gyt, *carried, source, *extra)
+
+    last_block = 2 * hidden // cols
+    out_keep, out_send, gx2, go_mine, go_send, grads, second_sums = call(
+        partial(second_norm_kernel, scale),
+        (seqs, 2),
+        [
+            rows_spec,
+            rows_spec,
+            rows_spec,
+            rows_spec,
+            pl.BlockSpec((part, 128), lambda s, h, *_: (2 * s + h, 0)),
+            part_spec,
+            part_spec,
+            whole((1, width)),
+        ]
+        + [anywhere] * 2,
+        [got_spec, got_spec, rows_spec, part_spec, part_spec]
+        + [pl.BlockSpec((16, shard_rows, cols), lambda *_: (0, 0, last_block))]
+        + [whole((8, width))],
+        [shape_of((seqs, part, width))] * 2
+        + [shape_of((own_rows, width), wide)]
+        + [shape_of((seqs, 2, part, cols))] * 2
+        + [grad_shape]
+        + [shape_of((8, width), wide)],
+        [pltpu.VMEM((width, width), low), pltpu.VMEM((width, width), wide), piece_sems],
+        "second_norm",
+        1,
+        alias={10: 5},
+    )(info, x2, gh, gy, total, valid, o_mine, o_got, gains[1:], shards_a, grads)
+    go_got = swap(go_send, "mlp")
+    out_swapped = swap(out_send, "seq")
+    scattered = lax.psum_scatter(grads, ("dp", "mlp"), scatter_dimension=0, tiled=True)[0]
+
+    def attention_back(pair, base, count, pins):
+        split_pair = pl.BlockSpec((1, 2, part, 128), lambda s, *_: (s + base, 0, 0, pair))
+        columns = pl.BlockSpec((1, length, 128), lambda s, *_: (s + base, 0, pair))
+        return call(
+            partial(attn_bwd_kernel, base),
+            (count,),
+            [pl.BlockSpec((1, length, 384), lambda s, *_: (s + base, 0, pair))]
+            + [split_pair] * 4
+            + [
+                columns,
+                pl.BlockSpec((1, length, 256), lambda s, *_: (s + base, 0, pair)),
+                pl.BlockSpec((1, length, 128), lambda s, *_: (s + base, 0, 0)),
+                whole((1, 128)),
+                pl.BlockSpec((1, 256), lambda s, *_: (0, pair)),
+                whole((128, 128)),
+            ],
+            [pl.BlockSpec((1, length, 384), lambda s, *_: (s, 0, 0)), whole((8, 128))],
+            [shape_of((count, length, 384)), shape_of((8, 128), wide)],
+            [pltpu.VMEM((length, 128), wide)] * 3,
+            "attn_bwd",
+            3,
+            pins,
+            3 * seqs // count,
+        )(
+            info, starts, kinds, projected, go_mine, go_got, o_mine, o_send, inverse, rates,
+            aug, side, head_gains, means,
+        )
+
+    def input_weights(grads):
+        if len(grads) == 1:
+            specs = [pl.BlockSpec((1, length, 384), lambda s, *_: (s, 0, 0))]
+        else:
+            specs = [whole((1, length, 384))] * len(grads)
+        shares = (2, 4, shard_rows, 384)
+        return call(
+            partial(gw_in_kernel, scale),
+            (seqs,),
+            [pl.BlockSpec((width, length), lambda s, *_: (0, s))] + specs,
+            whole(shares),
+            shape_of(shares),
+            [pltpu.VMEM((width, 384), wide)],
+            "gw_in",
+            1,
+            (),
+            3,
+        )(info, h1t, *grads)
+
+    def first_grads(seq, grads, pins):
+        return call(
+            gh1_kernel,
+            (2,),
+            [
+                pl.BlockSpec((1, half, 384), lambda h, *_, at=seq % grad.shape[0]: (at, h, 0))
+                for grad in grads
+            ]
+            + [anywhere] * 8,
+            [pl.BlockSpec((1, part, width), lambda h, *_: (h, 0, 0))] * 2,
+            [shape_of((2, part, width))] * 2,
+            [pltpu.VMEM((width, 3 * cols), low), piece_sems],
+            "gh1",
+            1,
+            pins,
+            3,
+        )(info, *grads, *in_pieces)
+
+    def first_back(seq, mine, got_part, pins):
+        halves = pl.BlockSpec((1, part, width), lambda h, *_: (h, 0, 0))
+        return call(
+            first_norm_kernel,
+            (2,),
+            [
+                pl.BlockSpec((1, part, width), lambda h, info: (seqs * info[0] + seq, info[1], 0)),
+                pl.BlockSpec((1, part, width), lambda h, *_: (seq, 0, 0)),
+                halves,
+                halves,
+                pl.BlockSpec((part, width), lambda h, *_: (2 * seq + h, 0)),
+                whole((1, width)),
+            ],
+            [whole((part, width))] * 2 + [whole((8, width))],
+            [shape_of((part, width))] * 2 + [shape_of((8, width), wide)],
+            [],
+            "first_norm",
+            1,
+            pins,
+            3,
+        )(info, turned, got, mine, got_part, gx2, gains[:1])
+
+    def finish_out():
+        out_six = in_order(y, out_keep, out_swapped, 0).reshape(seqs_all, part, 2, cols)
+        out_got = swap(pick(out_six, 1 - c, 2), "mlp")
+        return jnp.transpose(in_order(c, pick(out_six, c, 2), out_got, 1), (1, 0, 2))
+
+    full_grads, gain_sums, in_sums = [], [], []
+    out = None
+    for pair in range(pairs):
+        pins = advance()
+        if pair == 1:
+            pins.append(out_swapped)
+            out = finish_out()
+        if pair == 2:
+            pins.append(out)
+        grads, gain_sum = attention_back(pair, 0, seqs, pins)
+        full_grads.append(grads)
+        gain_sums.append(gain_sum)
+        if pair < pairs - 1:
+            in_sums.append(Reduce(input_weights([grads])))
+            sums.append(in_sums[-1])
+    halves_sent, backs = [], []
+    for seq in range(seqs):
+        mine, send = first_grads(seq, full_grads, ())
+        halves_sent.append((mine, swap(send, "mlp")))
+        if seq:
+            backs.append(first_back(seq - 1, *halves_sent[seq - 1], ()))
+    in_sums.append(Reduce(input_weights([grads])))
+    sums.append(in_sums[-1])
+    advance()
+    backs.append(first_back(seqs - 1, *halves_sent[seqs - 1], ()))
+    first_sums = sum(back[2] for back in backs)
+
+    mine_parts, other_parts = [], []
+    for keep, send, _ in backs:
+        got_rows = swap(send, "seq")
+        mine_parts.append(in_order(c, keep, swap(keep, "mlp"), 0))
+        other_parts.append(in_order(c, got_rows, swap(got_rows, "mlp"), 0))
+    grad_patches = in_order(y, jnp.stack(mine_parts), jnp.stack(other_parts), 0)
+    grad_patches = jnp.transpose(grad_patches, (1, 0, 2))
+
+    scattered = scattered.astype(wide) + swap(scattered, "seq").astype(wide)
+    gw_up = jnp.concatenate(
+        [scattered[:, 2 * f * chunk : (2 * f + 1) * chunk] for f in range(chunks)], axis=1
+    )
+    gw_down = jnp.concatenate(
+        [scattered[:, (2 * f + 1) * chunk : (2 * f + 2) * chunk] for f in range(chunks)], axis=1
+    )
+    gw_out = scattered[:, 2 * hidden :]
+    gw_in = jnp.stack([one.result() for one in in_sums], axis=1)
+    gw_in = gw_in.reshape(shard_rows, pairs, 3, 128)
+    gw_in = jnp.transpose(gw_in, (2, 0, 1, 3)).reshape(3, shard_rows, cols)
+    norms = jnp.concatenate([first_sums[:2], second_sums[:2]]) * scale
+    norms = norms + swap(norms, "mlp")
+    heads = jnp.stack([part[:2] for part in gain_sums], axis=1).reshape(2, cols) * scale
+    small = jnp.concatenate([norms, heads.reshape(1, width)])
+    small = small + swap(small, "seq")
+    for bit in (1, 2, 4):
+        small = small + lax.ppermute(small, "dp", [(i, i ^ bit) for i in range(8)])
+    norms = lax.dynamic_slice_in_dim(small[:4], d * shard_rows, shard_rows, 1)
+    heads = small[4].reshape(2, cols // 64, 64)
+    heads = lax.dynamic_slice_in_dim(heads, d * (64 // dp_size), 64 // dp_size, 2)
+    return (
+        out,
+        grad_patches,
+        gw_in,
+        jnp.transpose(gw_out),
+        gw_up,
+        jnp.transpose(gw_down),
+        norms[0::2],
+        norms[1::2],
+        heads,
+    )
+
+
 def solution(mesh):
+    shape = dict(mesh.shape)
+    small = shape["seq"] == 2 and shape["mlp"] == 2 and shape["dp"] == 8
     return jax.shard_map(
-        on_device,
+        on_device_small if small else on_device,
         mesh=mesh,
         in_specs=(
             P("seq", "dp", None),

time: 1780 us -> 529 us (0.30)
  waiting for transfers between devices: 906 us -> 72.1 us
  matrix products: 313 us -> 0.13 us
  Pallas kernels: 0 us -> 275 us
  other arithmetic: 223 us -> 51.9 us
  local copies, waits for them, and re-layouts: 182 us -> 45.4 us
  blocking collectives: 127 us -> 0 us
  starting transfers between devices: 1.53 us -> 62 us
    all_gather x17 -> x2, waiting for transfers between devices: 420 us -> 0.02 us  [gather_shards(): return lax.all_gather(jnp.concatenate(parts, axis=1), ('dp', 'mlp'), axis=0)]
    reduce_scatter x9 -> x1, waiting for transfers between devices: 330 us -> 0.01 us  [on_device_small(): lax.psum_scatter(grads, ('dp', 'mlp'), scatter_dimension=0, tiled=True)[0]]
    dot_general x54 -> x1, matrix products: 313 us -> 0.13 us  [on_device_small(): jnp.einsum('nr,rkw->knw', order, jnp.stack(small), preferred_element_type...]
    pallas_call x0 -> x19, Pallas kernels: none -> 275 us  [call(): return lambda *operands: run(*operands, *pins)]
    unnamed x21 -> x3, waiting for transfers between devices: 126 us -> 0.05 us
    all_gather x4 -> x0, blocking collectives: 102 us -> none  [the longest x1 33.5 us: on_device(): lax.all_gather(w_out.astype(jnp.bfloat16), 'dp', axis=1, tiled=True)]
    reduce_sum x24 -> x2, other arithmetic: 91 us -> 0.35 us  [the longest x1 0.22 us: window_table(): jnp.sum((begins[:, None, :] <= lasts[:, :, None]).astype(jnp.int32), axis=2)]
    convert_element_type x29 -> x12, other arithmetic: 89.1 us -> 5.81 us  [the longest x1 2.03 us: mask_columns(): return jnp.where(lane < 6, signs, jnp.where(lane < 9, 1.0, 0.0)).astype(low)]
  transfers between devices with their start and end apart: 34 -> 51, of which waited for: 30 -> 13; matrix products, arithmetic and copies ran while one was open for 14% -> 17% of each run, Pallas kernels for 0% -> 44%
where the time goes in v2:
time: 529 us; the launch traced here: 521 us
  Pallas kernels  275 us (52%)
  waiting for transfers between devices  72.1 us (14%)
  starting transfers between devices  62 us (12%)
  other arithmetic  51.9 us (10%)
  local copies, waits for them, and re-layouts  45.4 us (9%)
  between operations  15.1 us (3%)
    pallas_call x19, Pallas kernels, call(): return lambda *operands: run(*operands, *pins)  275 us
    ppermute x12, waiting for transfers between devices, shift_far(): lax.ppermute(values, 'dp', [(2 * ((z + step) % 4) + x, 2 * z + x) for z i...  30.9 us
    ppermute x7, starting transfers between devices, swap_x(): return lax.ppermute(values, 'dp', [(d, d ^ 1) for d in range(8)])  25.2 us
    ppermute x7, waiting for transfers between devices, swap_x(): return lax.ppermute(values, 'dp', [(d, d ^ 1) for d in range(8)])  23.7 us
    ppermute x26, waiting for transfers between devices, swap(): return lax.ppermute(values, axis, [(0, 1), (1, 0)])  16.4 us
    ppermute x26, starting transfers between devices, swap(): return lax.ppermute(values, axis, [(0, 1), (1, 0)])  16.3 us
    ppermute x12, starting transfers between devices, shift_far(): lax.ppermute(values, 'dp', [(2 * ((z + step) % 4) + x, 2 * z + x) for z i...  16.2 us
    unnamed x9, other arithmetic  12.9 us
  transfers between devices with their start and end apart: 51, of which 13 were waited for; matrix products, arithmetic and copies ran while one was open for 17% of the time, Pallas kernels for 44%

profile of v2, /device:TPU:0, one launch (start us, length us, event | category | flops | bytes accessed | tf_op | source)
XLA Modules:
  0.0 521.4 jit_solution(4261289741604727324)
XLA Ops:
  36.0 20.9 %collective-permute-done.5.refs_12_.refs_8_ = bf16[112,1152]{1,0:T(8,128)(2,1)} collective-permute-done((bf16[112,1152]{1,0:T(8,128)(2,1)}, bf16[112,1152]{1,0:T(8,128)(2,1)}, u32[]{:S(2)}, u32[]{:S(2)}) %collective-permute-start.5) | collective-permute-done | bytes 258080 | tf_op jit(solution)/shard_map/ppermute | solution.py:821
  75.4 29.3 %qkv.1 = (bf16[3,1024,1152]{2,1,0:T(8,128)(2,1)}, f32[3,1024,768]{2,1,0:T(8,128)}, bf16[768,3072]{1,0:T(8,128)(2,1)}) custom-call(s32[10]{0:T(128)} %concatenate.211.refs_0_, bf16[6,512,768]{2,1,0:T(8,128)(2,1)} %bitcast.217, bf16[3,256,768]{2,1,0:T(8,128)(2,1)} %collective-permute-done.refs_2_.refs_4_, bf16[3,256,768]{2,1,0:T(8,128)(2,1)} %collective-permute-done.1.refs_3_, ...), custom_call_target="tpu_custom_call" | custom-call | flops 26449999872 | bytes 1000000 | tf_op jit(solution)/shard_map/qkv/pallas_call | solution.py:994
  104.7 25.4 %attn_fwd.1 = (bf16[3,2,256,384]{3,2,1,0:T(8,128)(2,1)}, bf16[3,2,256,384]{3,2,1,0:T(8,128)(2,1)}, f32[3,1024,384]{2,1,0:T(8,128)}) custom-call(s32[10]{0:T(128)} %concatenate.211.refs_0_, s32[12]{0:T(128)} %reshape.552.refs_1_, s32[12]{0:T(128)} %reshape.553.refs_2_, bf16[3,1024,1152]{2,1,0:T(8,128)(2,1)} %get-tuple-element.56.refs_3_, ...), custom_call_target="tpu_custom_call" | custom-call | flops 33350000640 | bytes 1000000 | tf_op jit(solution)/shard_map/attn_fwd/pallas_call | solution.py:994
  135.3 13.7 %attn_out.1 = (f32[1536,768]{1,0:T(8,128)}, bf16[1536,768]{1,0:T(8,128)(2,1)}, bf16[768,1536]{1,0:T(8,128)(2,1)}, bf16[768,1536]{1,0:T(8,128)(2,1)}) custom-call(s32[10]{0:T(128)} %concatenate.211.refs_0_, bf16[3,2,256,384]{3,2,1,0:T(8,128)(2,1)} %get-tuple-element.57.refs_1_.refs_6_, bf16[3,2,256,384]{3,2,1,0:T(8,128)(2,1)} %collective-permute-done.9.refs_2_.refs_7_, ...), custom_call_target="tpu_custom_call" | custom-call | flops 14949999616 | bytes 1000000 | tf_op jit(solution)/shard_map/attn_out/pallas_call | solution.py:994
  149.0 25.5 %mlp.3 = (f32[1536,768]{1,0:T(8,128)}, f32[1536,768]{1,0:T(8,128)}, bf16[16,96,3456]{2,1,0:T(8,128)(2,1)}) custom-call(s32[10]{0:T(128)} %concatenate.211.refs_0_, bf16[1536,768]{1,0:T(8,128)(2,1)} %get-tuple-element.60.refs_1_, bf16[768,1536]{1,0:T(8,128)(2,1)} %get-tuple-element.61.refs_2_, bf16[1536,768]{1,0:T(8,128)(2,1)} %bitcast_select_fusion.refs_5_.refs_3_, ...), custom_call_target="tpu_custom_call" | custom-call | flops 29899999232 | bytes 1000000 | tf_op jit(solution)/shard_map/mlp/pallas_call | solution.py:994
  174.6 26.9 %mlp.4 = (f32[1536,768]{1,0:T(8,128)}, f32[1536,768]{1,0:T(8,128)}, bf16[16,96,3456]{2,1,0:T(8,128)(2,1)}) custom-call(s32[10]{0:T(128)} %concatenate.211.refs_0_, bf16[1536,768]{1,0:T(8,128)(2,1)} %get-tuple-element.60.refs_1_, bf16[768,1536]{1,0:T(8,128)(2,1)} %get-tuple-element.61.refs_2_, ...), custom_call_target="tpu_custom_call", output_to_operand_aliasing={{2}: (8, {})} | custom-call | flops 29899999232 | bytes 1000000 | tf_op jit(solution)/shard_map/mlp/pallas_call | solution.py:994
  201.5 26.6 %mlp.5 = (f32[1536,768]{1,0:T(8,128)}, f32[1536,768]{1,0:T(8,128)}, bf16[16,96,3456]{2,1,0:T(8,128)(2,1)}) custom-call(s32[10]{0:T(128)} %concatenate.211.refs_0_, bf16[1536,768]{1,0:T(8,128)(2,1)} %get-tuple-element.60.refs_1_, bf16[768,1536]{1,0:T(8,128)(2,1)} %get-tuple-element.61.refs_2_, ...), custom_call_target="tpu_custom_call", output_to_operand_aliasing={{2}: (8, {})} | custom-call | flops 29899999232 | bytes 1000000 | tf_op jit(solution)/shard_map/mlp/pallas_call | solution.py:994
  229.2 18.3 %second_norm.1 = (bf16[3,256,768]{2,1,0:T(8,128)(2,1)}, bf16[3,256,768]{2,1,0:T(8,128)(2,1)}, f32[1536,768]{1,0:T(8,128)}, bf16[3,2,256,384]{3,2,1,0:T(8,128)(2,...) custom-call(s32[10]{0:T(128)} %concatenate.211.refs_0_, ...), custom_call_target="tpu_custom_call", output_to_operand_aliasing={{5}: (10, {})} | custom-call | flops 20700000256 | bytes 1000000 | tf_op jit(solution)/shard_map/second_norm/pallas_call | solution.py:994
  257.4 17.6 %attn_bwd.3 = (bf16[3,1024,384]{2,1,0:T(8,128)(2,1)}, f32[8,128]{1,0:T(8,128)}) custom-call(s32[10]{0:T(128)} %concatenate.211.refs_0_, s32[12]{0:T(128)} %reshape.552.refs_1_, s32[12]{0:T(128)} %reshape.553.refs_2_, bf16[3,1024,1152]{2,1,0:T(8,128)(2,1)} %get-tuple-element.56.refs_3_, bf16[3,2,256,384]{3,2,1,0:T(8,128)(2,1)} %get-tuple-element.74.refs_4_, ...), custom_call_target="tpu_custom_call" | custom-call | flops 20316665856 | bytes 1000000 | tf_op jit(solution)/shard_map/attn_bwd/pallas_call | solution.py:994
  275.0 7.3 %gw_in.3 = bf16[2,4,96,384]{3,2,1,0:T(8,128)(2,1)} custom-call(s32[10]{0:T(128)} %concatenate.211.refs_0_, bf16[768,3072]{1,0:T(8,128)(2,1)} %get-tuple-element.80.refs_1_, bf16[3,1024,384]{2,1,0:T(8,128)(2,1)} %get-tuple-element.78.refs_2_.refs_1_), custom_call_target="tpu_custom_call" | custom-call | flops 4216666624 | bytes 1000000 | tf_op jit(solution)/shard_map/gw_in/pallas_call | solution.py:994
  283.3 6.7 %collective-permute-start.15 = (bf16[4,96,384]{2,1,0:T(8,128)(2,1)S(1)}, bf16[4,96,384]{2,1,0:T(8,128)(2,1)S(1)}, u32[]{:S(2)}, u32[]{:S(2)}) collective-permute-start(bf16[4,96,384]{2,1,0:T(8,128)(2,1)S(1)} %slice_bitcast_fusion.5), channel_id=1, source_target_pairs={{0,4},{4,0},{8,12},{12,8},{16,20},{20,16},{24,28},{28,24},{1,5},{5... | collective-permute-start | bytes 884744 | tf_op jit(solution)/shard_map/ppermute | solution.py:829
  297.2 17.3 %attn_bwd.4 = (bf16[3,1024,384]{2,1,0:T(8,128)(2,1)}, f32[8,128]{1,0:T(8,128)}) custom-call(s32[10]{0:T(128)} %concatenate.211.refs_0_, s32[12]{0:T(128)} %reshape.552.refs_1_, s32[12]{0:T(128)} %reshape.553.refs_2_, bf16[3,1024,1152]{2,1,0:T(8,128)(2,1)} %get-tuple-element.56.refs_3_, bf16[3,2,256,384]{3,2,1,0:T(8,128)(2,1)} %get-tuple-element.74.refs_4_, ...), custom_call_target="tpu_custom_call" | custom-call | flops 20316665856 | bytes 1000000 | tf_op jit(solution)/shard_map/attn_bwd/pallas_call | solution.py:994
  314.5 7.0 %gw_in.4 = bf16[2,4,96,384]{3,2,1,0:T(8,128)(2,1)} custom-call(s32[10]{0:T(128)} %concatenate.211.refs_0_, bf16[768,3072]{1,0:T(8,128)(2,1)} %get-tuple-element.80.refs_1_, bf16[3,1024,384]{2,1,0:T(8,128)(2,1)} %get-tuple-element.79.refs_2_), custom_call_target="tpu_custom_call" | custom-call | flops 4216666624 | bytes 1000000 | tf_op jit(solution)/shard_map/gw_in/pallas_call | solution.py:994
  323.3 5.6 %collective-permute-start.32 = (bf16[4,96,384]{2,1,0:T(8,128)(2,1)S(1)}, bf16[4,96,384]{2,1,0:T(8,128)(2,1)S(1)}, u32[]{:S(2)}, u32[]{:S(2)}) collective-permute-start(bf16[4,96,384]{2,1,0:T(8,128)(2,1)S(1)} %slice_bitcast_fusion.2), channel_id=1, source_target_pairs={{0,4},{4,0},{8,12},{12,8},{16,20},{20,16},{24,28},{28,24},{1,5},{5... | collective-permute-start | bytes 884744 | tf_op jit(solution)/shard_map/ppermute | solution.py:829
  333.5 9.1 %collective-permute-done.32 = bf16[4,96,384]{2,1,0:T(8,128)(2,1)S(1)} collective-permute-done((bf16[4,96,384]{2,1,0:T(8,128)(2,1)S(1)}, bf16[4,96,384]{2,1,0:T(8,128)(2,1)S(1)}, u32[]{:S(2)}, u32[]{:S(2)}) %collective-permute-start.32) | collective-permute-done | bytes 294944 | tf_op jit(solution)/shard_map/ppermute | solution.py:829
  353.9 5.3 %fusion.refs_15_ = bf16[512,6,384]{2,1,0:T(8,128)(2,1)} fusion(bf16[6,256,384]{2,0,1:T(8,128)(2,1)S(1)} %copy.82, bf16[6,256,384]{2,0,1:T(8,128)(2,1)S(1)} %get-tuple-element.144, pred[]{:T(512)S(6)} %eq.92), kind=kLoop, calls=%fused_computation.3 | loop fusion | flops 3538944 | bytes 4718593 | tf_op jit(solution)/shard_map/transpose | solution.py:1226
  359.2 17.0 %attn_bwd.5 = (bf16[3,1024,384]{2,1,0:T(8,128)(2,1)}, f32[8,128]{1,0:T(8,128)}) custom-call(s32[10]{0:T(128)} %concatenate.211.refs_0_, s32[12]{0:T(128)} %reshape.552.refs_1_, s32[12]{0:T(128)} %reshape.553.refs_2_, bf16[3,1024,1152]{2,1,0:T(8,128)(2,1)} %get-tuple-element.56.refs_3_, bf16[3,2,256,384]{3,2,1,0:T(8,128)(2,1)} %get-tuple-element.74.refs_4_, ...), custom_call_target="tpu_custom_call" | custom-call | flops 20316665856 | bytes 1000000 | tf_op jit(solution)/shard_map/attn_bwd/pallas_call | solution.py:994
  376.2 7.1 %gh1.5 = (bf16[2,256,768]{2,1,0:T(8,128)(2,1)}, bf16[2,256,768]{2,1,0:T(8,128)(2,1)}) custom-call(s32[10]{0:T(128)} %concatenate.211.refs_0_, bf16[3,1024,384]{2,1,0:T(8,128)(2,1)} %get-tuple-element.78.refs_2_.refs_1_, bf16[3,1024,384]{2,1,0:T(8,128)(2,1)} %get-tuple-element.79.refs_2_, bf16[3,1024,384]{2,1,0:T(8,128)(2,1)} %get-tuple-element.81.refs_3_.refs_2_, ...), custom_call_target="tpu_custom_call" | custom-call | flops 4600000000 | bytes 1000000 | tf_op jit(solution)/shard_map/gh1/pallas_call | solution.py:994
  383.4 7.1 %gh1.4 = (bf16[2,256,768]{2,1,0:T(8,128)(2,1)}, bf16[2,256,768]{2,1,0:T(8,128)(2,1)}) custom-call(s32[10]{0:T(128)} %concatenate.211.refs_0_, bf16[3,1024,384]{2,1,0:T(8,128)(2,1)} %get-tuple-element.78.refs_2_.refs_1_, bf16[3,1024,384]{2,1,0:T(8,128)(2,1)} %get-tuple-element.79.refs_2_, bf16[3,1024,384]{2,1,0:T(8,128)(2,1)} %get-tuple-element.81.refs_3_.refs_2_, ...), custom_call_target="tpu_custom_call" | custom-call | flops 4600000000 | bytes 1000000 | tf_op jit(solution)/shard_map/gh1/pallas_call | solution.py:994
  391.0 7.1 %gh1.3 = (bf16[2,256,768]{2,1,0:T(8,128)(2,1)}, bf16[2,256,768]{2,1,0:T(8,128)(2,1)}) custom-call(s32[10]{0:T(128)} %concatenate.211.refs_0_, bf16[3,1024,384]{2,1,0:T(8,128)(2,1)} %get-tuple-element.78.refs_2_.refs_1_, bf16[3,1024,384]{2,1,0:T(8,128)(2,1)} %get-tuple-element.79.refs_2_, bf16[3,1024,384]{2,1,0:T(8,128)(2,1)} %get-tuple-element.81.refs_3_.refs_2_, ...), custom_call_target="tpu_custom_call" | custom-call | flops 4600000000 | bytes 1000000 | tf_op jit(solution)/shard_map/gh1/pallas_call | solution.py:994
  398.2 6.8 %gw_in.5 = bf16[2,4,96,384]{3,2,1,0:T(8,128)(2,1)} custom-call(s32[10]{0:T(128)} %concatenate.211.refs_0_, bf16[768,3072]{1,0:T(8,128)(2,1)} %get-tuple-element.80.refs_1_, bf16[3,1024,384]{2,1,0:T(8,128)(2,1)} %get-tuple-element.81.refs_3_.refs_2_), custom_call_target="tpu_custom_call" | custom-call | flops 4216666624 | bytes 1000000 | tf_op jit(solution)/shard_map/gw_in/pallas_call | solution.py:994
  406.0 7.4 %collective-permute-start.37 = (bf16[4,96,384]{2,1,0:T(8,128)(2,1)S(1)}, bf16[4,96,384]{2,1,0:T(8,128)(2,1)S(1)}, u32[]{:S(2)}, u32[]{:S(2)}) collective-permute-start(bf16[4,96,384]{2,1,0:T(8,128)(2,1)S(1)} %slice_bitcast_fusion), channel_id=1, source_target_pairs={{0,4},{4,0},{8,12},{12,8},{16,20},{20,16},{24,28},{28,24},{1,5},{5... | collective-permute-start | bytes 884744 | tf_op jit(solution)/shard_map/ppermute | solution.py:829
  414.1 6.9 %collective-permute-done.37 = bf16[4,96,384]{2,1,0:T(8,128)(2,1)S(1)} collective-permute-done((bf16[4,96,384]{2,1,0:T(8,128)(2,1)S(1)}, bf16[4,96,384]{2,1,0:T(8,128)(2,1)S(1)}, u32[]{:S(2)}, u32[]{:S(2)}) %collective-permute-start.37) | collective-permute-done | bytes 294944 | tf_op jit(solution)/shard_map/ppermute | solution.py:829
  502.6 9.8 %collective-permute-done.42 = bf16[96,3456]{1,0:T(8,128)(2,1)S(1)} collective-permute-done((bf16[96,3456]{1,0:T(8,128)(2,1)}, bf16[96,3456]{1,0:T(8,128)(2,1)S(1)}, u32[]{:S(2)}, u32[]{:S(2)}) %collective-permute-start.42) | collective-permute-done | bytes 663584 | tf_op jit(solution)/shard_map/ppermute | solution.py:805
  (338 shorter events, 174.8 us)
Async XLA Ops:
  7.2 128.1 %all-gather.5.cloned.1.call-start = ((), (), s32[]{:S(2)}) async-start(), calls=%async_computation.2 | async-start | bytes 7938048 | tf_op jit(solution)/shard_map/all_gather | solution.py:934
  12.6 188.9 %all-gather.7.cloned.1.call-start = ((), (), s32[]{:S(2)}) async-start(), calls=%async_computation.3 | async-start | bytes 3342336 | tf_op jit(solution)/shard_map/all_gather | solution.py:934
  14.3 21.1 %collective-permute-start.2 = (bf16[112,1152]{1,0:T(8,128)(2,1)}, bf16[112,1152]{1,0:T(8,128)(2,1)}, u32[]{:S(2)}, u32[]{:S(2)}) collective-permute-start(bf16[112,1152]{1,0:T(8,128)(2,1)} %fusion.2.refs_8_.refs_4_), channel_id=1, source_target_pairs={{0,4},{4,0},{8,12},{12,8},{16,20},{20,16},{24,28},{28,24},{1,5},{5... | collective-permute-start | bytes 774152 | tf_op jit(solution)/shard_map/ppermute | solution.py:829
  17.3 18.2 %collective-permute-start.3 = (bf16[112,1152]{1,0:T(8,128)(2,1)}, bf16[112,1152]{1,0:T(8,128)(2,1)}, u32[]{:S(2)}, u32[]{:S(2)}) collective-permute-start(bf16[112,1152]{1,0:T(8,128)(2,1)} %fusion.2.refs_8_.refs_4_), channel_id=1, source_target_pairs={{8,0},{12,4},{16,8},{20,12},{24,16},{28,20},{0,24},{4,28},{9,1},{1... | collective-permute-start | bytes 774152 | tf_op jit(solution)/shard_map/ppermute | solution.py:821
  20.9 35.9 %collective-permute-start.5 = (bf16[112,1152]{1,0:T(8,128)(2,1)}, bf16[112,1152]{1,0:T(8,128)(2,1)}, u32[]{:S(2)}, u32[]{:S(2)}) collective-permute-start(bf16[112,1152]{1,0:T(8,128)(2,1)} %fusion.2.refs_8_.refs_4_), channel_id=1, source_target_pairs={{16,0},{20,4},{24,8},{28,12},{0,16},{4,20},{8,24},{12,28},{17,1},{... | collective-permute-start | bytes 774152 | tf_op jit(solution)/shard_map/ppermute | solution.py:821
  20.9 36.0 %collective-permute-start.7 = (bf16[112,1152]{1,0:T(8,128)(2,1)}, bf16[112,1152]{1,0:T(8,128)(2,1)}, u32[]{:S(2)}, u32[]{:S(2)}) collective-permute-start(bf16[112,1152]{1,0:T(8,128)(2,1)} %fusion.2.refs_8_.refs_4_), channel_id=1, source_target_pairs={{24,0},{28,4},{0,8},{4,12},{8,16},{12,20},{16,24},{20,28},{25,1},{... | collective-permute-start | bytes 774152 | tf_op jit(solution)/shard_map/ppermute | solution.py:821
  24.3 39.7 %collective-permute-start = (bf16[3,256,768]{2,1,0:T(8,128)(2,1)}, bf16[3,256,768]{2,1,0:T(8,128)(2,1)}, u32[]{:S(2)}, u32[]{:S(2)}) collective-permute-start(bf16[3,256,768]{2,1,0:T(8,128)(2,1)} %dynamic-slice_bitcast_fusion.5), channel_id=1, source_target_pairs={{0,2},{2,0},{1,3},{3,1},{4,6},{6,4},{5,7},{7,5},{8,10},{10,8},{9,1... | collective-permute-start | bytes 3538952 | tf_op jit(solution)/shard_map/ppermute | solution.py:805
  35.4 37.4 %collective-permute-start.10 = (bf16[256,6,384]{2,0,1:T(8,128)(2,1)}, bf16[256,6,384]{2,0,1:T(8,128)(2,1)S(1)}, u32[]{:S(2)}, u32[]{:S(2)}) collective-permute-start(bf16[256,6,384]{2,0,1:T(8,128)(2,1)} %get-tuple-element.149), channel_id=1, source_target_pairs={{0,1},{1,0},{2,3},{3,2},{4,5},{5,4},{6,7},{7,6},{8,9},{9,8},{10,11... | collective-permute-start | bytes 3538952 | tf_op jit(solution)/shard_map/ppermute | solution.py:805
  35.4 24.8 %collective-permute-start.4 = (bf16[112,1152]{1,0:T(8,128)(2,1)}, bf16[112,1152]{1,0:T(8,128)(2,1)S(1)}, u32[]{:S(2)}, u32[]{:S(2)}) collective-permute-start(bf16[112,1152]{1,0:T(8,128)(2,1)} %collective-permute-done.3.refs_10_.refs_6_), channel_id=1, source_target_pairs={{0,4},{4,0},{8,12},{12,8},{16,20},{20,16},{24,28},{28,24},{1,5},{5... | collective-permute-start | bytes 774152 | tf_op jit(solution)/shard_map/ppermute | solution.py:829
  73.6 59.5 %collective-permute-start.11 = (bf16[3,256,768]{2,1,0:T(8,128)(2,1)S(1)}, bf16[3,256,768]{2,1,0:T(8,128)(2,1)S(1)}, u32[]{:S(2)}, u32[]{:S(2)}) collective-permute-start(bf16[3,256,768]{2,1,0:T(8,128)(2,1)S(1)} %get-tuple-element.147), channel_id=1, source_target_pairs={{0,2},{2,0},{1,3},{3,1},{4,6},{6,4},{5,7},{7,5},{8,10},{10,8},{9,1... | collective-permute-start | bytes 3538952 | tf_op jit(solution)/shard_map/ppermute | solution.py:805
  130.8 364.6 %reduce-scatter.2.cloned.1.call-start = ((), (), s32[]{:S(2)}) async-start(), calls=%async_computation.1 | async-start | bytes 11280384 | tf_op jit(solution)/shard_map/reduce_scatter | solution.py:1134
  248.6 41.4 %collective-permute-start.12 = (bf16[3,256,768]{2,1,0:T(8,128)(2,1)}, bf16[3,256,768]{2,1,0:T(8,128)(2,1)}, u32[]{:S(2)}, u32[]{:S(2)}) collective-permute-start(bf16[3,256,768]{2,1,0:T(8,128)(2,1)} %get-tuple-element.73), channel_id=1, source_target_pairs={{0,2},{2,0},{1,3},{3,1},{4,6},{6,4},{5,7},{7,5},{8,10},{10,8},{9,1... | collective-permute-start | bytes 3538952 | tf_op jit(solution)/shard_map/ppermute | solution.py:805
  283.3 46.3 %collective-permute-start.15 = (bf16[4,96,384]{2,1,0:T(8,128)(2,1)S(1)}, bf16[4,96,384]{2,1,0:T(8,128)(2,1)S(1)}, u32[]{:S(2)}, u32[]{:S(2)}) collective-permute-start(bf16[4,96,384]{2,1,0:T(8,128)(2,1)S(1)} %slice_bitcast_fusion.5), channel_id=1, source_target_pairs={{0,4},{4,0},{8,12},{12,8},{16,20},{20,16},{24,28},{28,24},{1,5},{5... | collective-permute-start | bytes 884744 | tf_op jit(solution)/shard_map/ppermute | solution.py:829
  297.1 56.1 %collective-permute-start.13 = (bf16[6,256,384]{2,1,0:T(8,128)(2,1)S(1)}, bf16[6,256,384]{2,1,0:T(8,128)(2,1)S(1)}, u32[]{:S(2)}, u32[]{:S(2)}) collective-permute-start(bf16[6,256,384]{2,1,0:T(8,128)(2,1)S(1)} %bitcast.209), channel_id=1, source_target_pairs={{0,1},{1,0},{2,3},{3,2},{4,5},{5,4},{6,7},{7,6},{8,9},{9,8},{10,11... | collective-permute-start | bytes 3538952 | tf_op jit(solution)/shard_map/ppermute | solution.py:805
  323.3 19.4 %collective-permute-start.32 = (bf16[4,96,384]{2,1,0:T(8,128)(2,1)S(1)}, bf16[4,96,384]{2,1,0:T(8,128)(2,1)S(1)}, u32[]{:S(2)}, u32[]{:S(2)}) collective-permute-start(bf16[4,96,384]{2,1,0:T(8,128)(2,1)S(1)} %slice_bitcast_fusion.2), channel_id=1, source_target_pairs={{0,4},{4,0},{8,12},{12,8},{16,20},{20,16},{24,28},{28,24},{1,5},{5... | collective-permute-start | bytes 884744 | tf_op jit(solution)/shard_map/ppermute | solution.py:829
  329.8 16.9 %collective-permute-start.30 = (bf16[96,384]{1,0:T(8,128)(2,1)S(1)}, bf16[96,384]{1,0:T(8,128)(2,1)S(1)}, u32[]{:S(2)}, u32[]{:S(2)}) collective-permute-start(bf16[96,384]{1,0:T(8,128)(2,1)S(1)} %get-tuple-element.169), channel_id=1, source_target_pairs={{8,0},{12,4},{16,8},{20,12},{24,16},{28,20},{0,24},{4,28},{9,1},{1... | collective-permute-start | bytes 221192 | tf_op jit(solution)/shard_map/ppermute | solution.py:821
  352.5 102.6 %collective-permute-start.36 = (bf16[96,384]{1,0:T(8,128)(2,1)}, bf16[96,384]{1,0:T(8,128)(2,1)}, u32[]{:S(2)}, u32[]{:S(2)}) collective-permute-start(bf16[96,384]{1,0:T(8,128)(2,1)} %fusion.25), channel_id=1, source_target_pairs={{0,2},{2,0},{1,3},{3,1},{4,6},{6,4},{5,7},{7,5},{8,10},{10,8},{9,1... | collective-permute-start | bytes 221192 | tf_op jit(solution)/shard_map/ppermute | solution.py:805
  383.3 38.8 %collective-permute-start.20 = (bf16[2,256,768]{2,1,0:T(8,128)(2,1)}, bf16[2,256,768]{2,1,0:T(8,128)(2,1)S(1)}, u32[]{:S(2)}, u32[]{:S(2)}) collective-permute-start(bf16[2,256,768]{2,1,0:T(8,128)(2,1)} %get-tuple-element.90), channel_id=1, source_target_pairs={{0,1},{1,0},{2,3},{3,2},{4,5},{5,4},{6,7},{7,6},{8,9},{9,8},{10,11... | collective-permute-start | bytes 2359304 | tf_op jit(solution)/shard_map/ppermute | solution.py:805
  390.5 37.4 %collective-permute-start.18 = (bf16[2,256,768]{2,1,0:T(8,128)(2,1)}, bf16[2,256,768]{2,1,0:T(8,128)(2,1)S(1)}, u32[]{:S(2)}, u32[]{:S(2)}) collective-permute-start(bf16[2,256,768]{2,1,0:T(8,128)(2,1)} %get-tuple-element.87), channel_id=1, source_target_pairs={{0,1},{1,0},{2,3},{3,2},{4,5},{5,4},{6,7},{7,6},{8,9},{9,8},{10,11... | collective-permute-start | bytes 2359304 | tf_op jit(solution)/shard_map/ppermute | solution.py:805
  398.1 35.6 %collective-permute-start.16 = (bf16[2,256,768]{2,1,0:T(8,128)(2,1)}, bf16[2,256,768]{2,1,0:T(8,128)(2,1)S(1)}, u32[]{:S(2)}, u32[]{:S(2)}) collective-permute-start(bf16[2,256,768]{2,1,0:T(8,128)(2,1)} %get-tuple-element.83), channel_id=1, source_target_pairs={{0,1},{1,0},{2,3},{3,2},{4,5},{5,4},{6,7},{7,6},{8,9},{9,8},{10,11... | collective-permute-start | bytes 2359304 | tf_op jit(solution)/shard_map/ppermute | solution.py:805
  451.2 24.8 %collective-permute-start.24 = (bf16[256,768]{1,0:T(8,128)(2,1)}, bf16[256,768]{1,0:T(8,128)(2,1)S(1)}, u32[]{:S(2)}, u32[]{:S(2)}) collective-permute-start(bf16[256,768]{1,0:T(8,128)(2,1)} %get-tuple-element.93), channel_id=1, source_target_pairs={{0,2},{2,0},{1,3},{3,1},{4,6},{6,4},{5,7},{7,5},{8,10},{10,8},{9,1... | collective-permute-start | bytes 1179656 | tf_op jit(solution)/shard_map/ppermute | solution.py:805
  452.6 20.3 %collective-permute-start.22 = (bf16[256,768]{1,0:T(8,128)(2,1)}, bf16[256,768]{1,0:T(8,128)(2,1)}, u32[]{:S(2)}, u32[]{:S(2)}) collective-permute-start(bf16[256,768]{1,0:T(8,128)(2,1)} %get-tuple-element.92), channel_id=1, source_target_pairs={{0,2},{2,0},{1,3},{3,1},{4,6},{6,4},{5,7},{7,5},{8,10},{10,8},{9,1... | collective-permute-start | bytes 1179656 | tf_op jit(solution)/shard_map/ppermute | solution.py:805
  461.8 17.7 %collective-permute-start.26 = (bf16[256,768]{1,0:T(8,128)(2,1)}, bf16[256,768]{1,0:T(8,128)(2,1)S(1)}, u32[]{:S(2)}, u32[]{:S(2)}) collective-permute-start(bf16[256,768]{1,0:T(8,128)(2,1)} %get-tuple-element.94), channel_id=1, source_target_pairs={{0,2},{2,0},{1,3},{3,1},{4,6},{6,4},{5,7},{7,5},{8,10},{10,8},{9,1... | collective-permute-start | bytes 1179656 | tf_op jit(solution)/shard_map/ppermute | solution.py:805
  495.4 17.0 %collective-permute-start.42 = (bf16[96,3456]{1,0:T(8,128)(2,1)}, bf16[96,3456]{1,0:T(8,128)(2,1)S(1)}, u32[]{:S(2)}, u32[]{:S(2)}) collective-permute-start(bf16[96,3456]{1,0:T(8,128)(2,1)} %bitcast.210), channel_id=1, source_target_pairs={{0,2},{2,0},{1,3},{3,1},{4,6},{6,4},{5,7},{7,5},{8,10},{10,8},{9,1... | collective-permute-start | bytes 1990664 | tf_op jit(solution)/shard_map/ppermute | solution.py:805
  (77 other events, 756.7 us)
Sparse Core Ops, SparseCore 0:
  12.7 88.3 all-gather.4
  130.9 46.9 all-gather.6
  257.5 130.0 reduce-scatter.1

commit v3 on v2

--- a/solution.py
+++ b/solution.py
@@ -293,16 +293,14 @@
 query_block = 256
 windows = (384, 512, 1024)
 vmem_bytes = 56 * 1024 * 1024
+hidden_chunk = 512
 micros = {
-    "qkv": 23,
-    "attn_fwd": 29,
-    "attn_out": 13,
-    "mlp": 26,
-    "second_norm": 18,
-    "attn_bwd": 53,
-    "gw_in": 11,
-    "gh1": 12,
-    "first_norm": 10,
+    "qkv": 25,
+    "attn_fwd": 22,
+    "middle": 80,
+    "attn_bwd": 60,
+    "first_norm": 8,
+    "place": 4,
 }
 
 
@@ -312,16 +310,16 @@
     )
 
 
-def params(count):
+def params(count, vmem):
     return pltpu.CompilerParams(
-        dimension_semantics=("arbitrary",) * count, vmem_limit_bytes=vmem_bytes
+        dimension_semantics=("arbitrary",) * count, vmem_limit_bytes=vmem
     )
 
 
 def split_dot(values, ones_matrix):
     top = values.astype(low)
     rest = (values - top.astype(wide)).astype(low)
-    return dot(top, ones_matrix) + dot(rest, ones_matrix)
+    return dot(jnp.concatenate([top, rest], axis=1), ones_matrix)
 
 
 def load_pieces(info_ref, sets, scratch, sems):
@@ -375,16 +373,19 @@
     def _():
         run_all(load_pieces(info_ref, [(pieces, 0, w_ref.shape[1], 0)], w_ref, sems))
 
-    x = jnp.where(
-        sub // 2 == info_ref[0],
-        mine_ref[0],
-        jnp.where(sub % 2 == info_ref[1], got_ref[0], far_ref[0]),
-    ).astype(wide)
+    first_core = info_ref[1] == 0
+    moved = jnp.concatenate(
+        [
+            jnp.where(first_core, got_ref[0], far_ref[0]),
+            jnp.where(first_core, far_ref[0], got_ref[0]),
+        ],
+        axis=0,
+    )
+    x = jnp.where(sub == info_ref[0], mine_ref[0], moved).astype(wide)
     centered = x - jnp.mean(x, axis=1, keepdims=True)
     variance = jnp.mean(centered * centered, axis=1, keepdims=True)
-    h_wide = centered * lax.rsqrt(variance + norm_eps) * gain_ref[...] + bias_ref[...]
-    h = h_wide.astype(low)
-    ht_ref[...] = jnp.transpose(h_wide).astype(low)
+    h = (centered * lax.rsqrt(variance + norm_eps) * gain_ref[...] + bias_ref[...]).astype(low)
+    ht_ref[...] = jnp.transpose(h)
     means = mean_ref[...]
     projected = dot(h, w_ref[...])
     for at in range(0, projected.shape[1], 128):
@@ -393,7 +394,7 @@
             p_ref[0, :, at : at + 128] = raw.astype(low)
             continue
         inner = raw - split_dot(raw, means)
-        rate = lax.rsqrt(dot((inner * inner).astype(low), means) + norm_eps)
+        rate = lax.rsqrt(dot((inner * inner).astype(low), means[:128]) + norm_eps)
         to = at // 384 * 256 + at % 384
         rate_ref[0, :, to : to + 128] = rate
         p_ref[0, :, at : at + 128] = (inner * rate * hg_ref[:, to : to + 128]).astype(low)
@@ -404,6 +405,7 @@
 ):
     seq = pl.program_id(0)
     blocks = p_ref.shape[1] // query_block
+    pairs = p_ref.shape[2] // 384
     lane = lax.broadcasted_iota(jnp.int32, (query_block, 128), 1)
 
     def step(block, carry):
@@ -412,31 +414,35 @@
 
         def body(size):
             begin = pl.multiple_of(start_ref[which], 16)
-            q_pair = p_ref[0, pl.ds(row, query_block), 0:128]
-            q_side = aug_ref[0, pl.ds(row, query_block), :] * side_ref[...]
-            keys = jnp.concatenate(
-                [p_ref[0, pl.ds(begin, size), 128:256], aug_ref[0, pl.ds(begin, size), :]], axis=1
-            )
-            values = jnp.concatenate(
-                [p_ref[0, pl.ds(begin, size), 256:384], jnp.ones((size, 128), low)], axis=1
-            )
-            mixed = []
-            for head in range(2):
-                mine = jnp.where(lane // 64 == head, q_pair, jnp.zeros_like(q_pair))
-                scores = dot(jnp.concatenate([mine, q_side], axis=1), keys, 1, 1)
-                mixed.append(dot(jnp.exp2(scores).astype(low), values))
-            inverse = 1.0 / jnp.where(lane < 64, mixed[0][:, 128:], mixed[1][:, 128:])
-            outcome = jnp.where(lane < 64, mixed[0][:, :128], mixed[1][:, :128]) * inverse
+            rows = pl.ds(row, query_block)
+            span = pl.ds(begin, size)
+            q_side = aug_ref[0, rows, :] * side_ref[...]
+            k_side = aug_ref[0, span, :]
+            ones = jnp.ones((size, 128), low)
+            outcomes = []
+            for pair in range(pairs):
+                at = 384 * pair
+                q_pair = p_ref[0, rows, at : at + 128]
+                keys = jnp.concatenate([p_ref[0, span, at + 128 : at + 256], k_side], axis=1)
+                values = jnp.concatenate([p_ref[0, span, at + 256 : at + 384], ones], axis=1)
+                mixed = []
+                for head in range(2):
+                    mine = jnp.where(lane // 64 == head, q_pair, jnp.zeros_like(q_pair))
+                    scores = dot(jnp.concatenate([mine, q_side], axis=1), keys, 1, 1)
+                    mixed.append(dot(jnp.exp2(scores).astype(low), values))
+                inverse = 1.0 / jnp.where(lane < 64, mixed[0][:, 128:], mixed[1][:, 128:])
+                outcome = jnp.where(lane < 64, mixed[0][:, :128], mixed[1][:, :128]) * inverse
+                outcomes.append(outcome.astype(low))
+                inv_ref[0, rows, 128 * pair : 128 * pair + 128] = inverse
+            outcome = jnp.concatenate(outcomes, axis=1)
 
             @pl.when(block % 2 == info_ref[1])
             def _():
-                mine_ref[0, block // 2] = outcome.astype(low)
+                mine_ref[0, block // 2] = outcome
 
             @pl.when(block % 2 != info_ref[1])
             def _():
-                send_ref[0, block // 2] = outcome.astype(low)
-
-            inv_ref[0, pl.ds(row, query_block), :] = inverse
+                send_ref[0, block // 2] = outcome
 
         for index, size in enumerate(windows):
             pl.when(kind_ref[which] == index)(partial(body, size))
@@ -447,6 +453,9 @@
 
 def attn_bwd_kernel(
     base,
+    scale,
+    first,
+    final,
     info_ref,
     start_ref,
     kind_ref,
@@ -461,15 +470,27 @@
     side_ref,
     hg_ref,
     mean_ref,
-    g_ref,
-    gain_ref,
-    gq_acc,
-    gk_acc,
-    gv_acc,
+    ht_ref,
+    *refs,
 ):
-    seq = pl.program_id(0) + base
+    pieces, refs = refs[:8], refs[8:]
+    if not first:
+        gw_in_ref, *refs = refs
+    mine_ref, send_ref, gw_ref, gain_ref, *refs = refs
+    gq_acc, gk_acc, gv_acc, g_all, gw_acc, w_ref, sems = refs
+    step_id = pl.program_id(0)
+    seq = step_id + base
     blocks = p_ref.shape[1] // query_block
+    pairs = p_ref.shape[2] // 384
     lane = lax.broadcasted_iota(jnp.int32, (query_block, 128), 1)
+
+    @pl.when(step_id == 0)
+    def _():
+        for copy in load_pieces(info_ref, [(pieces, 0, w_ref.shape[1], 0)], w_ref, sems):
+            copy.start()
+        gain_ref[...] = jnp.zeros_like(gain_ref)
+        gw_acc[...] = jnp.zeros_like(gw_acc) if first else gw_in_ref[...]
+
     gk_acc[...] = jnp.zeros_like(gk_acc)
     gv_acc[...] = jnp.zeros_like(gv_acc)
 
@@ -481,99 +502,106 @@
             begin = pl.multiple_of(start_ref[which], 16)
             rows = pl.ds(row, query_block)
             span = pl.ds(begin, size)
-            q_pair = p_ref[0, rows, 0:128]
             q_side = aug_ref[0, rows, :] * side_ref[...]
-            k_pair = p_ref[0, span, 128:256]
             k_side = aug_ref[0, span, :]
-            keys = jnp.concatenate([k_pair, k_side], axis=1)
-            values = jnp.concatenate([p_ref[0, span, 256:384], k_side], axis=1)
             near = block % 2 == info_ref[1]
-            go = jnp.where(near, go_mine_ref[0, block // 2], go_got_ref[0, block // 2])
-            o = jnp.where(near, o_mine_ref[0, block // 2], o_send_ref[0, block // 2])
-            scaled = go.astype(wide) * inv_ref[0, rows, :]
-            scaled_low = scaled.astype(low)
-            product = scaled_low.astype(wide) * o.astype(wide)
-            powers, grads, queries, pulls = [], [], [], []
-            for head in range(2):
-                mine = lane // 64 == head
-                inner = jnp.sum(jnp.where(mine, product, 0.0), axis=1, keepdims=True)
-                one = inner.astype(low)
-                two = (inner - one.astype(wide)).astype(low)
-                three = (inner - one.astype(wide) - two.astype(wide)).astype(low)
-                go_side = jnp.where(
-                    lane == 6,
-                    -one,
-                    jnp.where(lane == 7, -two, jnp.where(lane == 8, -three, jnp.zeros_like(q_pair))),
+            for pair in range(pairs):
+                at = 384 * pair
+                lanes = slice(128 * pair, 128 * pair + 128)
+                q_pair = p_ref[0, rows, at : at + 128]
+                k_pair = p_ref[0, span, at + 128 : at + 256]
+                keys = jnp.concatenate([k_pair, k_side], axis=1)
+                values = jnp.concatenate([p_ref[0, span, at + 256 : at + 384], k_side], axis=1)
+                go = jnp.where(
+                    near, go_mine_ref[0, block // 2, :, lanes], go_got_ref[0, block // 2, :, lanes]
                 )
-                q_mine = jnp.where(mine, q_pair, jnp.zeros_like(q_pair))
-                go_mine = jnp.where(mine, scaled_low, jnp.zeros_like(q_pair))
-                power = jnp.exp2(dot(keys, jnp.concatenate([q_mine, q_side], axis=1), 1, 1))
-                slope = dot(values, jnp.concatenate([go_mine, go_side], axis=1), 1, 1)
-                grad = (power * slope).astype(low)
-                powers.append(power.astype(low))
-                grads.append(grad)
-                queries.append(q_mine)
-                pulls.append(go_mine)
-            gv_acc[span, :] += dot(
-                jnp.concatenate(powers, axis=1), jnp.concatenate(pulls, axis=0)
-            )
-            gk_acc[span, :] += dot(
-                jnp.concatenate(grads, axis=1), jnp.concatenate(queries, axis=0)
-            )
-            gq_acc[rows, :] = jnp.where(
-                lane < 64, dot(grads[0], k_pair, 0, 0), dot(grads[1], k_pair, 0, 0)
-            )
+                o = jnp.where(
+                    near, o_mine_ref[0, block // 2, :, lanes], o_send_ref[0, block // 2, :, lanes]
+                )
+                scaled = (go.astype(wide) * inv_ref[0, rows, lanes]).astype(low)
+                product = scaled.astype(wide) * o.astype(wide)
+                powers, grads, queries, pulls = [], [], [], []
+                for head in range(2):
+                    mine = lane // 64 == head
+                    inner = jnp.sum(jnp.where(mine, product, 0.0), axis=1, keepdims=True)
+                    one = inner.astype(low)
+                    two = (inner - one.astype(wide)).astype(low)
+                    three = (inner - one.astype(wide) - two.astype(wide)).astype(low)
+                    none = jnp.zeros_like(q_pair)
+                    go_side = jnp.where(
+                        lane == 6,
+                        -one,
+                        jnp.where(lane == 7, -two, jnp.where(lane == 8, -three, none)),
+                    )
+                    q_mine = jnp.where(mine, q_pair, none)
+                    go_mine = jnp.where(mine, scaled, none)
+                    power = jnp.exp2(dot(keys, jnp.concatenate([q_mine, q_side], axis=1), 1, 1))
+                    slope = dot(values, jnp.concatenate([go_mine, go_side], axis=1), 1, 1)
+                    powers.append(power.astype(low))
+                    grads.append((power * slope).astype(low))
+                    queries.append(q_mine)
+                    pulls.append(go_mine)
+                gv_acc[span, lanes] += dot(
+                    jnp.concatenate(powers, axis=1), jnp.concatenate(pulls, axis=0)
+                )
+                gk_acc[span, lanes] += dot(
+                    jnp.concatenate(grads, axis=1), jnp.concatenate(queries, axis=0)
+                )
+                keys_turned = jnp.transpose(k_pair)
+                turned = [dot(keys_turned[64 * i : 64 * i + 64], grads[i]) for i in range(2)]
+                gq_acc[rows, lanes] = jnp.transpose(jnp.concatenate(turned, axis=0))
 
         for index, size in enumerate(windows):
             pl.when(kind_ref[which] == index)(partial(body, size))
         return carry
 
     lax.fori_loop(0, blocks, step, 0)
-    g_ref[0, :, 256:384] = gv_acc[...].astype(low)
     means = mean_ref[...]
-
-    @pl.when(pl.program_id(0) == 0)
+    for pair in range(pairs):
+        lanes = slice(128 * pair, 128 * pair + 128)
+        g_all[:, 384 * pair + 256 : 384 * pair + 384] = gv_acc[:, lanes].astype(low)
+        for index, acc, factor, unscale in (
+            (0, gq_acc, 0.125, 8.0 / log2e),
+            (1, gk_acc, 1.0 / log2e, 1.0),
+        ):
+            to = slice(384 * pair + 128 * index, 384 * pair + 128 * index + 128)
+            at = slice(256 * pair + 128 * index, 256 * pair + 128 * index + 128)
+            gain = hg_ref[:, at]
+            grad = acc[:, lanes] * factor
+            normed = p_ref[0, :, to].astype(wide) * unscale
+            weighted = grad * gain
+            cross = grad * normed
+            inner = split_dot(weighted, means)
+            outer = split_dot(cross, means)
+            g_all[:, to] = (
+                rate_ref[0, :, at] * (weighted - inner - normed / gain * outer)
+            ).astype(low)
+            gain_ref[0:1, at] += jnp.sum(cross, axis=0, keepdims=True) / gain
+
+    @pl.when(step_id == 0)
     def _():
-        gain_ref[...] = jnp.zeros_like(gain_ref)
-
-    for index, acc, scale, unscale in (
-        (0, gq_acc, 0.125, 8.0 / log2e),
-        (1, gk_acc, 1.0 / log2e, 1.0),
-    ):
-        at = slice(128 * index, 128 * index + 128)
-        gain = hg_ref[:, at]
-        grad = acc[...] * scale
-        normed = p_ref[0, :, at].astype(wide) * unscale
-        weighted = grad * gain
-        cross = grad * normed
-        first = split_dot(weighted, means)
-        second = split_dot(cross, means)
-        g_ref[0, :, at] = (
-            rate_ref[0, :, at] * (weighted - first - normed / gain * second)
-        ).astype(low)
-        gain_ref[index : index + 1, :] += jnp.sum(cross, axis=0, keepdims=True) / gain
-
-
-def attn_out_kernel(info_ref, o_mine_ref, o_got_ref, mine_ref, got_ref, gy_ref, gain_ref, bias_ref, shards, *refs):
-    x2_ref, h_ref, ht_ref, gyt_ref, w_ref, sems = refs
-    cols = o_mine_ref.shape[3]
-    c = info_ref[1]
-
-    @pl.when((pl.program_id(0) == 0) & (pl.program_id(1) == 0))
+        for copy in load_pieces(info_ref, [(pieces, 0, w_ref.shape[1], 0)], w_ref, sems):
+            copy.wait()
+
+    gw_acc[...] += dot(ht_ref[...], g_all[...])
+    everything = dot(g_all[...], w_ref[...], 1, 1).astype(low)
+    for block in range(blocks):
+        result = everything[block * query_block : (block + 1) * query_block]
+
+        @pl.when(block % 2 == info_ref[1])
+        def _():
+            mine_ref[0, block // 2] = result
+
+        @pl.when(block % 2 != info_ref[1])
+        def _():
+            send_ref[0, block // 2] = result
+
+    @pl.when(step_id == pl.num_programs(0) - 1)
     def _():
-        run_all(
-            load_shards([(shards, c, 0, cols, 0), (shards, 1 - c, 0, cols, cols)], w_ref, sems)
-        )
-
-    x = jnp.where(pl.program_id(1) == info_ref[0], mine_ref[0], got_ref[0]).astype(wide)
-    x2 = x + dot(jnp.concatenate([o_mine_ref[0, 0], o_got_ref[0, 0]], axis=1), w_ref[...], 1, 1)
-    x2_ref[...] = x2
-    centered = x2 - jnp.mean(x2, axis=1, keepdims=True)
-    variance = jnp.mean(centered * centered, axis=1, keepdims=True)
-    h = centered * lax.rsqrt(variance + norm_eps) * gain_ref[...] + bias_ref[...]
-    h_ref[...] = h.astype(low)
-    ht_ref[...] = jnp.transpose(h).astype(low)
-    gyt_ref[...] = jnp.transpose(gy_ref[...].astype(wide)).astype(low)
+        if final:
+            spread(info_ref, gw_acc, scale, gw_ref, None, 0, 0, gw_acc.shape[1])
+        else:
+            gw_ref[...] = gw_acc[...]
 
 
 def spread(info_ref, acc, scale, mine_ref, other_ref, from_col, to_col, count):
@@ -589,61 +617,14 @@
             ).astype(low)
 
 
-def blocks(grad_ref, acc, scale, owners, to_col, count):
-    rows = grad_ref.shape[1]
+def put_blocks(stage, acc, scale, owners, to_col, count):
+    rows = stage.shape[1]
     for number, owner in enumerate(owners):
         for index in range(8):
-            grad_ref[2 * index + owner, :, to_col : to_col + count] = (
+            stage[2 * index + owner, :, to_col : to_col + count] = (
                 acc[index * rows : (index + 1) * rows, number * count : (number + 1) * count]
                 * scale
             ).astype(low)
-
-
-def mlp_kernel(first, begin, scale, info_ref, h_ref, ht_ref, gy_ref, gyt_ref, out_in_ref, *refs):
-    if not first:
-        gh_in_ref, *refs = refs
-    shards, *refs = refs if first else [refs[0], *refs[2:]]
-    out_ref, gh_ref, grad_ref, up_ref, down_ref, up_acc, down_acc, sems = refs
-    step = pl.program_id(0)
-    chunk = up_ref.shape[1] // 2
-
-    @pl.when(step == 0)
-    def _():
-        run_all(
-            load_shards([(shards, m, begin, chunk, m * chunk) for m in range(2)], up_ref, sems)
-            + load_shards(
-                [(shards, m, begin + chunk, chunk, m * chunk) for m in range(2)],
-                down_ref,
-                sems.at[pl.ds(2, 2)],
-            )
-        )
-
-    root = math.sqrt(2.0 / math.pi)
-    t = dot(h_ref[...], up_ref[...])
-    square = t * t
-    gate = 0.5 + 0.5 * jnp.tanh(t * (root + (root * 0.044715) * square))
-    act = t * gate
-    slope = gate + 2.0 * act * (1.0 - gate) * (root + (3.0 * root * 0.044715) * square)
-    act = act.astype(low)
-    grad = (dot(gy_ref[...], down_ref[...]) * slope).astype(low)
-    out_ref[...] = out_in_ref[...] + dot(act, down_ref[...], 1, 1)
-    back = dot(grad, up_ref[...], 1, 1)
-    gh_ref[...] = back if first else gh_in_ref[...] + back
-
-    @pl.when(step == 0)
-    def _():
-        up_acc[...] = dot(ht_ref[...], grad)
-        down_acc[...] = dot(gyt_ref[...], act)
-
-    @pl.when(step > 0)
-    def _():
-        up_acc[...] += dot(ht_ref[...], grad)
-        down_acc[...] += dot(gyt_ref[...], act)
-
-    @pl.when(step == pl.num_programs(0) - 1)
-    def _():
-        blocks(grad_ref, up_acc, scale, (0, 1), 0, chunk)
-        blocks(grad_ref, down_acc, scale, (0, 1), chunk, chunk)
 
 
 def norm_back(values, grad, gain):
@@ -659,27 +640,217 @@
     return result, normed
 
 
-def second_norm_kernel(
-    scale, info_ref, x2_ref, gh_ref, gy_ref, y_ref, valid_ref, o_mine_ref, o_got_ref, gain_ref, *refs
+def gelu_parts(t):
+    root = math.sqrt(2.0 / math.pi)
+    square = t * t
+    gate = 0.5 + 0.5 * jnp.tanh(t * (root + (root * 0.044715) * square))
+    act = t * gate
+    slope = gate + 2.0 * act * (1.0 - gate) * (root + (3.0 * root * 0.044715) * square)
+    return act, slope
+
+
+def middle_kernel(
+    scale,
+    chunks,
+    info_ref,
+    o_mine_ref,
+    o_got_ref,
+    mine_ref,
+    got_ref,
+    gy_ref,
+    valid_ref,
+    gain_ref,
+    bias_ref,
+    shards,
+    keep_near_ref,
+    keep_far_ref,
+    send_near_ref,
+    send_far_ref,
+    gx_ref,
+    go_mine_ref,
+    go_send_ref,
+    sums_ref,
+    grads,
+    out_grads,
+    x2_all,
+    h_all,
+    ht_all,
+    gy_all,
+    gyt_all,
+    out_all,
+    gh_all,
+    up_both,
+    down_both,
+    up_acc,
+    down_acc,
+    act_all,
+    grad_all,
+    wo_ref,
+    wo_acc,
+    stage,
+    stage_out,
+    weight_sems,
+    stage_sem,
 ):
-    shards, refs = refs[0], refs[2:]
-    keep_ref, send_ref, gx_ref, go_mine_ref, go_send_ref, grad_ref, sums_ref = refs[:7]
-    w_ref, acc, sems = refs[7:]
+    phase = pl.program_id(0)
+    r = pl.program_id(1)
+    last = pl.num_programs(1) - 1
+    cols = o_mine_ref.shape[3]
+    part = o_mine_ref.shape[2]
+    chunk = up_both.shape[2] // 2
     c = info_ref[1]
-    cols = o_mine_ref.shape[3]
+    first_half = info_ref[0] == 0
+
+    def weight_copies(f, slot):
+        begin = cols + f * 2 * chunk
+        sems = weight_sems.at[slot]
+        return load_shards(
+            [(shards, m, begin, chunk, m * chunk) for m in range(2)], up_both.at[slot], sems
+        ) + load_shards(
+            [(shards, m, begin + chunk, chunk, m * chunk) for m in range(2)],
+            down_both.at[slot],
+            sems.at[pl.ds(2, 2)],
+        )
+
+    def stage_copy(f):
+        return pltpu.make_async_copy(
+            stage, grads.at[:, :, pl.ds(f * 2 * chunk, 2 * chunk)], stage_sem.at[0]
+        )
+
+    def both_heads():
+        return jnp.concatenate(
+            [o_mine_ref[0].reshape(2 * part, cols), o_got_ref[0].reshape(2 * part, cols)], axis=1
+        )
+
+    @pl.when((phase == 0) & (r == 0))
+    def _():
+        copies = load_shards(
+            [(shards, c, 0, cols, 0), (shards, 1 - c, 0, cols, cols)], wo_ref, weight_sems.at[1]
+        )
+        run_all(copies)
+        for copy in weight_copies(0, 0):
+            copy.start()
+        sums_ref[...] = jnp.zeros_like(sums_ref)
+
+    @pl.when(phase == 0)
+    def _():
+        x = jnp.concatenate(
+            [
+                jnp.where(first_half, mine_ref[0], got_ref[0]),
+                jnp.where(first_half, got_ref[0], mine_ref[0]),
+            ],
+            axis=0,
+        ).astype(wide)
+        x2 = x + dot(both_heads(), wo_ref[...], 1, 1)
+        x2_all[r] = x2
+        centered = x2 - jnp.mean(x2, axis=1, keepdims=True)
+        variance = jnp.mean(centered * centered, axis=1, keepdims=True)
+        h = (centered * lax.rsqrt(variance + norm_eps) * gain_ref[...] + bias_ref[...]).astype(low)
+        h_all[r] = h
+        ht_all[r] = jnp.transpose(h)
+        gy = gy_ref[...]
+        gy_all[r] = gy
+        gyt_all[r] = jnp.transpose(gy)
+
+    def mlp_step(f):
+        slot = f % 2
+
+        @pl.when(r == 0)
+        def _():
+            for copy in weight_copies(f, slot):
+                copy.wait()
+            if f + 1 < chunks:
+                for copy in weight_copies(f + 1, 1 - slot):
+                    copy.start()
+
+        up_ref = up_both.at[slot]
+        down_ref = down_both.at[slot]
+        h = h_all[r]
+        gy = gy_all[r]
+        size = 512
+        for at in range(0, 2 * chunk, size):
+            act, slope = gelu_parts(dot(h, up_ref[:, at : at + size]))
+            act_all[:, at : at + size] = act.astype(low)
+            grad_all[:, at : at + size] = (dot(gy, down_ref[:, at : at + size]) * slope).astype(low)
+        base = x2_all[r] if f == 0 else out_all[r]
+        out_all[r] = base + dot(act_all[...], down_ref[...], 1, 1)
+        back = dot(grad_all[...], up_ref[...], 1, 1)
+        gh_all[r] = back if f == 0 else gh_all[r] + back
+
+        @pl.when(r == 0)
+        def _():
+            up_acc[...] = dot(ht_all[r], grad_all[...])
+            down_acc[...] = dot(gyt_all[r], act_all[...])
+
+        @pl.when(r > 0)
+        def _():
+            up_acc[...] += dot(ht_all[r], grad_all[...])
+            down_acc[...] += dot(gyt_all[r], act_all[...])
+
+        @pl.when(r == last)
+        def _():
+            if f > 0:
+                stage_copy(f - 1).wait()
+            put_blocks(stage, up_acc, scale, (0, 1), 0, chunk)
+            put_blocks(stage, down_acc, scale, (0, 1), chunk, chunk)
+            stage_copy(f).start()
+
+    for f in range(chunks):
+        pl.when(phase == f + 1)(partial(mlp_step, f))
+
+    @pl.when(phase == chunks + 1)
+    def _():
+        out = (out_all[r] * valid_ref[...][:, :1]).astype(low)
+        keep = jnp.where(first_half, out[:part], out[part:])
+        send = jnp.where(first_half, out[part:], out[:part])
+        keep_near_ref[0] = jnp.where(c == 0, keep[:, :cols], keep[:, cols:])
+        keep_far_ref[0] = jnp.where(c == 0, keep[:, cols:], keep[:, :cols])
+        send_near_ref[0] = jnp.where(c == 0, send[:, :cols], send[:, cols:])
+        send_far_ref[0] = jnp.where(c == 0, send[:, cols:], send[:, :cols])
+        gh = gh_all[r]
+        back, normed = norm_back(x2_all[r], gh, gain_ref[...])
+        gx = gy_all[r].astype(wide) + back
+        gx_ref[...] = gx
+        gx_low = gx.astype(low)
+        go = dot(gx_low, wo_ref[...]).astype(low)
+        go_mine_ref[0] = go[:, :cols].reshape(2, part, cols)
+        go_send_ref[0] = go[:, cols:].reshape(2, part, cols)
+        turned = jnp.transpose(gx_low)
+        sums_ref[0:1, :] += jnp.sum(gh * normed, axis=0, keepdims=True)
+        sums_ref[1:2, :] += jnp.sum(gh, axis=0, keepdims=True)
+        product = dot(turned, both_heads())
+
+        @pl.when(r == 0)
+        def _():
+            wo_acc[...] = product
+
+        @pl.when(r > 0)
+        def _():
+            wo_acc[...] += product
+
+        @pl.when(r == last)
+        def _():
+            stage_copy(chunks - 1).wait()
+            rows = stage_out.shape[3]
+            for side in range(2):
+                for index in range(8):
+                    place = pl.multiple_of(info_ref[2 + index] * rows, rows)
+                    stage_out[side, index % 2, index // 2] = (
+                        wo_acc[pl.ds(place, rows), side * cols : (side + 1) * cols] * scale
+                    ).astype(low)
+            copy = pltpu.make_async_copy(stage_out, out_grads, stage_sem.at[1])
+            copy.start()
+            copy.wait()
+
+
+def first_norm_kernel(
+    info_ref, mine_ref, got_ref, a_ref, b_ref, gx2_ref, gain_ref, keep_ref, send_ref, sums_ref
+):
     half = pl.program_id(1)
-    start = (pl.program_id(0) == 0) & (half == 0)
-    end = (pl.program_id(0) == pl.num_programs(0) - 1) & (half == 1)
-
-    @pl.when(start)
-    def _():
-        run_all(
-            load_shards([(shards, c, 0, cols, 0), (shards, 1 - c, 0, cols, cols)], w_ref, sems)
-        )
-        sums_ref[...] = jnp.zeros_like(sums_ref)
-        acc[...] = jnp.zeros_like(acc)
-
-    out = (y_ref[...] * valid_ref[...][:, :1]).astype(low)
+    x = jnp.where(half == info_ref[0], mine_ref[0], got_ref[0]).astype(wide)
+    gh = a_ref[0, 0].astype(wide) + b_ref[0, 0].astype(wide)
+    back, normed = norm_back(x, gh, gain_ref[...])
+    out = (gx2_ref[...] + back).astype(low)
 
     @pl.when(half == info_ref[0])
     def _():
@@ -689,85 +860,28 @@
     def _():
         send_ref[0] = out
 
-    gh = gh_ref[...]
-    back, normed = norm_back(x2_ref[...], gh, gain_ref[...])
-    gx = gy_ref[...].astype(wide) + back
-    gx_ref[...] = gx
-    go = dot(gx.astype(low), w_ref[...]).astype(low)
-    go_mine_ref[0, 0] = go[:, :cols]
-    go_send_ref[0, 0] = go[:, cols:]
-    turned = jnp.transpose(gx).astype(low)
+    @pl.when((pl.program_id(0) == 0) & (half == 0))
+    def _():
+        sums_ref[...] = jnp.zeros_like(sums_ref)
+
     sums_ref[0:1, :] += jnp.sum(gh * normed, axis=0, keepdims=True)
     sums_ref[1:2, :] += jnp.sum(gh, axis=0, keepdims=True)
-    acc[...] += dot(turned, jnp.concatenate([o_mine_ref[0, 0], o_got_ref[0, 0]], axis=1))
-
-    @pl.when(end)
-    def _():
-        blocks(grad_ref, acc, scale, (c, 1 - c), 0, cols)
-
-
-def gw_in_kernel(scale, info_ref, ht_ref, *refs):
-    grads, (out_ref, acc) = refs[:-2], refs[-2:]
-    step = pl.program_id(0)
-
-    def add(grad_ref):
-        @pl.when(step == 0)
-        def _():
-            acc[...] = dot(ht_ref[...], grad_ref[0])
-
-        @pl.when(step > 0)
-        def _():
-            acc[...] += dot(ht_ref[...], grad_ref[0])
-
-    if len(grads) == 1:
-        add(grads[0])
-    else:
-        for index, grad_ref in enumerate(grads):
-            pl.when(step == index)(partial(add, grad_ref))
-
-    @pl.when(step == pl.num_programs(0) - 1)
-    def _():
-        spread(info_ref, acc, scale, out_ref, None, 0, 0, out_ref.shape[3])
-
-
-def gh1_kernel(info_ref, *refs):
-    grads, pieces = refs[:3], refs[3:11]
-    mine_ref, send_ref, w_ref, sems = refs[11:]
-
-    @pl.when(pl.program_id(0) == 0)
-    def _():
-        run_all(load_pieces(info_ref, [(pieces, 0, w_ref.shape[1], 0)], w_ref, sems))
-
-    both = dot(jnp.concatenate([ref[0] for ref in grads], axis=1), w_ref[...], 1, 1).astype(low)
-    part = mine_ref.shape[1]
-    near = info_ref[1] == 0
-    mine_ref[0] = jnp.where(near, both[:part], both[part:])
-    send_ref[0] = jnp.where(near, both[part:], both[:part])
-
-
-def first_norm_kernel(
-    info_ref, mine_ref, got_ref, a_ref, b_ref, gx2_ref, gain_ref, keep_ref, send_ref, sums_ref
-):
-    half = pl.program_id(0)
-    x = jnp.where(half == info_ref[0], mine_ref[0], got_ref[0]).astype(wide)
-    gh = a_ref[0].astype(wide) + b_ref[0].astype(wide)
-    back, normed = norm_back(x, gh, gain_ref[...])
-    out = (gx2_ref[...] + back).astype(low)
-
-    @pl.when(half == info_ref[0])
-    def _():
-        keep_ref[...] = out
-
-    @pl.when(half != info_ref[0])
-    def _():
-        send_ref[...] = out
-
-    @pl.when(half == 0)
-    def _():
-        sums_ref[...] = jnp.zeros_like(sums_ref)
-
-    sums_ref[0:1, :] += jnp.sum(gh * normed, axis=0, keepdims=True)
-    sums_ref[1:2, :] += jnp.sum(gh, axis=0, keepdims=True)
+
+
+def place_kernel(plan, seqs, info_ref, *refs):
+    sources, (out_ref, sems) = refs[: len(plan)], refs[len(plan) :]
+    y, c = info_ref[0], info_ref[1]
+    copies = []
+    for number, (source, (own_y, own_c, begin)) in enumerate(zip(sources, plan)):
+        at = seqs * (y if own_y else 1 - y) + begin
+        copies.append(
+            pltpu.make_async_copy(
+                source,
+                out_ref.at[pl.ds(at, source.shape[0]), c if own_c else 1 - c],
+                sems.at[number],
+            )
+        )
+    run_all(copies)
 
 
 def shape_of(dims, kind=low):
@@ -921,7 +1035,7 @@
         )
     )
     small = [piece[shard_rows : shard_rows + 8, :shard_rows] for piece in in_pieces]
-    chunk = 512
+    chunk = hidden_chunk
     chunks = hidden // chunk
     up_low = w_up.astype(low)
     down_low = jnp.transpose(w_down.astype(low))
@@ -933,9 +1047,7 @@
     def gather_shards(parts):
         return lax.all_gather(jnp.concatenate(parts, axis=1), ("dp", "mlp"), axis=0)
 
-    split = 5
-    shards_a = gather_shards(parts[:split])
-    shards_b = gather_shards(parts[split:])
+    shards = gather_shards(parts)
 
     order = (places[None, :] == jnp.arange(8)[:, None]).astype(low)
     small = jnp.einsum("nr,rkw->knw", order, jnp.stack(small), preferred_element_type=wide)
@@ -964,13 +1076,14 @@
     side = jnp.where(lanes < 6, mask_weight, jnp.where(lanes == 6, -6.0 * mask_weight, 0.0))
     side = side.astype(low)[None]
     means = jnp.where(lanes[:, None] // 64 == lanes[None] // 64, 1.0 / 64, 0.0).astype(low)
+    means = jnp.concatenate([means, means])
     anywhere = pl.BlockSpec(memory_space=pl.ANY)
 
     def whole(dims):
         return pl.BlockSpec(dims, lambda *ids: (0,) * len(dims))
 
-    def call(kernel, grid, in_specs, out_specs, out_shape, scratch, name, scalars, pins=(), share=1, alias=None):
-        work = micros[name] * 1150000000 // share
+    def call(kernel, grid, in_specs, out_specs, out_shape, scratch, name, scalars, pins=(), share=1, vmem=vmem_bytes):
+        work = int(micros[name] * 1150000000 / share)
         ends = scalars + len(in_specs)
 
         def unpinned(*refs):
@@ -986,8 +1099,7 @@
                 scratch_shapes=scratch,
             ),
             out_shape=out_shape,
-            compiler_params=params(len(grid)),
-            input_output_aliases=alias or {},
+            compiler_params=params(len(grid), vmem),
             cost_estimate=pl.CostEstimate(flops=work, bytes_accessed=1000000, transcendentals=0),
             name=name,
         )
@@ -997,21 +1109,21 @@
     one_seq = pl.BlockSpec((1, part, width), lambda s, j, *_: (s, 0, 0))
     projected, rates, h1t = call(
         qkv_kernel,
-        (seqs, 4),
+        (seqs, 2),
         [
-            pl.BlockSpec((1, part, width), lambda s, j, info: (seqs * info[0] + s, j % 2, 0)),
+            pl.BlockSpec((1, half, width), lambda s, j, info: (seqs * info[0] + s, 0, 0)),
             one_seq,
             one_seq,
             whole((1, width)),
             whole((1, width)),
             whole((1, 2 * cols)),
-            whole((128, 128)),
+            whole((256, 128)),
         ]
         + [anywhere] * 8,
         [
-            pl.BlockSpec((1, part, 3 * cols), lambda s, j, *_: (s, j, 0)),
-            pl.BlockSpec((1, part, 2 * cols), lambda s, j, *_: (s, j, 0)),
-            pl.BlockSpec((width, part), lambda s, j, *_: (0, 4 * s + j)),
+            pl.BlockSpec((1, half, 3 * cols), lambda s, j, *_: (s, j, 0)),
+            pl.BlockSpec((1, half, 2 * cols), lambda s, j, *_: (s, j, 0)),
+            pl.BlockSpec((width, half), lambda s, j, *_: (0, 2 * s + j)),
         ],
         [
             shape_of((seqs, length, 3 * cols)),
@@ -1022,16 +1134,14 @@
         "qkv",
         1,
     )(info, turned, got, far, gains[:1], biases[:1], head_scaled, means, *in_pieces)
-    split_seq = pl.BlockSpec((1, 2, part, 128), lambda s, p, *_: (s, 0, 0, p))
+    def per_seq(*dims, base=0):
+        return pl.BlockSpec((1,) + dims, lambda s, *_: (s + base,) + (0,) * len(dims))
+
     o_mine, o_send, inverse = call(
         attn_fwd_kernel,
-        (seqs, pairs),
-        [
-            pl.BlockSpec((1, length, 384), lambda s, p, *_: (s, 0, p)),
-            pl.BlockSpec((1, length, 128), lambda s, p, *_: (s, 0, 0)),
-            whole((1, 128)),
-        ],
-        [split_seq, split_seq, pl.BlockSpec((1, length, 128), lambda s, p, *_: (s, 0, p))],
+        (seqs,),
+        [per_seq(length, 3 * cols), per_seq(length, 128), whole((1, 128))],
+        [per_seq(2, part, cols), per_seq(2, part, cols), per_seq(length, cols)],
         [shape_of((seqs, 2, part, cols))] * 2 + [shape_of((seqs, length, cols), wide)],
         [],
         "attn_fwd",
@@ -1039,33 +1149,86 @@
     )(info, starts, kinds, projected, aug, side)
 
     o_got = swap(o_send, "mlp")
-    mine_spec = pl.BlockSpec((1, part, width), lambda s, h, info: (seqs * info[0] + s, info[1], 0))
-    got_spec = pl.BlockSpec((1, part, width), lambda s, h, *_: (s, 0, 0))
-    rows_spec = pl.BlockSpec((part, width), lambda s, h, *_: (2 * s + h, 0))
-    turned_spec = pl.BlockSpec((width, part), lambda s, h, *_: (0, 2 * s + h))
-    part_spec = pl.BlockSpec((1, 1, part, cols), lambda s, h, *_: (s, h, 0, 0))
-    x2, h2, h2t, gyt = call(
-        attn_out_kernel,
-        (seqs, 2),
-        [part_spec, part_spec, mine_spec, got_spec, rows_spec, whole((1, width)), whole((1, width))]
-        + [anywhere],
-        [rows_spec, rows_spec, turned_spec, turned_spec],
+    seq_of = seqs - 1
+    final = chunks + 1
+
+    def at_ends(p, r):
+        return jnp.where((p == 0) | (p == final), r, seq_of)
+
+    def at_start(p, r):
+        return jnp.where(p == 0, r, seq_of)
+
+    def at_final(p, r):
+        return jnp.where(p == final, r, 0)
+
+    heads_spec = pl.BlockSpec((1, 2, part, cols), lambda p, r, *_: (at_ends(p, r), 0, 0, 0))
+    moved_spec = pl.BlockSpec((1, part, cols), lambda p, r, *_: (at_final(p, r), 0, 0))
+    heads_out = pl.BlockSpec((1, 2, part, cols), lambda p, r, *_: (at_final(p, r), 0, 0, 0))
+    by_seq_bf = pltpu.VMEM((seqs, half, width), low)
+    by_seq_turned = pltpu.VMEM((seqs, width, half), low)
+    by_seq_wide = pltpu.VMEM((seqs, half, width), wide)
+    grad_shape = (16, shard_rows, 2 * hidden)
+    keep_near, keep_far, send_near, send_far, gx2, go_mine, go_send, second_sums, grads, out_grads = call(
+        partial(middle_kernel, scale, chunks),
+        (chunks + 2, seqs),
         [
+            heads_spec,
+            heads_spec,
+            pl.BlockSpec(
+                (1, part, width), lambda p, r, info: (seqs * info[0] + at_start(p, r), info[1], 0)
+            ),
+            pl.BlockSpec((1, part, width), lambda p, r, *_: (at_start(p, r), 0, 0)),
+            pl.BlockSpec((half, width), lambda p, r, *_: (at_start(p, r), 0)),
+            pl.BlockSpec((half, 128), lambda p, r, *_: (at_final(p, r), 0)),
+            whole((1, width)),
+            whole((1, width)),
+            anywhere,
+        ],
+        [
+            moved_spec,
+            moved_spec,
+            moved_spec,
+            moved_spec,
+            pl.BlockSpec((half, width), lambda p, r, *_: (at_final(p, r), 0)),
+            heads_out,
+            heads_out,
+            whole((8, width)),
+            anywhere,
+            anywhere,
+        ],
+        [
+            shape_of((seqs, part, cols)),
+            shape_of((seqs, part, cols)),
+            shape_of((seqs, part, cols)),
+            shape_of((seqs, part, cols)),
             shape_of((own_rows, width), wide),
-            shape_of((own_rows, width)),
-            shape_of((width, own_rows)),
-            shape_of((width, own_rows)),
+            shape_of((seqs, 2, part, cols)),
+            shape_of((seqs, 2, part, cols)),
+            shape_of((8, width), wide),
+            shape_of(grad_shape),
+            shape_of((2, 2, 4, shard_rows, cols)),
         ],
-        [pltpu.VMEM((width, width), low), piece_sems],
-        "attn_out",
+        [by_seq_wide, by_seq_bf, by_seq_turned, by_seq_bf, by_seq_turned, by_seq_wide, by_seq_wide]
+        + [pltpu.VMEM((2, width, 2 * chunk), low)] * 2
+        + [pltpu.VMEM((width, 2 * chunk), wide)] * 2
+        + [pltpu.VMEM((half, 2 * chunk), low)] * 2
+        + [
+            pltpu.VMEM((width, width), low),
+            pltpu.VMEM((width, width), wide),
+            pltpu.VMEM((16, shard_rows, 2 * chunk), low),
+            pltpu.VMEM((2, 2, 4, shard_rows, cols), low),
+            pltpu.SemaphoreType.DMA((2, 4, 8)),
+            pltpu.SemaphoreType.DMA((2,)),
+        ],
+        "middle",
         1,
-    )(info, o_mine, o_got, turned, got, gy, gains[1:], biases[1:], shards_a)
-
-    block = half
-    block_spec = pl.BlockSpec((block, width), lambda i, *_: (i, 0))
-    block_turned = pl.BlockSpec((width, block), lambda i, *_: (0, i))
-    total, gh = x2, None
-    sums = []
+        vmem=62 * 1024 * 1024,
+    )(info, o_mine, o_got, turned, got, gy, valid, gains[1:], biases[1:], shards)
+    go_got = swap(go_send, "mlp")
+    got_near = swap(send_near, "seq")
+    got_far = swap(send_far, "seq")
+    scattered = lax.psum_scatter(grads, ("dp", "mlp"), scatter_dimension=0, tiled=True)[0]
+    sums = [Reduce(out_grads[0], out_grads[1])]
 
     def advance():
         pins = []
@@ -1074,191 +1237,116 @@
             one.advance()
         return pins
 
-    grads = None
-    grad_shape = shape_of((16, shard_rows, cols + 2 * hidden))
-    for f in range(chunks):
-        first = f == 0
-        carried = [total] if first else [total, gh]
-        begin = cols + f * 2 * chunk
-        source = shards_a
-        if begin >= shards_a.shape[2]:
-            source, begin = shards_b, begin - shards_a.shape[2]
-        extra = [] if first else [grads]
-        total, gh, grads = call(
-            partial(mlp_kernel, first, begin, scale),
-            (seqs,),
-            [block_spec, block_turned, block_spec, block_turned]
-            + [block_spec] * len(carried)
-            + [anywhere] * (1 + len(extra)),
-            [block_spec] * 2
-            + [pl.BlockSpec((16, shard_rows, 2 * chunk), lambda *_, f=f: (0, 0, f))],
-            [shape_of((own_rows, width), wide)] * 2 + [grad_shape],
-            [pltpu.VMEM((width, 2 * chunk), low)] * 2
-            + [pltpu.VMEM((width, 2 * chunk), wide)] * 2
-            + [piece_sems],
-            "mlp",
-            1,
-            alias={} if first else {8: 2},
-        )(info, h2, h2t, gy, gyt, *carried, source, *extra)
-
-    last_block = 2 * hidden // cols
-    out_keep, out_send, gx2, go_mine, go_send, grads, second_sums = call(
-        partial(second_norm_kernel, scale),
-        (seqs, 2),
-        [
-            rows_spec,
-            rows_spec,
-            rows_spec,
-            rows_spec,
-            pl.BlockSpec((part, 128), lambda s, h, *_: (2 * s + h, 0)),
-            part_spec,
-            part_spec,
-            whole((1, width)),
-        ]
-        + [anywhere] * 2,
-        [got_spec, got_spec, rows_spec, part_spec, part_spec]
-        + [pl.BlockSpec((16, shard_rows, cols), lambda *_: (0, 0, last_block))]
-        + [whole((8, width))],
-        [shape_of((seqs, part, width))] * 2
-        + [shape_of((own_rows, width), wide)]
-        + [shape_of((seqs, 2, part, cols))] * 2
-        + [grad_shape]
-        + [shape_of((8, width), wide)],
-        [pltpu.VMEM((width, width), low), pltpu.VMEM((width, width), wide), piece_sems],
-        "second_norm",
-        1,
-        alias={10: 5},
-    )(info, x2, gh, gy, total, valid, o_mine, o_got, gains[1:], shards_a, grads)
-    go_got = swap(go_send, "mlp")
-    out_swapped = swap(out_send, "seq")
-    scattered = lax.psum_scatter(grads, ("dp", "mlp"), scatter_dimension=0, tiled=True)[0]
-
-    def attention_back(pair, base, count, pins):
-        split_pair = pl.BlockSpec((1, 2, part, 128), lambda s, *_: (s + base, 0, 0, pair))
-        columns = pl.BlockSpec((1, length, 128), lambda s, *_: (s + base, 0, pair))
+
+    def attention_back(base, count, partial_sum, pins):
+        first = partial_sum is None
+        final = base + count == seqs
+        shares = (2, 4, shard_rows, 3 * cols)
+        carried = [] if first else [partial_sum]
         return call(
-            partial(attn_bwd_kernel, base),
+            partial(attn_bwd_kernel, base, scale, first, final),
             (count,),
-            [pl.BlockSpec((1, length, 384), lambda s, *_: (s + base, 0, pair))]
-            + [split_pair] * 4
+            [per_seq(length, 3 * cols, base=base)]
+            + [per_seq(2, part, cols, base=base)] * 4
             + [
-                columns,
-                pl.BlockSpec((1, length, 256), lambda s, *_: (s + base, 0, pair)),
-                pl.BlockSpec((1, length, 128), lambda s, *_: (s + base, 0, 0)),
+                per_seq(length, cols, base=base),
+                per_seq(length, 2 * cols, base=base),
+                per_seq(length, 128, base=base),
                 whole((1, 128)),
-                pl.BlockSpec((1, 256), lambda s, *_: (0, pair)),
-                whole((128, 128)),
+                whole((1, 2 * cols)),
+                whole((256, 128)),
+                pl.BlockSpec((width, length), lambda s, *_: (0, s + base)),
+            ]
+            + [anywhere] * 8
+            + [whole((width, 3 * cols))] * len(carried),
+            [per_seq(2, part, width)] * 2
+            + [whole(shares if final else (width, 3 * cols)), whole((8, 2 * cols))],
+            [shape_of((count, 2, part, width))] * 2
+            + [shape_of(shares) if final else shape_of((width, 3 * cols), wide)]
+            + [shape_of((8, 2 * cols), wide)],
+            [pltpu.VMEM((length, cols), wide)] * 3
+            + [
+                pltpu.VMEM((length, 3 * cols), low),
+                pltpu.VMEM((width, 3 * cols), wide),
+                pltpu.VMEM((width, 3 * cols), low),
+                piece_sems,
             ],
-            [pl.BlockSpec((1, length, 384), lambda s, *_: (s, 0, 0)), whole((8, 128))],
-            [shape_of((count, length, 384)), shape_of((8, 128), wide)],
-            [pltpu.VMEM((length, 128), wide)] * 3,
             "attn_bwd",
             3,
             pins,
-            3 * seqs // count,
+            seqs / count,
         )(
             info, starts, kinds, projected, go_mine, go_got, o_mine, o_send, inverse, rates,
-            aug, side, head_gains, means,
+            aug, side, head_gains, means, h1t, *in_pieces, *carried,
         )
 
-    def input_weights(grads):
-        if len(grads) == 1:
-            specs = [pl.BlockSpec((1, length, 384), lambda s, *_: (s, 0, 0))]
-        else:
-            specs = [whole((1, length, 384))] * len(grads)
-        shares = (2, 4, shard_rows, 384)
-        return call(
-            partial(gw_in_kernel, scale),
-            (seqs,),
-            [pl.BlockSpec((width, length), lambda s, *_: (0, s))] + specs,
-            whole(shares),
-            shape_of(shares),
-            [pltpu.VMEM((width, 384), wide)],
-            "gw_in",
-            1,
-            (),
-            3,
-        )(info, h1t, *grads)
-
-    def first_grads(seq, grads, pins):
-        return call(
-            gh1_kernel,
-            (2,),
-            [
-                pl.BlockSpec((1, half, 384), lambda h, *_, at=seq % grad.shape[0]: (at, h, 0))
-                for grad in grads
-            ]
-            + [anywhere] * 8,
-            [pl.BlockSpec((1, part, width), lambda h, *_: (h, 0, 0))] * 2,
-            [shape_of((2, part, width))] * 2,
-            [pltpu.VMEM((width, 3 * cols), low), piece_sems],
-            "gh1",
-            1,
-            pins,
-            3,
-        )(info, *grads, *in_pieces)
-
-    def first_back(seq, mine, got_part, pins):
-        halves = pl.BlockSpec((1, part, width), lambda h, *_: (h, 0, 0))
+    def first_back(base, count, mine, got_part, pins):
+        here = pl.BlockSpec((1, 1, part, width), lambda s, h, *_: (s, h, 0, 0))
+        moved = pl.BlockSpec((1, part, width), lambda s, h, *_: (s, 0, 0))
         return call(
             first_norm_kernel,
-            (2,),
+            (count, 2),
             [
-                pl.BlockSpec((1, part, width), lambda h, info: (seqs * info[0] + seq, info[1], 0)),
-                pl.BlockSpec((1, part, width), lambda h, *_: (seq, 0, 0)),
-                halves,
-                halves,
-                pl.BlockSpec((part, width), lambda h, *_: (2 * seq + h, 0)),
+                pl.BlockSpec(
+                    (1, part, width), lambda s, h, info: (seqs * info[0] + s + base, info[1], 0)
+                ),
+                pl.BlockSpec((1, part, width), lambda s, h, *_: (s + base, 0, 0)),
+                here,
+                here,
+                pl.BlockSpec((part, width), lambda s, h, *_: (2 * (s + base) + h, 0)),
                 whole((1, width)),
             ],
-            [whole((part, width))] * 2 + [whole((8, width))],
-            [shape_of((part, width))] * 2 + [shape_of((8, width), wide)],
+            [moved, moved, whole((8, width))],
+            [shape_of((count, part, width))] * 2 + [shape_of((8, width), wide)],
             [],
             "first_norm",
             1,
             pins,
-            3,
+            seqs / count,
         )(info, turned, got, mine, got_part, gx2, gains[:1])
 
-    def finish_out():
-        out_six = in_order(y, out_keep, out_swapped, 0).reshape(seqs_all, part, 2, cols)
-        out_got = swap(pick(out_six, 1 - c, 2), "mlp")
-        return jnp.transpose(in_order(c, pick(out_six, c, 2), out_got, 1), (1, 0, 2))
-
-    full_grads, gain_sums, in_sums = [], [], []
-    out = None
-    for pair in range(pairs):
-        pins = advance()
-        if pair == 1:
-            pins.append(out_swapped)
-            out = finish_out()
-        if pair == 2:
-            pins.append(out)
-        grads, gain_sum = attention_back(pair, 0, seqs, pins)
-        full_grads.append(grads)
-        gain_sums.append(gain_sum)
-        if pair < pairs - 1:
-            in_sums.append(Reduce(input_weights([grads])))
-            sums.append(in_sums[-1])
-    halves_sent, backs = [], []
-    for seq in range(seqs):
-        mine, send = first_grads(seq, full_grads, ())
-        halves_sent.append((mine, swap(send, "mlp")))
-        if seq:
-            backs.append(first_back(seq - 1, *halves_sent[seq - 1], ()))
-    in_sums.append(Reduce(input_weights([grads])))
-    sums.append(in_sums[-1])
-    advance()
-    backs.append(first_back(seqs - 1, *halves_sent[seqs - 1], ()))
-    first_sums = sum(back[2] for back in backs)
-
-    mine_parts, other_parts = [], []
-    for keep, send, _ in backs:
-        got_rows = swap(send, "seq")
-        mine_parts.append(in_order(c, keep, swap(keep, "mlp"), 0))
-        other_parts.append(in_order(c, got_rows, swap(got_rows, "mlp"), 0))
-    grad_patches = in_order(y, jnp.stack(mine_parts), jnp.stack(other_parts), 0)
-    grad_patches = jnp.transpose(grad_patches, (1, 0, 2))
+    def place(sources, plan, feature_count):
+        return call(
+            partial(place_kernel, plan, seqs),
+            (1,),
+            [anywhere] * len(plan),
+            whole((seqs_all, 2, part, feature_count)),
+            shape_of((seqs_all, 2, part, feature_count)),
+            [pltpu.SemaphoreType.DMA((len(plan),))],
+            "place",
+            1,
+        )(info, *sources)
+
+    early = seqs - 1
+    pins = advance()
+    mine_a, send_a, partial_sum, head_sums_a = attention_back(0, early, None, pins)
+    far_a = swap(send_a, "mlp")
+    keep_a, give_a, norm_sums_a = first_back(0, early, mine_a, far_a, ())
+    got_a = swap(give_a, "seq")
+    keep_core_a = swap(keep_a, "mlp")
+    keep_core, got_core = swap(keep_far, "mlp"), swap(got_far, "mlp")
+    pins = advance() + [got_near, got_far, keep_a]
+    mine_b, send_b, gw_in, head_sums_b = attention_back(early, 1, partial_sum, pins)
+    far_b = swap(send_b, "mlp")
+    in_sums = Reduce(gw_in)
+    sums.append(in_sums)
+    pins = advance() + [got_a, keep_core_a]
+    keep_b, give_b, norm_sums_b = first_back(early, 1, mine_b, far_b, pins)
+    first_sums = norm_sums_a + norm_sums_b
+    head_sums = head_sums_a + head_sums_b
+
+    plan = [(True, True, 0), (True, False, 0), (False, True, 0), (False, False, 0)]
+    out = place([keep_near, keep_core, got_near, got_core], plan, cols)
+    out = jnp.transpose(out.reshape(seqs_all, half, cols), (1, 0, 2))
+    got_b = swap(give_b, "seq")
+    late = [(own_y, own_c, early) for own_y, own_c, _ in plan]
+    grad_patches = place(
+        [keep_a, keep_core_a, got_a, swap(got_a, "mlp")]
+        + [keep_b, swap(keep_b, "mlp"), got_b, swap(got_b, "mlp")],
+        plan + late,
+        width,
+    )
+    grad_patches = jnp.transpose(grad_patches.reshape(seqs_all, half, width), (1, 0, 2))
 
     scattered = scattered.astype(wide) + swap(scattered, "seq").astype(wide)
     gw_up = jnp.concatenate(
@@ -1267,13 +1355,13 @@
     gw_down = jnp.concatenate(
         [scattered[:, (2 * f + 1) * chunk : (2 * f + 2) * chunk] for f in range(chunks)], axis=1
     )
-    gw_out = scattered[:, 2 * hidden :]
-    gw_in = jnp.stack([one.result() for one in in_sums], axis=1)
+    gw_out = sums[0].result()
+    gw_in = in_sums.result()
     gw_in = gw_in.reshape(shard_rows, pairs, 3, 128)
     gw_in = jnp.transpose(gw_in, (2, 0, 1, 3)).reshape(3, shard_rows, cols)
     norms = jnp.concatenate([first_sums[:2], second_sums[:2]]) * scale
     norms = norms + swap(norms, "mlp")
-    heads = jnp.stack([part[:2] for part in gain_sums], axis=1).reshape(2, cols) * scale
+    heads = jnp.transpose(head_sums[0].reshape(pairs, 2, 128), (1, 0, 2)).reshape(2, cols) * scale
     small = jnp.concatenate([norms, heads.reshape(1, width)])
     small = small + swap(small, "seq")
     for bit in (1, 2, 4):

time: 529 us -> 457 us (0.86)
  Pallas kernels: 275 us -> 227 us
  other arithmetic: 51.9 us -> 22 us
  local copies, waits for them, and re-layouts: 45.4 us -> 31.2 us
  starting transfers between devices: 62 us -> 74.4 us
  waiting for transfers between devices: 72.1 us -> 79 us
    pallas_call x19 -> x9, Pallas kernels: 275 us -> 227 us  [call(): return lambda *operands: run(*operands, *pins)]
    ppermute x12 -> x9, starting transfers between devices: 16.2 us -> 38.5 us  [shift_far(): lax.ppermute(values, 'dp', [(2 * ((z + step) % 4) + x, 2 * z + x) for z i...]
    ppermute x7 -> x6, starting transfers between devices: 25.2 us -> 7.73 us  [swap_x(): return lax.ppermute(values, 'dp', [(d, d ^ 1) for d in range(8)])]
    ppermute x3, waiting for transfers between devices: 1.01 us -> 15.5 us  [on_device_small(): small = small + lax.ppermute(small, 'dp', [(i, i ^ bit) for i in range(8)])]
    unnamed x9 -> x2, other arithmetic: 12.9 us -> 0.09 us
    ppermute x7 -> x6, waiting for transfers between devices: 23.7 us -> 13.5 us  [swap_x(): return lax.ppermute(values, 'dp', [(d, d ^ 1) for d in range(8)])]
    transpose x3 -> x1, other arithmetic: 11.5 us -> 1.59 us  [on_device_small(): jnp.transpose(gw_out)]
    concatenate x4 -> x1, local copies, waits for them, and re-layouts: 7.61 us -> 0.01 us  [gather_shards(): return lax.all_gather(jnp.concatenate(parts, axis=1), ('dp', 'mlp'), axis=0)]
  transfers between devices with their start and end apart: 51 -> 44, of which waited for: 13 -> 14; matrix products, arithmetic and copies ran while one was open for 17% -> 9% of each run, Pallas kernels for 44% -> 28%
where the time goes in v3:
time: 457 us; the launch traced here: 449 us
  Pallas kernels  227 us (50%)
  waiting for transfers between devices  79 us (17%)
  starting transfers between devices  74.4 us (16%)
  local copies, waits for them, and re-layouts  31.2 us (7%)
  other arithmetic  22 us (5%)
  between operations  15.1 us (3%)
    pallas_call x9, Pallas kernels, call(): return lambda *operands: run(*operands, *pins)  227 us
    ppermute x9, starting transfers between devices, shift_far(): lax.ppermute(values, 'dp', [(2 * ((z + step) % 4) + x, 2 * z + x) for z i...  38.5 us
    ppermute x9, waiting for transfers between devices, shift_far(): lax.ppermute(values, 'dp', [(2 * ((z + step) % 4) + x, 2 * z + x) for z i...  24.1 us
    ppermute x24, starting transfers between devices, swap(): return lax.ppermute(values, axis, [(0, 1), (1, 0)])  23.9 us
    ppermute x24, waiting for transfers between devices, swap(): return lax.ppermute(values, axis, [(0, 1), (1, 0)])  23.7 us
    ppermute x3, waiting for transfers between devices, on_device_small(): small = small + lax.ppermute(small, 'dp', [(i, i ^ bit) for i in range(8)])  15.5 us
    ppermute x6, waiting for transfers between devices, swap_x(): return lax.ppermute(values, 'dp', [(d, d ^ 1) for d in range(8)])  13.5 us
    unnamed x88, local copies, waits for them, and re-layouts  10.9 us
  transfers between devices with their start and end apart: 44, of which 14 were waited for; matrix products, arithmetic and copies ran while one was open for 9% of the time, Pallas kernels for 28%

profile of v3, /device:TPU:0, one launch (start us, length us, event | category | flops | bytes accessed | tf_op | source)
XLA Modules:
  0.0 448.7 jit_solution(15983573112811161054)
XLA Ops:
  12.4 3.0 collective-permute-start.7
  15.4 2.6 collective-permute-start.5
  20.8 2.5 dynamic-slice_bitcast_fusion.4
  34.1 12.9 %collective-permute-done.5.refs_12_.refs_19_ = bf16[112,1152]{1,0:T(8,128)(2,1)} collective-permute-done((bf16[112,1152]{1,0:T(8,128)(2,1)}, bf16[112,1152]{1,0:T(8,128)(2,1)}, u32[]{:S(2)}, u32[]{:S(2)}) %collective-permute-start.5) | collective-permute-done | bytes 258080 | tf_op jit(solution)/shard_map/ppermute | solution.py:935
  51.9 13.5 %collective-permute-done.4.refs_11_.refs_18_ = bf16[112,1152]{1,0:T(8,128)(2,1)S(1)} collective-permute-done((bf16[112,1152]{1,0:T(8,128)(2,1)}, bf16[112,1152]{1,0:T(8,128)(2,1)S(1)}, u32[]{:S(2)}, u32[]{:S(2)}) %collective-permute-start.4) | collective-permute-done | bytes 258080 | tf_op jit(solution)/shard_map/ppermute | solution.py:943
  73.4 23.0 %qkv.1 = (bf16[3,1024,1152]{2,1,0:T(8,128)(2,1)}, f32[3,1024,768]{2,1,0:T(8,128)}, bf16[768,3072]{1,0:T(8,128)(2,1)}) custom-call(s32[10]{0:T(128)} %concatenate.40.refs_0_, bf16[6,512,768]{2,1,0:T(8,128)(2,1)} %bitcast.164, bf16[3,256,768]{2,1,0:T(8,128)(2,1)} %collective-permute-done.refs_2_.refs_4_, bf16[3,256,768]{2,1,0:T(8,128)(2,1)} %collective-permute-done.1.refs_3_, ...), custom_call_target="tpu_custom_call" | custom-call | flops 28750000128 | bytes 1000000 | tf_op jit(solution)/shard_map/qkv/pallas_call | solution.py:1106
  96.4 17.9 %attn_fwd.1 = (bf16[3,2,256,384]{3,2,1,0:T(8,128)(2,1)}, bf16[3,2,256,384]{3,2,1,0:T(8,128)(2,1)}, f32[3,1024,384]{2,1,0:T(8,128)}) custom-call(s32[10]{0:T(128)} %concatenate.40.refs_0_, s32[12]{0:T(128)} %reshape.229.refs_1_, s32[12]{0:T(128)} %reshape.230.refs_2_, bf16[3,1024,1152]{2,1,0:T(8,128)(2,1)} %get-tuple-element.39.refs_3_, ...), custom_call_target="tpu_custom_call" | custom-call | flops 25300000768 | bytes 1000000 | tf_op jit(solution)/shard_map/attn_fwd/pallas_call | solution.py:1106
  122.4 100.7 %middle.1 = (bf16[3,256,384]{2,1,0:T(8,128)(2,1)}, bf16[3,256,384]{2,1,0:T(8,128)(2,1)}, bf16[3,256,384]{2,1,0:T(8,128)(2,1)}, bf16[3,256,384]{2,1,0:T(8,128)(2,...) custom-call(s32[10]{0:T(128)} %concatenate.40.refs_0_, ...), custom_call_target="tpu_custom_call" | custom-call | flops 92000002048 | bytes 1000000 | tf_op jit(solution)/shard_map/middle/pallas_call | solution.py:1106
  227.2 39.9 %attn_bwd.2 = (bf16[2,2,256,768]{3,2,1,0:T(8,128)(2,1)}, bf16[2,2,256,768]{3,2,1,0:T(8,128)(2,1)}, f32[768,1152]{1,0:T(8,128)}, f32[8,768]{1,0:T(8,128)}) custom-call(s32[10]{0:T(128)} %concatenate.40.refs_0_, s32[12]{0:T(128)} %reshape.229.refs_1_, s32[12]{0:T(128)} %reshape.230.refs_2_, bf16[3,1024,1152]{2,1,0:T(8,128)(2,1)} %get-tuple-element.39.refs_3_, ...), custom_call_target="tpu_custom_call" | custom-call | flops 46000001024 | bytes 1000000 | tf_op jit(solution)/shard_map/attn_bwd/pallas_call | solution.py:1106
  268.6 11.2 %collective-permute-start.13 = (bf16[3,256,384]{2,1,0:T(8,128)(2,1)}, bf16[3,256,384]{2,1,0:T(8,128)(2,1)S(1)}, u32[]{:S(2)}, u32[]{:S(2)}) collective-permute-start(bf16[3,256,384]{2,1,0:T(8,128)(2,1)} %get-tuple-element.44), channel_id=1, source_target_pairs={{0,2},{2,0},{1,3},{3,1},{4,6},{6,4},{5,7},{7,5},{8,10},{10,8},{9,1... | collective-permute-start | bytes 1769480 | tf_op jit(solution)/shard_map/ppermute | solution.py:919
  279.9 2.7 collective-permute-start.23
  283.8 7.2 %first_norm.2 = (bf16[2,256,768]{2,1,0:T(8,128)(2,1)}, bf16[2,256,768]{2,1,0:T(8,128)(2,1)}, f32[8,768]{1,0:T(8,128)}) custom-call(s32[10]{0:T(128)} %concatenate.40.refs_0_, bf16[6,512,768]{2,1,0:T(8,128)(2,1)} %bitcast.166, bf16[3,256,768]{2,1,0:T(8,128)(2,1)} %collective-permute-done.refs_2_.refs_4_, bf16[2,2,256,768]{3,2,1,0:T(8,128)(2,1)} %get-tuple-element.51.refs_3_, ...), custom_call_target="tpu_custom_call" | custom-call | flops 6133333504 | bytes 1000000 | tf_op jit(solution)/shard_map/first_norm/pallas_call | solution.py:1106
  291.0 2.8 collective-permute-start.19
  294.0 12.6 %collective-permute-done.14.refs_26_ = bf16[3,256,384]{2,1,0:T(8,128)(2,1)S(1)} collective-permute-done((bf16[3,256,384]{2,1,0:T(8,128)(2,1)}, bf16[3,256,384]{2,1,0:T(8,128)(2,1)S(1)}, u32[]{:S(2)}, u32[]{:S(2)}) %collective-permute-start.14) | collective-permute-done | bytes 589856 | tf_op jit(solution)/shard_map/ppermute | solution.py:919
  307.5 24.3 %attn_bwd.3 = (bf16[1,2,256,768]{3,2,1,0:T(8,128)(2,1)}, bf16[1,2,256,768]{3,2,1,0:T(8,128)(2,1)}, bf16[2,4,96,1152]{3,2,1,0:T(8,128)(2,1)}, f32[8,768]{1,0:T(8,128)}) custom-call(s32[10]{0:T(128)} %concatenate.40.refs_0_, s32[12]{0:T(128)} %reshape.229.refs_1_, s32[12]{0:T(128)} %reshape.230.refs_2_, bf16[3,1024,1152]{2,1,0:T(8,128)(2,1)} %get-tuple-element.39.refs_3_, ...), custom_call_target="tpu_custom_call" | custom-call | flops 23000000512 | bytes 1000000 | tf_op jit(solution)/shard_map/attn_bwd/pallas_call | solution.py:1106
  332.7 26.1 %collective-permute-start.32 = (bf16[96,384]{1,0:T(8,128)(2,1)}, bf16[96,384]{1,0:T(8,128)(2,1)S(1)}, u32[]{:S(2)}, u32[]{:S(2)}) collective-permute-start(bf16[96,384]{1,0:T(8,128)(2,1)} %get-tuple-element.109), channel_id=1, source_target_pairs={{24,0},{28,4},{0,8},{4,12},{8,16},{12,20},{16,24},{20,28},{25,1},{... | collective-permute-start | bytes 221192 | tf_op jit(solution)/shard_map/ppermute | solution.py:935
  361.6 4.8 %first_norm.3 = (bf16[1,256,768]{2,1,0:T(8,128)(2,1)}, bf16[1,256,768]{2,1,0:T(8,128)(2,1)}, f32[8,768]{1,0:T(8,128)}) custom-call(s32[10]{0:T(128)} %concatenate.40.refs_0_, bf16[6,512,768]{2,1,0:T(8,128)(2,1)} %bitcast.167, bf16[3,256,768]{2,1,0:T(8,128)(2,1)} %collective-permute-done.refs_2_.refs_4_, bf16[1,2,256,768]{3,2,1,0:T(8,128)(2,1)} %get-tuple-element.58.refs_3_, ...), custom_call_target="tpu_custom_call" | custom-call | flops 3066666752 | bytes 1000000 | tf_op jit(solution)/shard_map/first_norm/pallas_call | solution.py:1106
  379.0 13.9 %collective-permute-done.39 = f32[5,768]{1,0:T(8,128)S(1)} collective-permute-done((f32[5,768]{1,0:T(8,128)S(1)}, f32[5,768]{1,0:T(8,128)S(1)}, u32[]{:S(2)}, u32[]{:S(2)}) %collective-permute-start.39) | collective-permute-done | bytes 15392 | tf_op jit(solution)/shard_map/ppermute | solution.py:1368
  404.6 3.7 place.2
  410.2 2.3 collective-permute-done.30
  412.5 8.7 %collective-permute-done.29 = bf16[96,1152]{1,0:T(8,128)(2,1)S(1)} collective-permute-done((bf16[96,1152]{1,0:T(8,128)(2,1)S(1)}, bf16[96,1152]{1,0:T(8,128)(2,1)S(1)}, u32[]{:S(2)}, u32[]{:S(2)}) %collective-permute-start.29) | collective-permute-done | bytes 221216 | tf_op jit(solution)/shard_map/ppermute | solution.py:935
  424.3 5.4 %collective-permute-done.31 = bf16[96,1152]{1,0:T(8,128)(2,1)} collective-permute-done((bf16[96,1152]{1,0:T(8,128)(2,1)S(1)}, bf16[96,1152]{1,0:T(8,128)(2,1)}, u32[]{:S(2)}, u32[]{:S(2)}) %collective-permute-start.31) | collective-permute-done | bytes 221216 | tf_op jit(solution)/shard_map/ppermute | solution.py:919
  432.1 5.4 %place.3 = bf16[6,2,256,768]{3,2,1,0:T(8,128)(2,1)} custom-call(s32[10]{0:T(128)} %concatenate.40.refs_0_, bf16[2,256,768]{2,1,0:T(8,128)(2,1)} %get-tuple-element.54.refs_27_.refs_1_, bf16[2,256,768]{2,1,0:T(8,128)(2,1)} %copy-done.5, bf16[2,256,768]{2,1,0:T(8,128)(2,1)} %collective-permute-done.19.refs_8_.refs_3_, ...), custom_call_target="tpu_custom_call" | custom-call | flops 4600000000 | bytes 1000000 | tf_op jit(solution)/shard_map/place/pallas_call | solution.py:1106
  437.5 2.8 collective-permute-done.36
  (260 shorter events, 83.6 us)
Async XLA Ops:
  7.2 114.0 %all-gather.3.cloned.1.call-start = ((), (), s32[]{:S(2)}) async-start(), calls=%async_computation.2 | async-start | bytes 11280384 | tf_op jit(solution)/shard_map/all_gather | solution.py:1048
  10.6 411.6 %reduce-scatter.2.cloned.1.call-start = ((), (), s32[]{:S(2)}) async-start(), calls=%async_computation.1 | async-start | bytes 10027008 | tf_op jit(solution)/shard_map/reduce_scatter | solution.py:1230
  12.4 21.7 %collective-permute-start.7 = (bf16[112,1152]{1,0:T(8,128)(2,1)}, bf16[112,1152]{1,0:T(8,128)(2,1)}, u32[]{:S(2)}, u32[]{:S(2)}) collective-permute-start(bf16[112,1152]{1,0:T(8,128)(2,1)} %fusion.3.refs_8_.refs_15_), channel_id=1, source_target_pairs={{24,0},{28,4},{0,8},{4,12},{8,16},{12,20},{16,24},{20,28},{25,1},{... | collective-permute-start | bytes 774152 | tf_op jit(solution)/shard_map/ppermute | solution.py:935
  15.4 31.6 %collective-permute-start.5 = (bf16[112,1152]{1,0:T(8,128)(2,1)}, bf16[112,1152]{1,0:T(8,128)(2,1)}, u32[]{:S(2)}, u32[]{:S(2)}) collective-permute-start(bf16[112,1152]{1,0:T(8,128)(2,1)} %fusion.3.refs_8_.refs_15_), channel_id=1, source_target_pairs={{16,0},{20,4},{24,8},{28,12},{0,16},{4,20},{8,24},{12,28},{17,1},{... | collective-permute-start | bytes 774152 | tf_op jit(solution)/shard_map/ppermute | solution.py:935
  18.0 30.5 %collective-permute-start.3 = (bf16[112,1152]{1,0:T(8,128)(2,1)}, bf16[112,1152]{1,0:T(8,128)(2,1)}, u32[]{:S(2)}, u32[]{:S(2)}) collective-permute-start(bf16[112,1152]{1,0:T(8,128)(2,1)} %fusion.3.refs_8_.refs_15_), channel_id=1, source_target_pairs={{8,0},{12,4},{16,8},{20,12},{24,16},{28,20},{0,24},{4,28},{9,1},{1... | collective-permute-start | bytes 774152 | tf_op jit(solution)/shard_map/ppermute | solution.py:935
  19.4 29.7 %collective-permute-start.2 = (bf16[112,1152]{1,0:T(8,128)(2,1)}, bf16[112,1152]{1,0:T(8,128)(2,1)}, u32[]{:S(2)}, u32[]{:S(2)}) collective-permute-start(bf16[112,1152]{1,0:T(8,128)(2,1)} %fusion.3.refs_8_.refs_15_), channel_id=1, source_target_pairs={{0,4},{4,0},{8,12},{12,8},{16,20},{20,16},{24,28},{28,24},{1,5},{5... | collective-permute-start | bytes 774152 | tf_op jit(solution)/shard_map/ppermute | solution.py:943
  23.3 43.4 %collective-permute-start = (bf16[3,256,768]{2,1,0:T(8,128)(2,1)}, bf16[3,256,768]{2,1,0:T(8,128)(2,1)}, u32[]{:S(2)}, u32[]{:S(2)}) collective-permute-start(bf16[3,256,768]{2,1,0:T(8,128)(2,1)} %dynamic-slice_bitcast_fusion.4), channel_id=1, source_target_pairs={{0,2},{2,0},{1,3},{3,1},{4,6},{6,4},{5,7},{7,5},{8,10},{10,8},{9,1... | collective-permute-start | bytes 3538952 | tf_op jit(solution)/shard_map/ppermute | solution.py:919
  34.1 37.0 %collective-permute-start.10 = (bf16[256,6,384]{2,0,1:T(8,128)(2,1)}, bf16[256,6,384]{2,0,1:T(8,128)(2,1)S(1)}, u32[]{:S(2)}, u32[]{:S(2)}) collective-permute-start(bf16[256,6,384]{2,0,1:T(8,128)(2,1)} %get-tuple-element.99), channel_id=1, source_target_pairs={{0,1},{1,0},{2,3},{3,2},{4,5},{5,4},{6,7},{7,6},{8,9},{9,8},{10,11... | collective-permute-start | bytes 3538952 | tf_op jit(solution)/shard_map/ppermute | solution.py:919
  47.0 19.8 %collective-permute-start.8 = (bf16[112,1152]{1,0:T(8,128)(2,1)}, bf16[112,1152]{1,0:T(8,128)(2,1)S(1)}, u32[]{:S(2)}, u32[]{:S(2)}) collective-permute-start(bf16[112,1152]{1,0:T(8,128)(2,1)} %collective-permute-done.7.refs_14_.refs_21_), channel_id=1, source_target_pairs={{0,4},{4,0},{8,12},{12,8},{16,20},{20,16},{24,28},{28,24},{1,5},{5... | collective-permute-start | bytes 774152 | tf_op jit(solution)/shard_map/ppermute | solution.py:943
  71.9 45.0 %collective-permute-start.11 = (bf16[3,256,768]{2,1,0:T(8,128)(2,1)S(1)}, bf16[3,256,768]{2,1,0:T(8,128)(2,1)S(1)}, u32[]{:S(2)}, u32[]{:S(2)}) collective-permute-start(bf16[3,256,768]{2,1,0:T(8,128)(2,1)S(1)} %get-tuple-element.97), channel_id=1, source_target_pairs={{0,2},{2,0},{1,3},{3,1},{4,6},{6,4},{5,7},{7,5},{8,10},{10,8},{9,1... | collective-permute-start | bytes 3538952 | tf_op jit(solution)/shard_map/ppermute | solution.py:919
  268.6 25.5 %collective-permute-start.13 = (bf16[3,256,384]{2,1,0:T(8,128)(2,1)}, bf16[3,256,384]{2,1,0:T(8,128)(2,1)S(1)}, u32[]{:S(2)}, u32[]{:S(2)}) collective-permute-start(bf16[3,256,384]{2,1,0:T(8,128)(2,1)} %get-tuple-element.44), channel_id=1, source_target_pairs={{0,2},{2,0},{1,3},{3,1},{4,6},{6,4},{5,7},{7,5},{8,10},{10,8},{9,1... | collective-permute-start | bytes 1769480 | tf_op jit(solution)/shard_map/ppermute | solution.py:919
  279.7 26.9 %collective-permute-start.14 = (bf16[3,256,384]{2,1,0:T(8,128)(2,1)}, bf16[3,256,384]{2,1,0:T(8,128)(2,1)S(1)}, u32[]{:S(2)}, u32[]{:S(2)}) collective-permute-start(bf16[3,256,384]{2,1,0:T(8,128)(2,1)} %get-tuple-element.45), channel_id=1, source_target_pairs={{0,2},{2,0},{1,3},{3,1},{4,6},{6,4},{5,7},{7,5},{8,10},{10,8},{9,1... | collective-permute-start | bytes 1769480 | tf_op jit(solution)/shard_map/ppermute | solution.py:919
  279.9 52.0 %collective-permute-start.23 = (bf16[4,96,384]{2,1,0:T(8,128)(2,1)S(1)}, bf16[4,96,384]{2,1,0:T(8,128)(2,1)S(1)}, u32[]{:S(2)}, u32[]{:S(2)}) collective-permute-start(bf16[4,96,384]{2,1,0:T(8,128)(2,1)S(1)} %fusion), channel_id=1, source_target_pairs={{0,4},{4,0},{8,12},{12,8},{16,20},{20,16},{24,28},{28,24},{1,5},{5... | collective-permute-start | bytes 884744 | tf_op jit(solution)/shard_map/ppermute | solution.py:943
  291.0 67.9 %collective-permute-start.19 = (bf16[2,256,768]{2,1,0:T(8,128)(2,1)}, bf16[2,256,768]{2,1,0:T(8,128)(2,1)}, u32[]{:S(2)}, u32[]{:S(2)}) collective-permute-start(bf16[2,256,768]{2,1,0:T(8,128)(2,1)} %get-tuple-element.55), channel_id=1, source_target_pairs={{0,2},{2,0},{1,3},{3,1},{4,6},{6,4},{5,7},{7,5},{8,10},{10,8},{9,1... | collective-permute-start | bytes 2359304 | tf_op jit(solution)/shard_map/ppermute | solution.py:919
  293.9 66.6 %collective-permute-start.18 = (bf16[2,256,768]{2,1,0:T(8,128)(2,1)}, bf16[2,256,768]{2,1,0:T(8,128)(2,1)S(1)}, u32[]{:S(2)}, u32[]{:S(2)}) collective-permute-start(bf16[2,256,768]{2,1,0:T(8,128)(2,1)} %get-tuple-element.54.refs_27_.refs_1_), channel_id=1, source_target_pairs={{0,1},{1,0},{2,3},{3,2},{4,5},{5,4},{6,7},{7,6},{8,9},{9,8},{10,11... | collective-permute-start | bytes 2359304 | tf_op jit(solution)/shard_map/ppermute | solution.py:919
  331.8 28.6 %collective-permute-start.22 = (bf16[1,2,256,768]{3,2,1,0:T(8,128)(2,1)}, bf16[1,2,256,768]{3,2,1,0:T(8,128)(2,1)S(1)}, u32[]{:S(2)}, u32[]{:S(2)}) collective-permute-start(bf16[1,2,256,768]{3,2,1,0:T(8,128)(2,1)} %get-tuple-element.59), channel_id=1, source_target_pairs={{0,1},{1,0},{2,3},{3,2},{4,5},{5,4},{6,7},{7,6},{8,9},{9,8},{10,11... | collective-permute-start | bytes 2359304 | tf_op jit(solution)/shard_map/ppermute | solution.py:919
  332.7 39.2 %collective-permute-start.32 = (bf16[96,384]{1,0:T(8,128)(2,1)}, bf16[96,384]{1,0:T(8,128)(2,1)S(1)}, u32[]{:S(2)}, u32[]{:S(2)}) collective-permute-start(bf16[96,384]{1,0:T(8,128)(2,1)} %get-tuple-element.109), channel_id=1, source_target_pairs={{24,0},{28,4},{0,8},{4,12},{8,16},{12,20},{16,24},{20,28},{25,1},{... | collective-permute-start | bytes 221192 | tf_op jit(solution)/shard_map/ppermute | solution.py:935
  370.4 27.9 %collective-permute-start.27 = (bf16[4,96,1152]{2,1,0:T(8,128)(2,1)S(1)}, bf16[4,96,1152]{2,1,0:T(8,128)(2,1)}, u32[]{:S(2)}, u32[]{:S(2)}) collective-permute-start(bf16[4,96,1152]{2,1,0:T(8,128)(2,1)S(1)} %slice_bitcast_fusion), channel_id=1, source_target_pairs={{0,4},{4,0},{8,12},{12,8},{16,20},{20,16},{24,28},{28,24},{1,5},{5... | collective-permute-start | bytes 2654216 | tf_op jit(solution)/shard_map/ppermute | solution.py:943
  372.6 21.0 %collective-permute-start.35 = (bf16[96,384]{1,0:T(8,128)(2,1)}, bf16[96,384]{1,0:T(8,128)(2,1)}, u32[]{:S(2)}, u32[]{:S(2)}) collective-permute-start(bf16[96,384]{1,0:T(8,128)(2,1)} %fusion.13), channel_id=1, source_target_pairs={{0,2},{2,0},{1,3},{3,1},{4,6},{6,4},{5,7},{7,5},{8,10},{10,8},{9,1... | collective-permute-start | bytes 221192 | tf_op jit(solution)/shard_map/ppermute | solution.py:919
  378.5 25.0 %collective-permute-start.12 = (bf16[3,256,384]{2,1,0:T(8,128)(2,1)}, bf16[3,256,384]{2,1,0:T(8,128)(2,1)S(1)}, u32[]{:S(2)}, u32[]{:S(2)}) collective-permute-start(bf16[3,256,384]{2,1,0:T(8,128)(2,1)} %get-tuple-element.43), channel_id=1, source_target_pairs={{0,1},{1,0},{2,3},{3,2},{4,5},{5,4},{6,7},{7,6},{8,9},{9,8},{10,11... | collective-permute-start | bytes 1769480 | tf_op jit(solution)/shard_map/ppermute | solution.py:919
  378.5 25.0 %collective-permute-start.15 = (bf16[3,256,384]{2,1,0:T(8,128)(2,1)}, bf16[3,256,384]{2,1,0:T(8,128)(2,1)S(1)}, u32[]{:S(2)}, u32[]{:S(2)}) collective-permute-start(bf16[3,256,384]{2,1,0:T(8,128)(2,1)} %copy-done.33), channel_id=1, source_target_pairs={{0,1},{1,0},{2,3},{3,2},{4,5},{5,4},{6,7},{7,6},{8,9},{9,8},{10,11... | collective-permute-start | bytes 1769480 | tf_op jit(solution)/shard_map/ppermute | solution.py:919
  408.4 23.7 %collective-permute-start.24 = (bf16[1,256,768]{2,1,0:T(8,128)(2,1)}, bf16[1,256,768]{2,1,0:T(8,128)(2,1)}, u32[]{:S(2)}, u32[]{:S(2)}) collective-permute-start(bf16[1,256,768]{2,1,0:T(8,128)(2,1)} %get-tuple-element.60.refs_5_), channel_id=1, source_target_pairs={{0,1},{1,0},{2,3},{3,2},{4,5},{5,4},{6,7},{7,6},{8,9},{9,8},{10,11... | collective-permute-start | bytes 1179656 | tf_op jit(solution)/shard_map/ppermute | solution.py:919
  409.9 22.2 %collective-permute-start.20 = (bf16[2,256,768]{2,1,0:T(8,128)(2,1)}, bf16[2,256,768]{2,1,0:T(8,128)(2,1)}, u32[]{:S(2)}, u32[]{:S(2)}) collective-permute-start(bf16[2,256,768]{2,1,0:T(8,128)(2,1)} %collective-permute-done.19.refs_8_.refs_3_), channel_id=1, source_target_pairs={{0,1},{1,0},{2,3},{3,2},{4,5},{5,4},{6,7},{7,6},{8,9},{9,8},{10,11... | collective-permute-start | bytes 2359304 | tf_op jit(solution)/shard_map/ppermute | solution.py:919
  422.2 18.1 %collective-permute-start.36 = (bf16[96,3072]{1,0:T(8,128)(2,1)}, bf16[96,3072]{1,0:T(8,128)(2,1)S(1)}, u32[]{:S(2)}, u32[]{:S(2)}) collective-permute-start(bf16[96,3072]{1,0:T(8,128)(2,1)} %bitcast.172), channel_id=1, source_target_pairs={{0,2},{2,0},{1,3},{3,1},{4,6},{6,4},{5,7},{7,5},{8,10},{10,8},{9,1... | collective-permute-start | bytes 1769480 | tf_op jit(solution)/shard_map/ppermute | solution.py:919
  (58 other events, 507.9 us)
Sparse Core Ops, SparseCore 0:
  10.7 110.4 all-gather.2
  223.6 127.0 reduce-scatter.1

commit v4 on v3

--- a/solution.py
+++ b/solution.py
@@ -298,7 +298,7 @@
     "qkv": 25,
     "attn_fwd": 22,
     "middle": 80,
-    "attn_bwd": 60,
+    "attn_bwd": 75,
     "first_norm": 8,
     "place": 4,
 }
@@ -671,7 +671,6 @@
     go_send_ref,
     sums_ref,
     grads,
-    out_grads,
     x2_all,
     h_all,
     ht_all,
@@ -702,7 +701,7 @@
     first_half = info_ref[0] == 0
 
     def weight_copies(f, slot):
-        begin = cols + f * 2 * chunk
+        begin = pl.multiple_of(cols + f * 2 * chunk, 128)
         sems = weight_sems.at[slot]
         return load_shards(
             [(shards, m, begin, chunk, m * chunk) for m in range(2)], up_both.at[slot], sems
@@ -714,7 +713,9 @@
 
     def stage_copy(f):
         return pltpu.make_async_copy(
-            stage, grads.at[:, :, pl.ds(f * 2 * chunk, 2 * chunk)], stage_sem.at[0]
+            stage,
+            grads.at[:, :, pl.ds(pl.multiple_of(f * 2 * chunk, 128), 2 * chunk)],
+            stage_sem.at[0],
         )
 
     def both_heads():
@@ -731,6 +732,7 @@
         for copy in weight_copies(0, 0):
             copy.start()
         sums_ref[...] = jnp.zeros_like(sums_ref)
+        wo_acc[...] = jnp.zeros_like(wo_acc)
 
     @pl.when(phase == 0)
     def _():
@@ -743,6 +745,8 @@
         ).astype(wide)
         x2 = x + dot(both_heads(), wo_ref[...], 1, 1)
         x2_all[r] = x2
+        out_all[r] = x2
+        gh_all[r] = jnp.zeros_like(x2)
         centered = x2 - jnp.mean(x2, axis=1, keepdims=True)
         variance = jnp.mean(centered * centered, axis=1, keepdims=True)
         h = (centered * lax.rsqrt(variance + norm_eps) * gain_ref[...] + bias_ref[...]).astype(low)
@@ -752,16 +756,20 @@
         gy_all[r] = gy
         gyt_all[r] = jnp.transpose(gy)
 
-    def mlp_step(f):
+    @pl.when((phase > 0) & (phase <= chunks))
+    def _():
+        f = phase - 1
         slot = f % 2
 
         @pl.when(r == 0)
         def _():
             for copy in weight_copies(f, slot):
                 copy.wait()
-            if f + 1 < chunks:
-                for copy in weight_copies(f + 1, 1 - slot):
-                    copy.start()
+
+        @pl.when((r == 0) & (f + 1 < chunks))
+        def _():
+            for copy in weight_copies(f + 1, 1 - slot):
+                copy.start()
 
         up_ref = up_both.at[slot]
         down_ref = down_both.at[slot]
@@ -772,31 +780,26 @@
             act, slope = gelu_parts(dot(h, up_ref[:, at : at + size]))
             act_all[:, at : at + size] = act.astype(low)
             grad_all[:, at : at + size] = (dot(gy, down_ref[:, at : at + size]) * slope).astype(low)
-        base = x2_all[r] if f == 0 else out_all[r]
-        out_all[r] = base + dot(act_all[...], down_ref[...], 1, 1)
-        back = dot(grad_all[...], up_ref[...], 1, 1)
-        gh_all[r] = back if f == 0 else gh_all[r] + back
+        out_all[r] += dot(act_all[...], down_ref[...], 1, 1)
+        gh_all[r] += dot(grad_all[...], up_ref[...], 1, 1)
 
         @pl.when(r == 0)
         def _():
-            up_acc[...] = dot(ht_all[r], grad_all[...])
-            down_acc[...] = dot(gyt_all[r], act_all[...])
-
-        @pl.when(r > 0)
+            up_acc[...] = jnp.zeros_like(up_acc)
+            down_acc[...] = jnp.zeros_like(down_acc)
+
+        up_acc[...] += dot(ht_all[r], grad_all[...])
+        down_acc[...] += dot(gyt_all[r], act_all[...])
+
+        @pl.when((r == last) & (f > 0))
         def _():
-            up_acc[...] += dot(ht_all[r], grad_all[...])
-            down_acc[...] += dot(gyt_all[r], act_all[...])
+            stage_copy(f - 1).wait()
 
         @pl.when(r == last)
         def _():
-            if f > 0:
-                stage_copy(f - 1).wait()
             put_blocks(stage, up_acc, scale, (0, 1), 0, chunk)
             put_blocks(stage, down_acc, scale, (0, 1), chunk, chunk)
             stage_copy(f).start()
-
-    for f in range(chunks):
-        pl.when(phase == f + 1)(partial(mlp_step, f))
 
     @pl.when(phase == chunks + 1)
     def _():
@@ -818,27 +821,15 @@
         turned = jnp.transpose(gx_low)
         sums_ref[0:1, :] += jnp.sum(gh * normed, axis=0, keepdims=True)
         sums_ref[1:2, :] += jnp.sum(gh, axis=0, keepdims=True)
-        product = dot(turned, both_heads())
-
-        @pl.when(r == 0)
-        def _():
-            wo_acc[...] = product
-
-        @pl.when(r > 0)
-        def _():
-            wo_acc[...] += product
+        wo_acc[...] += dot(turned, both_heads())
 
         @pl.when(r == last)
         def _():
             stage_copy(chunks - 1).wait()
-            rows = stage_out.shape[3]
-            for side in range(2):
-                for index in range(8):
-                    place = pl.multiple_of(info_ref[2 + index] * rows, rows)
-                    stage_out[side, index % 2, index // 2] = (
-                        wo_acc[pl.ds(place, rows), side * cols : (side + 1) * cols] * scale
-                    ).astype(low)
-            copy = pltpu.make_async_copy(stage_out, out_grads, stage_sem.at[1])
+            put_blocks(stage_out, wo_acc, scale, (c, 1 - c), 0, cols)
+            copy = pltpu.make_async_copy(
+                stage_out, grads.at[:, :, pl.ds(chunks * 2 * chunk, cols)], stage_sem.at[1]
+            )
             copy.start()
             copy.wait()
 
@@ -949,47 +940,6 @@
         piece = shard if step == 0 else shift_far(shard, step)
         pieces += [piece, swap_x(piece)]
     return pieces
-
-
-class Reduce:
-    def __init__(self, mine, other=None):
-        self.mine = mine
-        self.other = other
-        self.got = None
-        self.state = None
-        self.phase = "core" if other is not None else "x"
-
-    def advance(self):
-        if self.phase == "core":
-            self.state = self.got = swap(self.other, "mlp")
-            self.phase = "x"
-        elif self.phase == "x":
-            far = self.mine[1]
-            if self.got is not None:
-                far = (far.astype(wide) + self.got[1].astype(wide)).astype(low)
-            self.state = swap_x(far)
-            self.phase = "z"
-        elif self.phase == "z":
-            total = self.mine[0].astype(wide) + self.state.astype(wide)
-            if self.got is not None:
-                total = total + self.got[0].astype(wide)
-            low_total = total.astype(low)
-            self.mine = total[0]
-            self.state = [shift_far(low_total[step], 4 - step) for step in range(1, 4)]
-            self.phase = "y"
-        elif self.phase == "y":
-            self.mine = self.mine + sum(part.astype(wide) for part in self.state)
-            self.state = swap(self.mine.astype(low), "seq")
-            self.phase = "end"
-        elif self.phase == "end":
-            self.mine = self.mine + self.state.astype(wide)
-            self.state = None
-            self.phase = "done"
-
-    def result(self):
-        while self.phase != "done":
-            self.advance()
-        return self.mine
 
 
 def on_device_small(
@@ -1167,8 +1117,8 @@
     by_seq_bf = pltpu.VMEM((seqs, half, width), low)
     by_seq_turned = pltpu.VMEM((seqs, width, half), low)
     by_seq_wide = pltpu.VMEM((seqs, half, width), wide)
-    grad_shape = (16, shard_rows, 2 * hidden)
-    keep_near, keep_far, send_near, send_far, gx2, go_mine, go_send, second_sums, grads, out_grads = call(
+    grad_shape = (16, shard_rows, 2 * hidden + cols)
+    keep_near, keep_far, send_near, send_far, gx2, go_mine, go_send, second_sums, grads = call(
         partial(middle_kernel, scale, chunks),
         (chunks + 2, seqs),
         [
@@ -1194,7 +1144,6 @@
             heads_out,
             whole((8, width)),
             anywhere,
-            anywhere,
         ],
         [
             shape_of((seqs, part, cols)),
@@ -1206,7 +1155,6 @@
             shape_of((seqs, 2, part, cols)),
             shape_of((8, width), wide),
             shape_of(grad_shape),
-            shape_of((2, 2, 4, shard_rows, cols)),
         ],
         [by_seq_wide, by_seq_bf, by_seq_turned, by_seq_bf, by_seq_turned, by_seq_wide, by_seq_wide]
         + [pltpu.VMEM((2, width, 2 * chunk), low)] * 2
@@ -1216,7 +1164,7 @@
             pltpu.VMEM((width, width), low),
             pltpu.VMEM((width, width), wide),
             pltpu.VMEM((16, shard_rows, 2 * chunk), low),
-            pltpu.VMEM((2, 2, 4, shard_rows, cols), low),
+            pltpu.VMEM((16, shard_rows, cols), low),
             pltpu.SemaphoreType.DMA((2, 4, 8)),
             pltpu.SemaphoreType.DMA((2,)),
         ],
@@ -1228,15 +1176,6 @@
     got_near = swap(send_near, "seq")
     got_far = swap(send_far, "seq")
     scattered = lax.psum_scatter(grads, ("dp", "mlp"), scatter_dimension=0, tiled=True)[0]
-    sums = [Reduce(out_grads[0], out_grads[1])]
-
-    def advance():
-        pins = []
-        for one in sums:
-            pins += jax.tree.leaves(one.state)
-            one.advance()
-        return pins
-
 
     def attention_back(base, count, partial_sum, pins):
         first = partial_sum is None
@@ -1305,7 +1244,7 @@
             seqs / count,
         )(info, turned, got, mine, got_part, gx2, gains[:1])
 
-    def place(sources, plan, feature_count):
+    def place(sources, plan, feature_count, pins=()):
         return call(
             partial(place_kernel, plan, seqs),
             (1,),
@@ -1315,60 +1254,57 @@
             [pltpu.SemaphoreType.DMA((len(plan),))],
             "place",
             1,
+            pins,
         )(info, *sources)
 
-    early = seqs - 1
-    pins = advance()
-    mine_a, send_a, partial_sum, head_sums_a = attention_back(0, early, None, pins)
-    far_a = swap(send_a, "mlp")
-    keep_a, give_a, norm_sums_a = first_back(0, early, mine_a, far_a, ())
-    got_a = swap(give_a, "seq")
-    keep_core_a = swap(keep_a, "mlp")
-    keep_core, got_core = swap(keep_far, "mlp"), swap(got_far, "mlp")
-    pins = advance() + [got_near, got_far, keep_a]
-    mine_b, send_b, gw_in, head_sums_b = attention_back(early, 1, partial_sum, pins)
-    far_b = swap(send_b, "mlp")
-    in_sums = Reduce(gw_in)
-    sums.append(in_sums)
-    pins = advance() + [got_a, keep_core_a]
-    keep_b, give_b, norm_sums_b = first_back(early, 1, mine_b, far_b, pins)
-    first_sums = norm_sums_a + norm_sums_b
-    head_sums = head_sums_a + head_sums_b
+    mine, send, gw_in, head_sums = attention_back(0, seqs, None, ())
+    keep_core = swap(keep_far, "mlp")
+    far_x = swap_x(gw_in[1])
+    moved = swap(send, "mlp")
+    keep, give, first_sums = first_back(0, seqs, mine, moved, [got_near, got_far, keep_core])
+    got_core = swap(got_far, "mlp")
+    keep_moved = swap(keep, "mlp")
+    got_grad = swap(give, "seq")
+
+    norms = jnp.concatenate([first_sums[:2], second_sums[:2]]) * scale
+    heads = jnp.transpose(head_sums[0].reshape(pairs, 2, 128), (1, 0, 2)) * scale
+    heads = heads.reshape(2, cols // 64, dp_size, 64 // dp_size)
+    heads = jnp.transpose(heads, (2, 0, 1, 3)).reshape(1, width)
+    small = jnp.concatenate([norms + swap(norms, "mlp"), heads])
+    small = small + lax.ppermute(small, "dp", [(i, i ^ 1) for i in range(8)])
+    small = small.reshape(5, 4, 2, shard_rows)
+    small = lax.dynamic_index_in_dim(small, d % 2, 2, keepdims=False)
+    small = jnp.concatenate([small, small], axis=1)
+    small = lax.dynamic_slice_in_dim(small, d // 2, 4, 1)
+    small = jnp.pad(jnp.transpose(small, (1, 2, 0)), ((0, 0), (0, 0), (0, 123)))
+    total = gw_in[0].astype(wide) + far_x.astype(wide)
+    total = jnp.concatenate([total, small], axis=2)
+    low_total = total.astype(low)
+    moved = [shift_far(low_total[step], 4 - step) for step in range(1, 4)]
+
+    total = total[0] + sum(part.astype(wide) for part in moved)
+    both = jnp.concatenate([scattered, total.astype(low)], axis=1)
+    both_got = swap(both, "seq").astype(wide)
+    scattered = scattered.astype(wide) + both_got[:, : scattered.shape[1]]
+    total = total + both_got[:, scattered.shape[1] :]
 
     plan = [(True, True, 0), (True, False, 0), (False, True, 0), (False, False, 0)]
-    out = place([keep_near, keep_core, got_near, got_core], plan, cols)
+    out = place([keep_near, keep_core, got_near, got_core], plan, cols, [])
     out = jnp.transpose(out.reshape(seqs_all, half, cols), (1, 0, 2))
-    got_b = swap(give_b, "seq")
-    late = [(own_y, own_c, early) for own_y, own_c, _ in plan]
-    grad_patches = place(
-        [keep_a, keep_core_a, got_a, swap(got_a, "mlp")]
-        + [keep_b, swap(keep_b, "mlp"), got_b, swap(got_b, "mlp")],
-        plan + late,
-        width,
-    )
+    grad_patches = place([keep, keep_moved, got_grad, swap(got_grad, "mlp")], plan, width, [])
     grad_patches = jnp.transpose(grad_patches.reshape(seqs_all, half, width), (1, 0, 2))
 
-    scattered = scattered.astype(wide) + swap(scattered, "seq").astype(wide)
     gw_up = jnp.concatenate(
         [scattered[:, 2 * f * chunk : (2 * f + 1) * chunk] for f in range(chunks)], axis=1
     )
     gw_down = jnp.concatenate(
         [scattered[:, (2 * f + 1) * chunk : (2 * f + 2) * chunk] for f in range(chunks)], axis=1
     )
-    gw_out = sums[0].result()
-    gw_in = in_sums.result()
-    gw_in = gw_in.reshape(shard_rows, pairs, 3, 128)
+    gw_out = scattered[:, 2 * hidden :]
+    gw_in = total[:, : 3 * cols].reshape(shard_rows, pairs, 3, 128)
     gw_in = jnp.transpose(gw_in, (2, 0, 1, 3)).reshape(3, shard_rows, cols)
-    norms = jnp.concatenate([first_sums[:2], second_sums[:2]]) * scale
-    norms = norms + swap(norms, "mlp")
-    heads = jnp.transpose(head_sums[0].reshape(pairs, 2, 128), (1, 0, 2)).reshape(2, cols) * scale
-    small = jnp.concatenate([norms, heads.reshape(1, width)])
-    small = small + swap(small, "seq")
-    for bit in (1, 2, 4):
-        small = small + lax.ppermute(small, "dp", [(i, i ^ bit) for i in range(8)])
-    norms = lax.dynamic_slice_in_dim(small[:4], d * shard_rows, shard_rows, 1)
-    heads = small[4].reshape(2, cols // 64, 64)
-    heads = lax.dynamic_slice_in_dim(heads, d * (64 // dp_size), 64 // dp_size, 2)
+    norms = jnp.transpose(total[:, 3 * cols : 3 * cols + 4])
+    heads = total[:, 3 * cols + 4].reshape(2, cols // 64, 64 // dp_size)
     return (
         out,
         grad_patches,

time: 457 us -> 413 us (0.904)
  the two profiles are of different devices: /device:TPU:0 before, /device:TPU:8 now
where the time goes in v4:
time: 413 us; the launch traced here: 406 us
  Pallas kernels  202 us (49%)
  waiting for transfers between devices  101 us (24%)
  starting transfers between devices  40 us (10%)
  local copies, waits for them, and re-layouts  29.9 us (7%)
  other arithmetic  17.6 us (4%)
  between operations  15.2 us (4%)
    pallas_call x7, Pallas kernels, call(): return lambda *operands: run(*operands, *pins)  202 us
    ppermute x16, waiting for transfers between devices, swap(): return lax.ppermute(values, axis, [(0, 1), (1, 0)])  43.6 us
    ppermute x6, waiting for transfers between devices, shift_far(): lax.ppermute(values, 'dp', [(2 * ((z + step) % 4) + x, 2 * z + x) for z i...  40.8 us
    ppermute x16, starting transfers between devices, swap(): return lax.ppermute(values, axis, [(0, 1), (1, 0)])  20.1 us
    ppermute x5, waiting for transfers between devices, swap_x(): return lax.ppermute(values, 'dp', [(d, d ^ 1) for d in range(8)])  16 us
    unnamed x83, local copies, waits for them, and re-layouts  10.4 us
    ppermute x6, starting transfers between devices, shift_far(): lax.ppermute(values, 'dp', [(2 * ((z + step) % 4) + x, 2 * z + x) for z i...  10.3 us
  transfers between devices with their start and end apart: 30, of which 11 were waited for; matrix products, arithmetic and copies ran while one was open for 8% of the time, Pallas kernels for 31%

profile of v4, /device:TPU:8, one launch (start us, length us, event | category | flops | bytes accessed | tf_op | source)
XLA Modules:
  0.0 405.6 jit_solution(16097368248502284210)
XLA Ops:
  15.0 2.0 collective-permute-start.3
  18.5 2.5 dynamic-slice_bitcast_fusion.4
  29.6 1.9 select_convert_fusion.refs_4_.refs_10_
  31.5 22.1 %collective-permute-done.5.refs_12_.refs_19_ = bf16[112,1152]{1,0:T(8,128)(2,1)} collective-permute-done((bf16[112,1152]{1,0:T(8,128)(2,1)}, bf16[112,1152]{1,0:T(8,128)(2,1)}, u32[]{:S(2)}, u32[]{:S(2)}) %collective-permute-start.5) | collective-permute-done | bytes 258080 | tf_op jit(solution)/shard_map/ppermute | solution.py:926
  55.1 3.5 collective-permute-done.3.refs_10_.refs_17_
  62.0 16.0 %collective-permute-done.4.refs_11_.refs_18_ = bf16[112,1152]{1,0:T(8,128)(2,1)S(1)} collective-permute-done((bf16[112,1152]{1,0:T(8,128)(2,1)}, bf16[112,1152]{1,0:T(8,128)(2,1)S(1)}, u32[]{:S(2)}, u32[]{:S(2)}) %collective-permute-start.4) | collective-permute-done | bytes 258080 | tf_op jit(solution)/shard_map/ppermute | solution.py:934
  86.1 23.0 %qkv.1 = (bf16[3,1024,1152]{2,1,0:T(8,128)(2,1)}, f32[3,1024,768]{2,1,0:T(8,128)}, bf16[768,3072]{1,0:T(8,128)(2,1)}) custom-call(s32[10]{0:T(128)} %concatenate.49.refs_0_, bf16[6,512,768]{2,1,0:T(8,128)(2,1)} %bitcast.140, bf16[3,256,768]{2,1,0:T(8,128)(2,1)} %collective-permute-done.refs_2_.refs_4_, bf16[3,256,768]{2,1,0:T(8,128)(2,1)} %collective-permute-done.1.refs_3_, ...), custom_call_target="tpu_custom_call" | custom-call | flops 28750000128 | bytes 1000000 | tf_op jit(solution)/shard_map/qkv/pallas_call | solution.py:1056
  109.1 17.9 %attn_fwd.1 = (bf16[3,2,256,384]{3,2,1,0:T(8,128)(2,1)}, bf16[3,2,256,384]{3,2,1,0:T(8,128)(2,1)}, f32[3,1024,384]{2,1,0:T(8,128)}) custom-call(s32[10]{0:T(128)} %concatenate.49.refs_0_, s32[12]{0:T(128)} %reshape.212.refs_1_, s32[12]{0:T(128)} %reshape.213.refs_2_, bf16[3,1024,1152]{2,1,0:T(8,128)(2,1)} %get-tuple-element.31.refs_3_, ...), custom_call_target="tpu_custom_call" | custom-call | flops 25300000768 | bytes 1000000 | tf_op jit(solution)/shard_map/attn_fwd/pallas_call | solution.py:1056
  129.9 1.8 bitcast_select_fusion.refs_5_
  132.8 75.6 %middle.1 = (bf16[3,256,384]{2,1,0:T(8,128)(2,1)}, bf16[3,256,384]{2,1,0:T(8,128)(2,1)}, bf16[3,256,384]{2,1,0:T(8,128)(2,1)}, bf16[3,256,384]{2,1,0:T(8,128)(2,...) custom-call(s32[10]{0:T(128)} %concatenate.49.refs_0_, ...), custom_call_target="tpu_custom_call" | custom-call | flops 92000002048 | bytes 1000000 | tf_op jit(solution)/shard_map/middle/pallas_call | solution.py:1056
  210.5 2.1 collective-permute-done.16.refs_5_
  213.6 66.9 %attn_bwd.1 = (bf16[3,2,256,768]{3,2,1,0:T(8,128)(2,1)}, bf16[3,2,256,768]{3,2,1,0:T(8,128)(2,1)}, bf16[2,4,96,1152]{3,2,1,0:T(8,128)(2,1)}, f32[8,768]{1,0:T(8,128)}) custom-call(s32[10]{0:T(128)} %concatenate.49.refs_0_, s32[12]{0:T(128)} %reshape.212.refs_1_, s32[12]{0:T(128)} %reshape.213.refs_2_, bf16[3,1024,1152]{2,1,0:T(8,128)(2,1)} %get-tuple-element.31.refs_3_, ...), custom_call_target="tpu_custom_call" | custom-call | flops 86249996288 | bytes 1000000 | tf_op jit(solution)/shard_map/attn_bwd/pallas_call | solution.py:1056
  280.7 15.0 %collective-permute-start.14 = (bf16[3,256,384]{2,1,0:T(8,128)(2,1)S(1)}, bf16[3,256,384]{2,1,0:T(8,128)(2,1)}, u32[]{:S(2)}, u32[]{:S(2)}) collective-permute-start(bf16[3,256,384]{2,1,0:T(8,128)(2,1)S(1)} %copy-done.31), channel_id=1, source_target_pairs={{0,2},{2,0},{1,3},{3,1},{4,6},{6,4},{5,7},{7,5},{8,10},{10,8},{9,1... | collective-permute-start | bytes 1769480 | tf_op jit(solution)/shard_map/ppermute | solution.py:910
  296.7 13.2 %collective-permute-done.14.refs_8_ = bf16[3,256,384]{2,1,0:T(8,128)(2,1)} collective-permute-done((bf16[3,256,384]{2,1,0:T(8,128)(2,1)S(1)}, bf16[3,256,384]{2,1,0:T(8,128)(2,1)}, u32[]{:S(2)}, u32[]{:S(2)}) %collective-permute-start.14) | collective-permute-done | bytes 589856 | tf_op jit(solution)/shard_map/ppermute | solution.py:910
  311.2 2.5 collective-permute-start.21
  313.7 8.5 %collective-permute-done.13.refs_3_.refs_7_ = bf16[3,256,384]{2,1,0:T(8,128)(2,1)} collective-permute-done((bf16[3,256,384]{2,1,0:T(8,128)(2,1)}, bf16[3,256,384]{2,1,0:T(8,128)(2,1)}, u32[]{:S(2)}, u32[]{:S(2)}) %collective-permute-start.13) | collective-permute-done | bytes 589856 | tf_op jit(solution)/shard_map/ppermute | solution.py:910
  323.6 9.8 %first_norm.1 = (bf16[3,256,768]{2,1,0:T(8,128)(2,1)}, bf16[3,256,768]{2,1,0:T(8,128)(2,1)}, f32[8,768]{1,0:T(8,128)}) custom-call(s32[10]{0:T(128)} %concatenate.49.refs_0_, bf16[6,512,768]{2,1,0:T(8,128)(2,1)} %bitcast.142, bf16[3,256,768]{2,1,0:T(8,128)(2,1)} %collective-permute-done.refs_2_.refs_4_, bf16[3,2,256,768]{3,2,1,0:T(8,128)(2,1)} %get-tuple-element.43.refs_3_, ...), custom_call_target="tpu_custom_call" | custom-call | flops 9200000000 | bytes 1000000 | tf_op jit(solution)/shard_map/first_norm/pallas_call | solution.py:1056
  335.5 2.1 collective-permute-start.23
  339.8 4.2 %collective-permute-start.24 = (bf16[96,1280]{1,0:T(8,128)(2,1)S(1)}, bf16[96,1280]{1,0:T(8,128)(2,1)S(1)}, u32[]{:S(2)}, u32[]{:S(2)}) collective-permute-start(bf16[96,1280]{1,0:T(8,128)(2,1)S(1)} %get-tuple-element.104), channel_id=1, source_target_pairs={{24,0},{28,4},{0,8},{4,12},{8,16},{12,20},{16,24},{20,28},{25,1},{... | collective-permute-start | bytes 737288 | tf_op jit(solution)/shard_map/ppermute | solution.py:926
  345.7 15.2 %collective-permute-done.24 = bf16[96,1280]{1,0:T(8,128)(2,1)S(1)} collective-permute-done((bf16[96,1280]{1,0:T(8,128)(2,1)S(1)}, bf16[96,1280]{1,0:T(8,128)(2,1)S(1)}, u32[]{:S(2)}, u32[]{:S(2)}) %collective-permute-start.24) | collective-permute-done | bytes 245792 | tf_op jit(solution)/shard_map/ppermute | solution.py:926
  360.9 6.3 %collective-permute-done.19.refs_3_ = bf16[3,256,768]{2,1,0:T(8,128)(2,1)} collective-permute-done((bf16[3,256,768]{2,1,0:T(8,128)(2,1)}, bf16[3,256,768]{2,1,0:T(8,128)(2,1)}, u32[]{:S(2)}, u32[]{:S(2)}) %collective-permute-start.19) | collective-permute-done | bytes 1179680 | tf_op jit(solution)/shard_map/ppermute | solution.py:910
  368.9 3.7 place.2
  372.7 5.2 %place.3 = bf16[6,2,256,768]{3,2,1,0:T(8,128)(2,1)} custom-call(s32[10]{0:T(128)} %concatenate.49.refs_0_, bf16[3,256,768]{2,1,0:T(8,128)(2,1)} %get-tuple-element.46.refs_1_, bf16[3,256,768]{2,1,0:T(8,128)(2,1)} %collective-permute-done.18.refs_2_, bf16[3,256,768]{2,1,0:T(8,128)(2,1)} %collective-permute-done.19.refs_3_, ...), custom_call_target="tpu_custom_call" | custom-call | flops 4600000000 | bytes 1000000 | tf_op jit(solution)/shard_map/place/pallas_call | solution.py:1056
  377.9 13.3 %collective-permute-done.27 = bf16[96,4736]{1,0:T(8,128)(2,1)S(1)} collective-permute-done((bf16[96,4736]{1,0:T(8,128)(2,1)S(1)}, bf16[96,4736]{1,0:T(8,128)(2,1)S(1)}, u32[]{:S(2)}, u32[]{:S(2)}) %collective-permute-start.27) | collective-permute-done | bytes 909344 | tf_op jit(solution)/shard_map/ppermute | solution.py:910
  (226 shorter events, 56.1 us)
Async XLA Ops:
  7.2 124.4 %all-gather.3.cloned.1.call-start = ((), (), s32[]{:S(2)}) async-start(), calls=%async_computation.2 | async-start | bytes 11280384 | tf_op jit(solution)/shard_map/all_gather | solution.py:998
  10.6 356.7 %reduce-scatter.2.cloned.1.call-start = ((), (), s32[]{:S(2)}) async-start(), calls=%async_computation.1 | async-start | bytes 11280384 | tf_op jit(solution)/shard_map/reduce_scatter | solution.py:1178
  12.4 19.1 %collective-permute-start.7 = (bf16[112,1152]{1,0:T(8,128)(2,1)}, bf16[112,1152]{1,0:T(8,128)(2,1)}, u32[]{:S(2)}, u32[]{:S(2)}) collective-permute-start(bf16[112,1152]{1,0:T(8,128)(2,1)} %fusion.2.refs_8_.refs_15_), channel_id=1, source_target_pairs={{24,0},{28,4},{0,8},{4,12},{8,16},{12,20},{16,24},{20,28},{25,1},{... | collective-permute-start | bytes 774152 | tf_op jit(solution)/shard_map/ppermute | solution.py:926
  14.0 39.6 %collective-permute-start.5 = (bf16[112,1152]{1,0:T(8,128)(2,1)}, bf16[112,1152]{1,0:T(8,128)(2,1)}, u32[]{:S(2)}, u32[]{:S(2)}) collective-permute-start(bf16[112,1152]{1,0:T(8,128)(2,1)} %fusion.2.refs_8_.refs_15_), channel_id=1, source_target_pairs={{16,0},{20,4},{24,8},{28,12},{0,16},{4,20},{8,24},{12,28},{17,1},{... | collective-permute-start | bytes 774152 | tf_op jit(solution)/shard_map/ppermute | solution.py:926
  15.0 43.6 %collective-permute-start.3 = (bf16[112,1152]{1,0:T(8,128)(2,1)}, bf16[112,1152]{1,0:T(8,128)(2,1)}, u32[]{:S(2)}, u32[]{:S(2)}) collective-permute-start(bf16[112,1152]{1,0:T(8,128)(2,1)} %fusion.2.refs_8_.refs_15_), channel_id=1, source_target_pairs={{8,0},{12,4},{16,8},{20,12},{24,16},{28,20},{0,24},{4,28},{9,1},{1... | collective-permute-start | bytes 774152 | tf_op jit(solution)/shard_map/ppermute | solution.py:926
  17.0 43.1 %collective-permute-start.2 = (bf16[112,1152]{1,0:T(8,128)(2,1)}, bf16[112,1152]{1,0:T(8,128)(2,1)}, u32[]{:S(2)}, u32[]{:S(2)}) collective-permute-start(bf16[112,1152]{1,0:T(8,128)(2,1)} %fusion.2.refs_8_.refs_15_), channel_id=1, source_target_pairs={{0,4},{4,0},{8,12},{12,8},{16,20},{20,16},{24,28},{28,24},{1,5},{5... | collective-permute-start | bytes 774152 | tf_op jit(solution)/shard_map/ppermute | solution.py:934
  21.0 58.4 %collective-permute-start = (bf16[3,256,768]{2,1,0:T(8,128)(2,1)}, bf16[3,256,768]{2,1,0:T(8,128)(2,1)}, u32[]{:S(2)}, u32[]{:S(2)}) collective-permute-start(bf16[3,256,768]{2,1,0:T(8,128)(2,1)} %dynamic-slice_bitcast_fusion.4), channel_id=1, source_target_pairs={{0,2},{2,0},{1,3},{3,1},{4,6},{6,4},{5,7},{7,5},{8,10},{10,8},{9,1... | collective-permute-start | bytes 3538952 | tf_op jit(solution)/shard_map/ppermute | solution.py:910
  31.5 52.2 %collective-permute-start.10 = (bf16[256,6,384]{2,0,1:T(8,128)(2,1)}, bf16[256,6,384]{2,0,1:T(8,128)(2,1)S(1)}, u32[]{:S(2)}, u32[]{:S(2)}) collective-permute-start(bf16[256,6,384]{2,0,1:T(8,128)(2,1)} %get-tuple-element.97), channel_id=1, source_target_pairs={{0,1},{1,0},{2,3},{3,2},{4,5},{5,4},{6,7},{7,6},{8,9},{9,8},{10,11... | collective-permute-start | bytes 3538952 | tf_op jit(solution)/shard_map/ppermute | solution.py:910
  53.6 25.8 %collective-permute-start.8 = (bf16[112,1152]{1,0:T(8,128)(2,1)}, bf16[112,1152]{1,0:T(8,128)(2,1)S(1)}, u32[]{:S(2)}, u32[]{:S(2)}) collective-permute-start(bf16[112,1152]{1,0:T(8,128)(2,1)} %collective-permute-done.7.refs_14_.refs_21_), channel_id=1, source_target_pairs={{0,4},{4,0},{8,12},{12,8},{16,20},{20,16},{24,28},{28,24},{1,5},{5... | collective-permute-start | bytes 774152 | tf_op jit(solution)/shard_map/ppermute | solution.py:934
  58.6 20.1 %collective-permute-start.6 = (bf16[112,1152]{1,0:T(8,128)(2,1)}, bf16[112,1152]{1,0:T(8,128)(2,1)S(1)}, u32[]{:S(2)}, u32[]{:S(2)}) collective-permute-start(bf16[112,1152]{1,0:T(8,128)(2,1)} %collective-permute-done.5.refs_12_.refs_19_), channel_id=1, source_target_pairs={{0,4},{4,0},{8,12},{12,8},{16,20},{20,16},{24,28},{28,24},{1,5},{5... | collective-permute-start | bytes 774152 | tf_op jit(solution)/shard_map/ppermute | solution.py:934
  60.1 17.9 %collective-permute-start.4 = (bf16[112,1152]{1,0:T(8,128)(2,1)}, bf16[112,1152]{1,0:T(8,128)(2,1)S(1)}, u32[]{:S(2)}, u32[]{:S(2)}) collective-permute-start(bf16[112,1152]{1,0:T(8,128)(2,1)} %collective-permute-done.3.refs_10_.refs_17_), channel_id=1, source_target_pairs={{0,4},{4,0},{8,12},{12,8},{16,20},{20,16},{24,28},{28,24},{1,5},{5... | collective-permute-start | bytes 774152 | tf_op jit(solution)/shard_map/ppermute | solution.py:934
  84.4 45.1 %collective-permute-start.11 = (bf16[3,256,768]{2,1,0:T(8,128)(2,1)S(1)}, bf16[3,256,768]{2,1,0:T(8,128)(2,1)S(1)}, u32[]{:S(2)}, u32[]{:S(2)}) collective-permute-start(bf16[3,256,768]{2,1,0:T(8,128)(2,1)S(1)} %get-tuple-element.95), channel_id=1, source_target_pairs={{0,2},{2,0},{1,3},{3,1},{4,6},{6,4},{5,7},{7,5},{8,10},{10,8},{9,1... | collective-permute-start | bytes 3538952 | tf_op jit(solution)/shard_map/ppermute | solution.py:910
  280.5 41.7 %collective-permute-start.17 = (bf16[3,2,256,768]{3,2,1,0:T(8,128)(2,1)}, bf16[3,2,256,768]{3,2,1,0:T(8,128)(2,1)S(1)}, u32[]{:S(2)}, u32[]{:S(2)}) collective-permute-start(bf16[3,2,256,768]{3,2,1,0:T(8,128)(2,1)} %get-tuple-element.44), channel_id=1, source_target_pairs={{0,1},{1,0},{2,3},{3,2},{4,5},{5,4},{6,7},{7,6},{8,9},{9,8},{10,11... | collective-permute-start | bytes 7077896 | tf_op jit(solution)/shard_map/ppermute | solution.py:910
  280.7 29.2 %collective-permute-start.14 = (bf16[3,256,384]{2,1,0:T(8,128)(2,1)S(1)}, bf16[3,256,384]{2,1,0:T(8,128)(2,1)}, u32[]{:S(2)}, u32[]{:S(2)}) collective-permute-start(bf16[3,256,384]{2,1,0:T(8,128)(2,1)S(1)} %copy-done.31), channel_id=1, source_target_pairs={{0,2},{2,0},{1,3},{3,1},{4,6},{6,4},{5,7},{7,5},{8,10},{10,8},{9,1... | collective-permute-start | bytes 1769480 | tf_op jit(solution)/shard_map/ppermute | solution.py:910
  295.7 18.0 %collective-permute-start.12 = (bf16[3,256,384]{2,1,0:T(8,128)(2,1)}, bf16[3,256,384]{2,1,0:T(8,128)(2,1)}, u32[]{:S(2)}, u32[]{:S(2)}) collective-permute-start(bf16[3,256,384]{2,1,0:T(8,128)(2,1)} %get-tuple-element.35), channel_id=1, source_target_pairs={{0,1},{1,0},{2,3},{3,2},{4,5},{5,4},{6,7},{7,6},{8,9},{9,8},{10,11... | collective-permute-start | bytes 1769480 | tf_op jit(solution)/shard_map/ppermute | solution.py:910
  295.7 26.5 %collective-permute-start.13 = (bf16[3,256,384]{2,1,0:T(8,128)(2,1)}, bf16[3,256,384]{2,1,0:T(8,128)(2,1)}, u32[]{:S(2)}, u32[]{:S(2)}) collective-permute-start(bf16[3,256,384]{2,1,0:T(8,128)(2,1)} %get-tuple-element.36), channel_id=1, source_target_pairs={{0,2},{2,0},{1,3},{3,1},{4,6},{6,4},{5,7},{7,5},{8,10},{10,8},{9,1... | collective-permute-start | bytes 1769480 | tf_op jit(solution)/shard_map/ppermute | solution.py:910
  309.9 59.0 %collective-permute-start.15 = (bf16[3,256,384]{2,1,0:T(8,128)(2,1)}, bf16[3,256,384]{2,1,0:T(8,128)(2,1)}, u32[]{:S(2)}, u32[]{:S(2)}) collective-permute-start(bf16[3,256,384]{2,1,0:T(8,128)(2,1)} %collective-permute-done.14.refs_8_), channel_id=1, source_target_pairs={{0,1},{1,0},{2,3},{3,2},{4,5},{5,4},{6,7},{7,6},{8,9},{9,8},{10,11... | collective-permute-start | bytes 1769480 | tf_op jit(solution)/shard_map/ppermute | solution.py:910
  311.2 26.4 %collective-permute-start.21 = (bf16[4,96,1152]{2,1,0:T(8,128)(2,1)S(1)}, bf16[4,96,1152]{2,1,0:T(8,128)(2,1)}, u32[]{:S(2)}, u32[]{:S(2)}) collective-permute-start(bf16[4,96,1152]{2,1,0:T(8,128)(2,1)S(1)} %slice_bitcast_fusion), channel_id=1, source_target_pairs={{0,4},{4,0},{8,12},{12,8},{16,20},{20,16},{24,28},{28,24},{1,5},{5... | collective-permute-start | bytes 2654216 | tf_op jit(solution)/shard_map/ppermute | solution.py:934
  338.9 28.3 %collective-permute-start.19 = (bf16[3,256,768]{2,1,0:T(8,128)(2,1)}, bf16[3,256,768]{2,1,0:T(8,128)(2,1)}, u32[]{:S(2)}, u32[]{:S(2)}) collective-permute-start(bf16[3,256,768]{2,1,0:T(8,128)(2,1)} %get-tuple-element.47), channel_id=1, source_target_pairs={{0,2},{2,0},{1,3},{3,1},{4,6},{6,4},{5,7},{7,5},{8,10},{10,8},{9,1... | collective-permute-start | bytes 3538952 | tf_op jit(solution)/shard_map/ppermute | solution.py:910
  339.8 21.1 %collective-permute-start.24 = (bf16[96,1280]{1,0:T(8,128)(2,1)S(1)}, bf16[96,1280]{1,0:T(8,128)(2,1)S(1)}, u32[]{:S(2)}, u32[]{:S(2)}) collective-permute-start(bf16[96,1280]{1,0:T(8,128)(2,1)S(1)} %get-tuple-element.104), channel_id=1, source_target_pairs={{24,0},{28,4},{0,8},{4,12},{8,16},{12,20},{16,24},{20,28},{25,1},{... | collective-permute-start | bytes 737288 | tf_op jit(solution)/shard_map/ppermute | solution.py:926
  344.0 23.2 %collective-permute-start.26 = (bf16[96,1280]{1,0:T(8,128)(2,1)S(1)}, bf16[96,1280]{1,0:T(8,128)(2,1)S(1)}, u32[]{:S(2)}, u32[]{:S(2)}) collective-permute-start(bf16[96,1280]{1,0:T(8,128)(2,1)S(1)} %get-tuple-element.105), channel_id=1, source_target_pairs={{8,0},{12,4},{16,8},{20,12},{24,16},{28,20},{0,24},{4,28},{9,1},{1... | collective-permute-start | bytes 737288 | tf_op jit(solution)/shard_map/ppermute | solution.py:926
  344.0 23.2 %collective-permute-start.25 = (bf16[96,1280]{1,0:T(8,128)(2,1)S(1)}, bf16[96,1280]{1,0:T(8,128)(2,1)S(1)}, u32[]{:S(2)}, u32[]{:S(2)}) collective-permute-start(bf16[96,1280]{1,0:T(8,128)(2,1)S(1)} %get-tuple-element.106), channel_id=1, source_target_pairs={{16,0},{20,4},{24,8},{28,12},{0,16},{4,20},{8,24},{12,28},{17,1},{... | collective-permute-start | bytes 737288 | tf_op jit(solution)/shard_map/ppermute | solution.py:926
  360.9 11.8 %collective-permute-start.18 = (bf16[3,256,768]{2,1,0:T(8,128)(2,1)}, bf16[3,256,768]{2,1,0:T(8,128)(2,1)}, u32[]{:S(2)}, u32[]{:S(2)}) collective-permute-start(bf16[3,256,768]{2,1,0:T(8,128)(2,1)} %get-tuple-element.46.refs_1_), channel_id=1, source_target_pairs={{0,1},{1,0},{2,3},{3,2},{4,5},{5,4},{6,7},{7,6},{8,9},{9,8},{10,11... | collective-permute-start | bytes 3538952 | tf_op jit(solution)/shard_map/ppermute | solution.py:910
  368.5 22.6 %collective-permute-start.27 = (bf16[96,4736]{1,0:T(8,128)(2,1)S(1)}, bf16[96,4736]{1,0:T(8,128)(2,1)S(1)}, u32[]{:S(2)}, u32[]{:S(2)}) collective-permute-start(bf16[96,4736]{1,0:T(8,128)(2,1)S(1)} %pad_maximum_fusion), channel_id=1, source_target_pairs={{0,2},{2,0},{1,3},{3,1},{4,6},{6,4},{5,7},{7,5},{8,10},{10,8},{9,1... | collective-permute-start | bytes 2727944 | tf_op jit(solution)/shard_map/ppermute | solution.py:910
  (41 other events, 280.2 us)
Sparse Core Ops, SparseCore 0:
  10.7 105.4 all-gather.2
  208.6 126.1 reduce-scatter.1
